TPU v7x, 256 devices: a whole 4x4x8 slice. The times are simulated.
256 devices in a mesh: dom: 16 (over x, z_lo, core), cls: 16 (over y, z_hi).
Axes of the slice: x: 4, y: 4, z: 8 (z_hi: 4, z_lo: 2; z = z_hi * 2 + z_lo), core: 2. Of those that a mesh axis runs over, the one named last changes fastest.
Arguments:
- images: bfloat16 [8192, 128, 256], P(('dom', 'cls')), may hold values from -400 to 400
- defocus: bfloat16 [8192], P(('dom', 'cls')), may hold values from 2 to 20
- assign: int32 [8192], P(('dom', 'cls')), may hold values from 0 to 1
- orient: int32 [8192], P(('dom', 'cls')), may hold values from 0 to 511
- owner: int32 [8192, 16], P(('dom', 'cls')), may hold values from 0 to 15, as said below
- slice_loc: int32 [512, 16], replicated, may hold values from 0 to 127
- volume: bfloat16 [2, 2048, 2048], P(None, 'cls'), may hold values from -6 to 6
Outputs:
- new_volume: float32 [2, 2048, 2048], P(None, 'cls', 'dom')
- correlation: float32 [8192], P(('dom', 'cls'))
Inputs may be any that keep to these rules, and one draw needn't show every extreme that they name: `owner`: of the 16 block rows of each of one device's 32 particles, at most 80 together name any one index of cls; in every draw one index is named by exactly 80 of these rows on every device, and on some devices a second index too.
All inputs are finite; a program needn't handle non-finite values.
Results may differ from a plain program's by a relative error of at most 0.0029.
Values may be sent and summed in bfloat16 or wider, within the bound.
No kernel may reach another device: no remote copies, remote signals or barrier semaphores. Data moves between devices by JAX's collectives and lax.ppermute only.
A program may use at most 128 MiB of HBM per device.

v0:
```python
import jax
import jax.numpy as jnp
from jax import lax
from jax.sharding import PartitionSpec as P


def wave_radius(row_index, width, extent):
    column = (jnp.arange(width, dtype=jnp.int32) % (width // 2)).astype(jnp.float32)
    row_value = row_index.astype(jnp.float32)
    return (row_value[:, None] * row_value[:, None] + column[None, :] * column[None, :]) / float(
        extent * extent
    )


def accumulate(segment_got, numer_got, denom_got, segment_total):
    segment_value = segment_got.reshape(-1).astype(jnp.float32)
    slot_value = jnp.arange(segment_total, dtype=jnp.int32).astype(jnp.float32)
    one_hot = (segment_value[:, None] == slot_value[None, :]).astype(jnp.bfloat16)
    contract_rows = (((0,), (0,)), ((), ()))
    numer_acc = lax.dot_general(
        one_hot,
        numer_got.reshape(segment_value.shape[0], -1),
        contract_rows,
        preferred_element_type=jnp.float32,
    )
    denom_acc = lax.dot_general(
        one_hot,
        denom_got.reshape(segment_value.shape[0], -1),
        contract_rows,
        preferred_element_type=jnp.float32,
    )
    return (numer_acc, denom_acc)


def shards(images, defocus, assign, orient, owner, slice_loc, volume):
    cls_size = lax.axis_size("cls")
    dom_size = lax.axis_size("dom")
    particles, image_rows, row_width = images.shape
    classes, owned_blocks, block_len = volume.shape
    block_rows = block_len // row_width
    slice_blocks = image_rows // block_rows
    row_count = particles * slice_blocks
    capacity = 5 * row_count // (2 * cls_size)
    slot_count = cls_size * capacity
    piece_width = block_len // dom_size
    radius = wave_radius(jnp.arange(image_rows, dtype=jnp.int32), row_width, image_rows)
    owner_flat = owner.reshape(row_count)
    place_flat = slice_loc[orient].reshape(row_count)
    class_flat = jnp.broadcast_to(assign[:, None], (particles, slice_blocks)).reshape(row_count)
    segment_flat = class_flat * owned_blocks + place_flat
    owner_match = (owner_flat[:, None] == jnp.arange(cls_size, dtype=jnp.int32)[None, :]).astype(
        jnp.int32
    )
    earlier = jnp.cumsum(owner_match, axis=0) - owner_match
    destination = owner_flat * capacity + jnp.sum(earlier * owner_match, axis=1)
    row_ids = jnp.arange(row_count, dtype=jnp.int32)
    source_row = jnp.zeros((slot_count,), jnp.int32).at[destination].set(row_ids)
    filled = jnp.zeros((slot_count,), jnp.int32).at[destination].set(1) > 0
    wanted_pos = owner_flat * owned_blocks + place_flat
    piece = lax.all_gather(volume, "cls", axis=1, tiled=True)
    span = piece.shape[1]
    inside = (wanted_pos >= 0) & (wanted_pos < span)
    safe = jnp.clip(wanted_pos, 0, span - 1)
    picked = piece.reshape(classes * span, block_len)[class_flat * span + safe]
    ref_rows = jnp.where(inside[:, None], picked, jnp.zeros((row_count, block_len), jnp.bfloat16))
    ref_rows = ref_rows.reshape(particles, image_rows, row_width)
    ctf_map = jnp.sin(defocus.astype(jnp.float32)[:, None, None] * radius[None, :, :] + 0.3)
    samples = images.astype(jnp.float32)
    projected = ctf_map * ref_rows.astype(jnp.float32)
    cross_sum = jnp.sum(projected * samples, axis=(1, 2))
    power_sum = jnp.sum(projected * projected, axis=(1, 2))
    noise_power = jnp.mean(samples * samples, axis=(1, 2)) + 1e-05
    correlation = cross_sum / jnp.sqrt((power_sum + 1e-05) * noise_power)
    weight = jax.nn.sigmoid(correlation) / noise_power
    segment_slots = (
        jnp.where(filled, segment_flat[source_row], -1)
        .astype(jnp.bfloat16)
        .reshape(cls_size, capacity)
    )
    scaled = weight[:, None, None] * ctf_map
    numer_term = (scaled * samples).astype(jnp.bfloat16).reshape(row_count, block_len)
    denom_term = (scaled * ctf_map).astype(jnp.bfloat16).reshape(row_count, block_len)
    numer_slots = jnp.where(filled[:, None], numer_term[source_row], 0.0)
    denom_slots = jnp.where(filled[:, None], denom_term[source_row], 0.0)
    numer_slots = numer_slots.reshape(cls_size, capacity, dom_size, piece_width)
    denom_slots = denom_slots.reshape(cls_size, capacity, dom_size, piece_width)
    rows_sent = jnp.concatenate((numer_slots, denom_slots), axis=3)
    small_sent = segment_slots[:, :, None, None]
    rows_got, small_got = (
        lax.all_to_all(rows_sent, "cls", split_axis=0, concat_axis=0, tiled=True),
        lax.all_to_all(small_sent, "cls", split_axis=0, concat_axis=0, tiled=True),
    )
    segment_got = small_got[:, :, 0, 0]
    numer_got = rows_got[..., :piece_width]
    denom_got = rows_got[..., piece_width:]
    numer_acc, denom_acc = accumulate(segment_got, numer_got, denom_got, classes * owned_blocks)
    numer_full = numer_acc.reshape(classes, owned_blocks, block_len)
    denom_full = denom_acc.reshape(classes, owned_blocks, block_len)
    numer_sum, denom_sum = (
        lax.psum_scatter(numer_full, "dom", scatter_dimension=2, tiled=True),
        lax.psum_scatter(denom_full, "dom", scatter_dimension=2, tiled=True),
    )
    new_volume = numer_sum / (denom_sum + 1.0)
    return (new_volume, correlation)


def solution(mesh):
    placed = (
        P(("dom", "cls"), None, None),
        P(("dom", "cls")),
        P(("dom", "cls")),
        P(("dom", "cls")),
        P(("dom", "cls"), None),
        P(),
        P(None, "cls", None),
    )
    return jax.shard_map(
        shards,
        mesh=mesh,
        in_specs=placed,
        out_specs=(P(None, "cls", "dom"), P(("dom", "cls"))),
        check_vma=False,
    )
```

profile of v0, /device:TPU:1, one launch (start us, length us, event | category | flops | bytes accessed | tf_op | source)
XLA Modules:
  0.0 743.2 jit_solution(17137549865704382692)
XLA Ops:
  19.2 8.0 %gather_fusion.1 = s32[1280]{0:T(1024)S(1)} fusion(s32[512]{0:T(512)S(1)} %add.150, s32[2048]{0:T(1024)S(1)} %pad_clamp_fusion), kind=kCustom, calls=%fused_computation.1 | custom fusion | bytes 15360 | tf_op jit(solution)/shard_map/gather | solution.py:76
  27.9 11.8 %all-to-all-start = ((bf16[16,80,1,1]{1,3,2,0:T(2,128)(2,1)}), bf16[16,80,1,1]{1,3,2,0:T(2,128)(2,1)S(1)}, u32[]{:S(2)}, u32[]{:S(2)}) async-start(bf16[16,80,1,1]{1,3,2,0:T(2,128)(2,1)} %broadcast_in_dim_reshape.5), calls=%async_computation | async-start | bytes 16384 | tf_op jit(solution)/shard_map/all_to_all | solution.py:91
  40.2 175.5 %all-gather.2.cloned.1.call-done = bf16[2,2048,2048]{2,1,0:T(8,128)(2,1)} async-done(((bf16[2,128,2048]{2,1,0:T(8,128)(2,1)}), bf16[2,2048,2048]{2,1,0:T(8,128)(2,1)}) %all-gather.2.cloned.1.call-update) | async-done | bytes 16777232 | tf_op jit(solution)/shard_map/all_gather | solution.py:60
  215.7 13.2 %gather_fusion.2 = bf16[512,2048]{1,0:T(8,128)(2,1)} fusion(bf16[4096,2048]{1,0:T(8,128)(2,1)} %bitcast.44, s32[1024]{0:T(1024)S(1)} %pad_clamp_fusion.1), kind=kCustom, calls=%fused_computation.2 | custom fusion | bytes 4196352 | tf_op jit(solution)/shard_map/gather | solution.py:64
  233.2 17.6 %multiply_reduce_fusion = (f32[32]{0:T(128)S(1)}, f32[32]{0:T(128)S(1)}, f32[32]{0:T(128)S(1)}) fusion(f32[128,256]{1,0:T(8,128)S(1)} %add_multiply_fusion, f32[32]{0:T(128)S(1)} %convert_element_type.68, bf16[32,128,256]{2,1,0:T(8,128)(2,1)} %gather.24, pred[32,128]{1,0:T(8,128)(4,1)S(1)} %copy.35, bf16[32,128,256]{2,1,0:T(8,128)(2,1)S(1)} %copy-done.1), kind=kLoop, calls=%fused_computation.18 | loop fusion | flops 12582816 | bytes 4329984 | tf_op jit(solution)/shard_map/reduce_sum | solution.py:71
  251.4 15.8 %fusion.2 = (bf16[32,128,256]{2,1,0:T(8,128)(2,1)}, f32[32,128,256]{2,1,0:T(8,128)}) fusion(bf16[32,128,256]{2,1,0:T(8,128)(2,1)S(1)} %copy-done.1, f32[32]{0:T(128)S(1)} %get-tuple-element.7, f32[128,256]{1,0:T(8,128)S(1)} %add_multiply_fusion, f32[32]{0:T(128)S(1)} %convert_element_type.68), kind=kLoop, calls=%fused_computation.16 | loop fusion | flops 6291456 | bytes 8519936 | tf_op jit(solution)/shard_map/convert_element_type | solution.py:81
  267.2 4.9 sin.8
  274.4 4.9 mul.140
  279.3 4.5 fusion.3
  283.8 6.1 gather_fusion.4
  289.9 6.6 copy.39
  299.4 6.1 gather_fusion.3
  305.5 4.4 copy.38
  310.0 5.5 bitcast_select_fusion.1
  315.4 9.5 %pad_maximum_fusion = bf16[16,80,16,256]{3,2,1,0:T(8,128)(2,1)} fusion(bf16[16,80,16,128]{3,2,1,0:T(8,128)(2,1)} %get-tuple-element.16, bf16[16,80,16,128]{3,2,1,0:T(8,128)(2,1)} %get-tuple-element.15), kind=kLoop, calls=%fused_computation.7 | loop fusion | flops 20971520 | bytes 20971520 | tf_op jit(solution)/shard_map/concatenate | solution.py:87
  324.9 7.3 all-to-all-start.1
  332.3 252.2 %all-to-all-done.1 = bf16[16,80,16,256]{3,2,1,0:T(8,128)(2,1)} async-done(((bf16[16,80,16,256]{3,2,1,0:T(8,128)(2,1)}), bf16[16,80,16,256]{3,2,1,0:T(8,128)(2,1)}, u32[]{:S(2)}, u32[]{:S(2)}) %all-to-all-start.1) | async-done | bytes 10485792 | tf_op jit(solution)/shard_map/all_to_all | solution.py:90
  584.6 10.9 %fusion.22 = (bf16[16,80,16,128]{3,2,1,0:T(8,128)(2,1)}, bf16[16,80,16,128]{3,2,1,0:T(8,128)(2,1)}) fusion(bf16[16,80,16,256]{3,2,1,0:T(8,128)(2,1)} %all-to-all-done.1), kind=kLoop, calls=%fused_computation.71 | loop fusion | bytes 20971520 | tf_op jit(solution)/shard_map/slice | solution.py:95
  595.4 8.8 %reshape.315 = bf16[1280,2048,1]{1,0,2:T(8,128)(2,1)} reshape(bf16[16,80,16,128]{3,2,1,0:T(8,128)(2,1)} %get-tuple-element.9) | data formatting | bytes 10485760 | tf_op jit(solution)/shard_map/reshape | solution.py:28
  604.3 5.4 fusion.4
  609.7 8.8 %reshape.314 = bf16[1280,2048,1]{1,0,2:T(8,128)(2,1)} reshape(bf16[16,80,16,128]{3,2,1,0:T(8,128)(2,1)} %get-tuple-element.10) | data formatting | bytes 10485760 | tf_op jit(solution)/shard_map/reshape | solution.py:22
  618.6 5.5 fusion.6
  624.1 43.4 %reduce-scatter.5.cloned.1.call-done = f32[2,128,128]{2,1,0:T(8,128)} async-done(((f32[2,128,2048]{2,1,0:T(8,128)}), f32[2,128,128]{2,1,0:T(8,128)}) %reduce-scatter.5.cloned.1.call-update) | async-done | bytes 131088 | tf_op jit(solution)/shard_map/reduce_scatter | solution.py:101
  667.4 67.6 %reduce-scatter.3.cloned.1.call-done = f32[2,128,128]{2,1,0:T(8,128)} async-done(((f32[2,128,2048]{2,1,0:T(8,128)}), f32[2,128,128]{2,1,0:T(8,128)}) %reduce-scatter.3.cloned.1.call-update) | async-done | bytes 131088 | tf_op jit(solution)/shard_map/reduce_scatter | solution.py:100
  (64 shorter events, 25.1 us)
Async XLA Ops:
  7.2 208.5 %all-gather.2.cloned.1.call-start = ((), (), s32[]{:S(2)}) async-start(), calls=%async_computation.4 | async-start | bytes 17825792 | tf_op jit(solution)/shard_map/all_gather | solution.py:60
  19.2 20.6 %copy-start.2 = (s32[32,16]{0,1:T(8,128)S(1)}, s32[32,16]{0,1:T(8,128)}, u32[]{:S(2)}) copy-start(s32[32,16]{0,1:T(8,128)} %param.11) | copy-start | bytes 6148
  19.2 20.8 %copy-start.3 = (bf16[32]{0:T(256)(128)(2,1)S(1)}, bf16[32]{0:T(256)(128)(2,1)}, u32[]{:S(2)}) copy-start(bf16[32]{0:T(256)(128)(2,1)} %param.8) | copy-start | bytes 196
  27.9 297.0 %all-to-all-start = ((bf16[16,80,1,1]{1,3,2,0:T(2,128)(2,1)}), bf16[16,80,1,1]{1,3,2,0:T(2,128)(2,1)S(1)}, u32[]{:S(2)}, u32[]{:S(2)}) async-start(bf16[16,80,1,1]{1,3,2,0:T(2,128)(2,1)} %broadcast_in_dim_reshape.5), calls=%async_computation | async-start | bytes 16384 | tf_op jit(solution)/shard_map/all_to_all | solution.py:91
  228.9 4.4 copy-start.1
  305.5 4.4 copy-start
  324.9 259.7 %all-to-all-start.1 = ((bf16[16,80,16,256]{3,2,1,0:T(8,128)(2,1)}), bf16[16,80,16,256]{3,2,1,0:T(8,128)(2,1)}, u32[]{:S(2)}, u32[]{:S(2)}) async-start(bf16[16,80,16,256]{3,2,1,0:T(8,128)(2,1)} %pad_maximum_fusion), calls=%async_computation.1 | async-start | bytes 20971520 | tf_op jit(solution)/shard_map/all_to_all | solution.py:90
  332.2 335.2 %reduce-scatter.5.cloned.1.call-start = ((), (), s32[]{:S(2)}) async-start(), calls=%async_computation.6 | async-start | bytes 2228224 | tf_op jit(solution)/shard_map/reduce_scatter | solution.py:101
  609.7 125.3 %reduce-scatter.3.cloned.1.call-start = ((), (), s32[]{:S(2)}) async-start(), calls=%async_computation.5 | async-start | bytes 2228224 | tf_op jit(solution)/shard_map/reduce_scatter | solution.py:100
Sparse Core Ops, SparseCore 0:
  10.5 205.1 all-gather.1
  609.8 57.5 reduce-scatter.4
  669.9 64.9 reduce-scatter.2
where the time goes:
time: 747 us; the launch traced here: 743 us
  waiting for transfers between devices  539 us (72%)
  local copies, waits for them, and re-layouts  101 us (14%)
  other arithmetic  58.6 us (8%)
  starting transfers between devices  19.1 us (3%)
  between operations  14 us (2%)
  matrix products  10.9 us (1%)
    all_to_all x1, waiting for transfers between devices, shards(): lax.all_to_all(rows_sent, 'cls', split_axis=0, concat_axis=0, tiled=True)  252 us
    all_gather x1, waiting for transfers between devices, shards(): piece = lax.all_gather(volume, 'cls', axis=1, tiled=True)  175 us
    reduce_scatter x1, waiting for transfers between devices, shards(): lax.psum_scatter(numer_full, 'dom', scatter_dimension=2, tiled=True)  67.6 us
    reduce_scatter x1, waiting for transfers between devices, shards(): lax.psum_scatter(denom_full, 'dom', scatter_dimension=2, tiled=True)  43.4 us
    reduce_sum x1, other arithmetic, shards(): power_sum = jnp.sum(projected * projected, axis=(1, 2))  17.6 us
    gather x2, local copies, waits for them, and re-layouts, shards(): picked = piece.reshape(classes * span, block_len)[class_flat * span + safe]  17.6 us
    convert_element_type x1, other arithmetic, shards(): (scaled * samples).astype(jnp.bfloat16).reshape(row_count, block_len)  15.8 us
  transfers between devices with their start and end apart: 5, of which 4 were waited for; matrix products, arithmetic and copies ran while one was open for 19% of the time, Pallas kernels for 0%

commit v1 on v0

v1 whole, which is shorter than its diff:
```python
import functools
import jax
import jax.numpy as jnp
from jax import lax
from jax.experimental import pallas as pl
from jax.experimental.pallas import tpu as pltpu
from jax.sharding import PartitionSpec as P

F32 = jnp.float32
BF16 = jnp.bfloat16
LANES = 128
PHASE = 0.3
EPS = 1e-05
VMEM_LIMIT = 56 * 1024 * 1024


def params(semantics=None):
    return pltpu.CompilerParams(vmem_limit_bytes=VMEM_LIMIT, dimension_semantics=semantics)


def split_kernel(particles, slices, block_rows, img_ref, out_ref, scratch):
    rows = slices * block_rows
    for h in range(2):
        half = img_ref[:, :, h * LANES : (h + 1) * LANES].astype(F32)
        scratch[h] = half.reshape(particles * rows, LANES)
    for j in range(slices):
        for b in range(block_rows):
            picked = pl.ds(j * block_rows + b, particles, stride=rows)
            for h in range(2):
                out_ref[2 * b + h, j] = scratch[h, picked, :].astype(BF16)


def split_images(images, slices):
    particles, rows, width = images.shape
    block_rows = rows // slices
    step = 16
    return pl.pallas_call(
        functools.partial(split_kernel, step, slices, block_rows),
        grid=(particles // step,),
        in_specs=[pl.BlockSpec((step, rows, width), lambda i: (i, 0, 0))],
        out_specs=pl.BlockSpec((2 * block_rows, slices, step, LANES), lambda i: (0, 0, i, 0)),
        out_shape=jax.ShapeDtypeStruct((2 * block_rows, slices, particles, LANES), BF16),
        scratch_shapes=[pltpu.VMEM((2, step * rows, LANES), F32)],
        compiler_params=params(),
        cost_estimate=pl.CostEstimate(flops=0, bytes_accessed=images.size * 8, transcendentals=0),
    )(images)


def project_kernel(
    slices, particles, extent, row_ref, key_ref, focus_ref, vol_ref, proj_ref, ctf_ref, power_ref
):
    count = slices * particles
    key = jnp.broadcast_to(key_ref[0], (8, count)).T[:, :1]
    half = vol_ref.shape[0] // 2
    blocks = vol_ref.shape[1]
    upper = key >= float(half * blocks)
    low = jnp.where(upper, key - float(half * blocks), key)
    low = jnp.broadcast_to(low, (count, blocks))
    lane = lax.broadcasted_iota(jnp.int32, (count, blocks), 1).astype(F32)
    acc = jnp.zeros((count, 2 * LANES), F32)
    for o in range(half):
        one_hot = (low == lane + float(o * blocks)).astype(BF16)
        both = jnp.concatenate([vol_ref[o], vol_ref[o + half]], axis=1)
        acc += jnp.dot(one_hot, both, preferred_element_type=F32)
    picked = jnp.where(
        jnp.broadcast_to(upper, (count, LANES)), acc[:, LANES:], acc[:, :LANES]
    ).reshape(slices, particles, LANES)
    focus = jnp.broadcast_to(focus_ref[0], (8, particles)).T[:, :1]
    focus = jnp.broadcast_to(focus, (particles, LANES)) / extent
    column = lax.broadcasted_iota(jnp.int32, (particles, LANES), 1).astype(F32)
    angle = focus * (column * column)
    cos_col, sin_col = jnp.cos(angle), jnp.sin(angle)
    row = column * 8.0 + row_ref[0]
    angle = focus * (row * row) + PHASE
    cos_row, sin_row = jnp.cos(angle), jnp.sin(angle)
    power = jnp.zeros((particles, LANES), F32)
    for j in range(slices):
        ctf = sin_row[:, j : j + 1] * cos_col + cos_row[:, j : j + 1] * sin_col
        proj = ctf * picked[j]
        power += proj * proj
        ctf_ref[0, j] = ctf
        proj_ref[0, j] = proj
    power_ref[0] = power


def project(row, keys, focus, vol, extent):
    senders, slices, particles = keys.shape
    owners, blocks, _ = vol.shape
    shape = (senders, slices, particles, LANES)
    block = pl.BlockSpec((1, slices, particles, LANES), lambda s: (s, 0, 0, 0))
    return pl.pallas_call(
        functools.partial(project_kernel, slices, particles, extent),
        grid=(senders,),
        in_specs=[
            pl.BlockSpec(memory_space=pltpu.SMEM),
            pl.BlockSpec((1, 1, slices * particles), lambda s: (s, 0, 0)),
            pl.BlockSpec((1, 1, particles), lambda s: (s, 0, 0)),
            pl.BlockSpec((owners, blocks, LANES), lambda s: (0, 0, 0)),
        ],
        out_specs=[block, block, pl.BlockSpec((1, particles, LANES), lambda s: (s, 0, 0))],
        out_shape=[
            jax.ShapeDtypeStruct(shape, F32),
            jax.ShapeDtypeStruct(shape, F32),
            jax.ShapeDtypeStruct((senders, particles, LANES), F32),
        ],
        compiler_params=params(),
        cost_estimate=pl.CostEstimate(
            flops=2 * senders * slices * particles * owners * blocks * LANES,
            bytes_accessed=10 * 1024 * 1024,
            transcendentals=0,
        ),
    )(row, keys.reshape(senders, 1, slices * particles), focus.reshape(senders, 1, particles), vol)


def sums_kernel(slices, particles, img_ref, proj_ref, power_ref, out_ref, cross_acc, noise_acc):
    s = pl.program_id(0)
    cross = jnp.zeros((particles, LANES), F32)
    noise = jnp.zeros((particles, LANES), F32)
    for j in range(slices):
        img = img_ref[0, j].astype(F32)
        cross += img * proj_ref[0, j]
        noise += img * img
    cross_acc[pl.ds(s * particles, particles), :] = cross
    noise_acc[pl.ds(s * particles, particles), :] = noise

    @pl.when(s == pl.num_programs(0) - 1)
    def _():
        total = out_ref.shape[1] // 3
        for i, ref in enumerate((cross_acc, power_ref, noise_acc)):
            out_ref[:, i * total : (i + 1) * total] = jnp.sum(ref[...].T, axis=0, keepdims=True)


def partial_sums(img, proj, power):
    senders, slices, particles, _ = img.shape
    total = senders * particles
    block = pl.BlockSpec((1, slices, particles, LANES), lambda s: (s, 0, 0, 0))
    return pl.pallas_call(
        functools.partial(sums_kernel, slices, particles),
        grid=(senders,),
        in_specs=[block, block, pl.BlockSpec((total, LANES), lambda s: (0, 0))],
        out_specs=pl.BlockSpec((1, 3 * total), lambda s: (0, 0)),
        out_shape=jax.ShapeDtypeStruct((1, 3 * total), F32),
        scratch_shapes=[pltpu.VMEM((total, LANES), F32), pltpu.VMEM((total, LANES), F32)],
        compiler_params=params(),
        cost_estimate=pl.CostEstimate(
            flops=img.size * 4, bytes_accessed=img.size * 6, transcendentals=0
        ),
    )(img, proj, power.reshape(total, LANES))


def terms_kernel(
    slices, particles, pixels, part_ref, img_ref, ctf_ref, terms_ref, corr_ref, weight_col
):
    s = pl.program_id(0)

    @pl.when(s == 0)
    def _():
        total = part_ref.shape[1] // 3
        sums = jnp.sum(part_ref[...], axis=0, keepdims=True)
        cross, power = sums[:, :total], sums[:, total : 2 * total]
        noise = sums[:, 2 * total :] / pixels + EPS
        corr = cross / jnp.sqrt((power + EPS) * noise)
        corr_ref[...] = corr
        weight = jax.nn.sigmoid(corr) / noise
        weight_col[...] = jnp.broadcast_to(weight, (LANES, total)).T

    weight = weight_col[pl.ds(s * particles, particles), :]
    for j in range(slices):
        ctf = ctf_ref[0, j]
        scaled = weight * ctf
        rows = pl.ds(j * particles, particles)
        terms_ref[rows, :LANES] = (scaled * img_ref[0, j].astype(F32)).astype(BF16)
        terms_ref[rows, LANES:] = (scaled * ctf).astype(BF16)


def make_terms(partials, img, ctf):
    senders, slices, particles, _ = img.shape
    total = senders * particles
    block = pl.BlockSpec((1, slices, particles, LANES), lambda s: (s, 0, 0, 0))
    return pl.pallas_call(
        functools.partial(terms_kernel, slices, particles, float(slices * 8 * 2 * LANES)),
        grid=(senders,),
        in_specs=[pl.BlockSpec(partials.shape, lambda s: (0, 0)), block, block],
        out_specs=[
            pl.BlockSpec((slices * particles, 2 * LANES), lambda s: (s, 0)),
            pl.BlockSpec((1, total), lambda s: (0, 0)),
        ],
        out_shape=[
            jax.ShapeDtypeStruct((senders * slices * particles, 2 * LANES), BF16),
            jax.ShapeDtypeStruct((1, total), F32),
        ],
        scratch_shapes=[pltpu.VMEM((total, LANES), F32)],
        compiler_params=params(),
        cost_estimate=pl.CostEstimate(
            flops=img.size * 4, bytes_accessed=img.size * 10, transcendentals=0
        ),
    )(partials, img, ctf)


def scatter_kernel(blocks, first, size, key_ref, terms_ref, out_ref):
    o = pl.program_id(0)
    rows = terms_ref.shape[0]
    base = (o * blocks + first).astype(F32)
    depth = 1024
    acc = jnp.zeros((size, 2 * LANES), F32)
    for i in range(rows // depth):
        key = key_ref[:, i * depth : (i + 1) * depth] - base
        slot = lax.broadcasted_iota(jnp.int32, (size, depth), 0).astype(F32)
        one_hot = (slot == key).astype(BF16)
        acc += jnp.dot(
            one_hot, terms_ref[i * depth : (i + 1) * depth, :], preferred_element_type=F32
        )
    out_ref[0] = acc.astype(BF16)


def scatter(keys, terms, owners, blocks, first, size):
    rows = terms.shape[0]
    return pl.pallas_call(
        functools.partial(scatter_kernel, blocks, first, size),
        grid=(owners,),
        in_specs=[
            pl.BlockSpec((1, rows), lambda o: (0, 0)),
            pl.BlockSpec((rows, 2 * LANES), lambda o: (0, 0)),
        ],
        out_specs=pl.BlockSpec((1, size, 2 * LANES), lambda o: (o, 0, 0)),
        out_shape=jax.ShapeDtypeStruct((owners, size, 2 * LANES), BF16),
        compiler_params=params(),
        cost_estimate=pl.CostEstimate(
            flops=2 * rows * owners * size * 2 * LANES,
            bytes_accessed=terms.size * 2 + owners * size * 512,
            transcendentals=0,
        ),
    )(keys.reshape(1, rows), terms)


def shards(images, defocus, assign, orient, owner, slice_loc, volume):
    owners = lax.axis_size("cls")
    groups = lax.axis_size("dom")
    me = lax.axis_index("dom")
    particles, image_rows, width = images.shape
    classes, owned, block_len = volume.shape
    slices = owner.shape[1]
    blocks = classes * owned
    total = groups * particles

    piece = lax.dynamic_slice_in_dim(volume, me * LANES, LANES, axis=2).reshape(blocks, LANES)
    vol = lax.all_gather(piece, "cls", axis=0, tiled=False)

    place = slice_loc[orient]
    key = (owner * blocks + assign[:, None] * owned + place).astype(F32).T
    meta = jnp.concatenate([key.reshape(-1), defocus.astype(F32)])
    meta = jnp.broadcast_to(meta[None, None, :], (groups, 1, meta.shape[0]))
    meta = lax.all_to_all(meta, "dom", 0, 0, tiled=True)[:, 0, :]
    keys = meta[:, : slices * particles].reshape(groups, slices, particles)
    focus = meta[:, slices * particles :]

    img = split_images(images, slices)
    img = lax.all_to_all(img, "dom", 0, 0, tiled=True)

    row = (me // 2).astype(F32).reshape(1)
    proj, ctf, power = project(row, keys, focus, vol, float(image_rows * image_rows))
    partial = partial_sums(img, proj, power)
    partial = jnp.broadcast_to(partial[None], (groups,) + partial.shape)
    partial = lax.all_to_all(partial, "dom", 0, 0, tiled=True)[:, 0, :]
    terms, corr = make_terms(partial, img, ctf)
    correlation = lax.dynamic_slice_in_dim(corr[0], me * particles, particles)

    volumes = []
    sent = []
    for c in range(classes):
        summed = scatter(keys, terms, owners, blocks, c * owned, owned)
        sent.append(lax.all_to_all(summed, "cls", 0, 0, tiled=True))
    for got in sent:
        whole = jnp.sum(got.astype(F32), axis=0)
        volumes.append(whole[:, :LANES] / (whole[:, LANES:] + 1.0))
    return (jnp.stack(volumes), correlation)


def solution(mesh):
    placed = (
        P(("dom", "cls"), None, None),
        P(("dom", "cls")),
        P(("dom", "cls")),
        P(("dom", "cls")),
        P(("dom", "cls"), None),
        P(),
        P(None, "cls", None),
    )
    return jax.shard_map(
        shards,
        mesh=mesh,
        in_specs=placed,
        out_specs=(P(None, "cls", "dom"), P(("dom", "cls"))),
        check_vma=False,
    )
```

time: 747 us -> 233 us (0.31)
  waiting for transfers between devices: 539 us -> 102 us
  local copies, waits for them, and re-layouts: 101 us -> 8.63 us
  Pallas kernels: 0 us -> 73.5 us
  other arithmetic: 58.6 us -> 4.49 us
  matrix products: 10.9 us -> 0 us
  starting transfers between devices: 19.1 us -> 28.7 us
    all_to_all x2 -> x5, waiting for transfers between devices: 252 us -> 45.4 us  [the longest x2 39.2 us: shards(): sent.append(lax.all_to_all(summed, 'cls', 0, 0, tiled=True))]
    all_gather x1, waiting for transfers between devices: 175 us -> 56.2 us  [shards(): vol = lax.all_gather(piece, 'cls', axis=0, tiled=False)]
    reduce_scatter x2 -> x0, waiting for transfers between devices: 111 us -> none  [the longest x1 67.6 us: shards(): lax.psum_scatter(numer_full, 'dom', scatter_dimension=2, tiled=True)]
    pallas_call x0 -> x6, Pallas kernels: none -> 73.5 us  [the longest x2 29 us: scatter(): pl.pallas_call(functools.partial(scatter_kernel, blocks, first, size), gr...]
    gather x7 -> x2, local copies, waits for them, and re-layouts: 38.5 us -> 0.65 us  [shards(): place = slice_loc[orient]]
    reshape x3 -> x1, local copies, waits for them, and re-layouts: 20.5 us -> 0.08 us  [shards(): meta = jnp.concatenate([key.reshape(-1), defocus.astype(F32)])]
    convert_element_type x7 -> x1, other arithmetic: 20.3 us -> 0.75 us  [shards(): meta = jnp.concatenate([key.reshape(-1), defocus.astype(F32)])]
    reduce_sum x2, other arithmetic: 17.7 us -> 0.28 us  [shards(): whole = jnp.sum(got.astype(F32), axis=0)]
  transfers between devices with their start and end apart: 5 -> 6, of which waited for: 4 -> 5; matrix products, arithmetic and copies ran while one was open for 19% -> 2% of each run, Pallas kernels for 0% -> 16%
where the time goes in v1:
time: 233 us; the launch traced here: 231 us
  waiting for transfers between devices  102 us (44%)
  Pallas kernels  73.5 us (32%)
  starting transfers between devices  28.7 us (12%)
  between operations  14.1 us (6%)
  local copies, waits for them, and re-layouts  8.63 us (4%)
  other arithmetic  4.49 us (2%)
    all_gather x1, waiting for transfers between devices, shards(): vol = lax.all_gather(piece, 'cls', axis=0, tiled=False)  56.2 us
    all_to_all x2, waiting for transfers between devices, shards(): sent.append(lax.all_to_all(summed, 'cls', 0, 0, tiled=True))  39.2 us
    pallas_call x2, Pallas kernels, scatter(): pl.pallas_call(functools.partial(scatter_kernel, blocks, first, size), gr...  29 us
    pallas_call x1, Pallas kernels, project(): pl.pallas_call(functools.partial(project_kernel, slices, particles, exten...  18.8 us
    pallas_call x1, Pallas kernels, make_terms(): pl.pallas_call(functools.partial(terms_kernel, slices, particles, float(s...  11.2 us
    all_to_all x2, starting transfers between devices, shards(): sent.append(lax.all_to_all(summed, 'cls', 0, 0, tiled=True))  10.4 us
    pallas_call x1, Pallas kernels, partial_sums(): pl.pallas_call(functools.partial(sums_kernel, slices, particles), grid=(s...  9.79 us
    all_to_all x1, starting transfers between devices, shards(): meta = lax.all_to_all(meta, 'dom', 0, 0, tiled=True)[:, 0, :]  7.17 us
  transfers between devices with their start and end apart: 6, of which 5 were waited for; matrix products, arithmetic and copies ran while one was open for 2% of the time, Pallas kernels for 16%

profile of v1, /device:TPU:1, one launch (start us, length us, event | category | flops | bytes accessed | tf_op | source)
XLA Modules:
  0.0 231.2 jit_solution(10307117327593833379)
XLA Ops:
  7.2 0.7 convert_element_type.16
  9.2 0.9 copy.20
  10.8 0.7 convert_bitcast_fusion
  12.2 7.2 %all-to-all-start = ((f32[16,1,544]{2,1,0:T(1,128)}), f32[16,1,544]{2,1,0:T(1,128)S(1)}, u32[]{:S(2)}, u32[]{:S(2)}) async-start(f32[16,1,544]{2,1,0:T(1,128)} %broadcast_in_dim.9), calls=%async_computation | async-start | bytes 81920 | tf_op jit(solution)/shard_map/all_to_all | solution.py:253
  19.4 4.8 %shard_map.86 = bf16[16,16,32,128]{3,2,1,0:T(8,128)(2,1)} custom-call(bf16[32,128,256]{2,1,0:T(8,128)(2,1)} %img_ref.1), custom_call_target="tpu_custom_call" | custom-call | bytes 8388608 | tf_op jit(solution)/shard_map/pallas_call | solution.py:37
  24.2 1.0 all-to-all-done
  25.2 4.7 %all-to-all-start.1 = ((bf16[16,16,32,128]{3,2,1,0:T(8,128)(2,1)}), bf16[16,16,32,128]{3,2,1,0:T(8,128)(2,1)S(1)}, u32[]{:S(2)}, u32[]{:S(2)}) async-start(bf16[16,16,32,128]{3,2,1,0:T(8,128)(2,1)} %shard_map.86), calls=%async_computation.1 | async-start | bytes 4194304 | tf_op jit(solution)/shard_map/all_to_all | solution.py:258
  31.9 56.2 %all-gather.2.cloned.1.call-done.vol_ref = bf16[16,256,128]{2,1,0:T(8,128)(2,1)} async-done(((bf16[1,256,128]{2,1,0:T(8,128)(2,1)}), bf16[16,256,128]{2,1,0:T(8,128)(2,1)}) %all-gather.2.cloned.1.call-update) | async-done | bytes 1048592 | tf_op jit(solution)/shard_map/all_gather | solution.py:247
  88.2 18.8 %shard_map.87 = (f32[16,16,32,128]{3,2,1,0:T(8,128)}, f32[16,16,32,128]{3,2,1,0:T(8,128)}, f32[16,32,128]{2,1,0:T(8,128)}) custom-call(f32[1]{0:T(128)} %bitcast.1.row_ref, f32[16,1,512]{2,1,0:T(1,128)} %copy.22.key_ref, f32[16,1,32]{2,1,0:T(1,128)} %bitcast.31, bf16[16,256,128]{2,1,0:T(8,128)(2,1)} %all-gather.2.cloned.1.call-done.vol_ref), custom_call_target="tpu_custom_call" | custom-call | flops 8589934592 | bytes 10485760 | tf_op jit(solution)/shard_map/pallas_call | solution.py:91
  107.0 1.4 copy-done.1
  108.4 9.8 %shard_map.88 = f32[1,1536]{1,0:T(1,128)} custom-call(bf16[16,16,32,128]{3,2,1,0:T(8,128)(2,1)} %copy-done.1, f32[16,16,32,128]{3,2,1,0:T(8,128)} %get-tuple-element.7.proj_ref, f32[512,128]{1,0:T(8,128)} %bitcast.26), custom_call_target="tpu_custom_call" | custom-call | flops 4194304 | bytes 6291456 | tf_op jit(solution)/shard_map/pallas_call | solution.py:137
  118.2 0.7 reduce
  118.9 0.7 broadcast_in_dim.21
  119.6 6.4 %all-to-all-start.2 = ((f32[16,1,1536]{2,1,0:T(1,128)}), f32[16,1,1536]{2,1,0:T(1,128)S(1)}, u32[]{:S(2)}, u32[]{:S(2)}) async-start(f32[16,1,1536]{2,1,0:T(1,128)} %broadcast_in_dim.21), calls=%async_computation.2 | async-start | bytes 196608 | tf_op jit(solution)/shard_map/all_to_all | solution.py:264
  126.6 5.2 %all-to-all-done.2 = f32[16,1,1536]{2,1,0:T(1,128)S(1)} async-done(((f32[16,1,1536]{2,1,0:T(1,128)}), f32[16,1,1536]{2,1,0:T(1,128)S(1)}, u32[]{:S(2)}, u32[]{:S(2)}) %all-to-all-start.2) | async-done | bytes 98336 | tf_op jit(solution)/shard_map/all_to_all | solution.py:264
  132.5 11.2 %shard_map.89 = (bf16[8192,256]{1,0:T(8,128)(2,1)}, f32[1,512]{1,0:T(1,128)}) custom-call(f32[16,1536]{1,0:T(8,128)} %bitcast.24, bf16[16,16,32,128]{3,2,1,0:T(8,128)(2,1)} %copy-done.1, f32[16,16,32,128]{3,2,1,0:T(8,128)} %get-tuple-element.9.ctf_ref), custom_call_target="tpu_custom_call" | custom-call | flops 4194304 | bytes 10485760 | tf_op jit(solution)/shard_map/pallas_call | solution.py:180
  143.7 14.5 %shard_map.90 = bf16[16,128,256]{2,1,0:T(8,128)(2,1)} custom-call(f32[1,8192]{1,0:T(1,128)} %bitcast.29, bf16[8192,256]{1,0:T(8,128)(2,1)} %get-tuple-element.10.terms_ref), custom_call_target="tpu_custom_call" | custom-call | flops 8589934592 | bytes 5242880 | tf_op jit(solution)/shard_map/pallas_call | solution.py:218
  158.1 5.2 %all-to-all-start.3 = ((bf16[16,128,256]{2,1,0:T(8,128)(2,1)}), bf16[16,128,256]{2,1,0:T(8,128)(2,1)S(1)}, u32[]{:S(2)}, u32[]{:S(2)}) async-start(bf16[16,128,256]{2,1,0:T(8,128)(2,1)} %shard_map.90), calls=%async_computation.3 | async-start | bytes 2097152 | tf_op jit(solution)/shard_map/all_to_all | solution.py:272
  163.3 14.5 %shard_map.91 = bf16[16,128,256]{2,1,0:T(8,128)(2,1)} custom-call(f32[1,8192]{1,0:T(1,128)} %bitcast.30, bf16[8192,256]{1,0:T(8,128)(2,1)} %get-tuple-element.10.terms_ref), custom_call_target="tpu_custom_call" | custom-call | flops 8589934592 | bytes 5242880 | tf_op jit(solution)/shard_map/pallas_call | solution.py:218
  177.8 13.3 %all-to-all-done.3 = bf16[16,128,256]{2,1,0:T(8,128)(2,1)S(1)} async-done(((bf16[16,128,256]{2,1,0:T(8,128)(2,1)}), bf16[16,128,256]{2,1,0:T(8,128)(2,1)S(1)}, u32[]{:S(2)}, u32[]{:S(2)}) %all-to-all-start.3) | async-done | bytes 1048608 | tf_op jit(solution)/shard_map/all_to_all | solution.py:272
  191.1 5.2 %all-to-all-start.4 = ((bf16[16,128,256]{2,1,0:T(8,128)(2,1)}), bf16[16,128,256]{2,1,0:T(8,128)(2,1)S(1)}, u32[]{:S(2)}, u32[]{:S(2)}) async-start(bf16[16,128,256]{2,1,0:T(8,128)(2,1)} %shard_map.91), calls=%async_computation.4 | async-start | bytes 2097152 | tf_op jit(solution)/shard_map/all_to_all | solution.py:272
  196.3 1.2 dynamic-slice_bitcast_fusion
  197.6 25.9 %all-to-all-done.4 = bf16[16,128,256]{2,1,0:T(8,128)(2,1)S(1)} async-done(((bf16[16,128,256]{2,1,0:T(8,128)(2,1)}), bf16[16,128,256]{2,1,0:T(8,128)(2,1)S(1)}, u32[]{:S(2)}, u32[]{:S(2)}) %all-to-all-start.4) | async-done | bytes 1048608 | tf_op jit(solution)/shard_map/all_to_all | solution.py:272
  223.7 0.7 pad_maximum_fusion
  (25 shorter events, 6.3 us)
Async XLA Ops:
  7.2 22.8 %copy-start = (bf16[2,128,2048]{2,1,0:T(8,128)(2,1)S(1)}, bf16[2,128,2048]{2,1,0:T(8,128)(2,1)}, u32[]{:S(2)}) copy-start(bf16[2,128,2048]{2,1,0:T(8,128)(2,1)} %param.13) | copy-start | bytes 3145732
  12.2 13.0 %all-to-all-start = ((f32[16,1,544]{2,1,0:T(1,128)}), f32[16,1,544]{2,1,0:T(1,128)S(1)}, u32[]{:S(2)}, u32[]{:S(2)}) async-start(f32[16,1,544]{2,1,0:T(1,128)} %broadcast_in_dim.9), calls=%async_computation | async-start | bytes 81920 | tf_op jit(solution)/shard_map/all_to_all | solution.py:253
  25.2 81.8 %all-to-all-start.1 = ((bf16[16,16,32,128]{3,2,1,0:T(8,128)(2,1)}), bf16[16,16,32,128]{3,2,1,0:T(8,128)(2,1)S(1)}, u32[]{:S(2)}, u32[]{:S(2)}) async-start(bf16[16,16,32,128]{3,2,1,0:T(8,128)(2,1)} %shard_map.86), calls=%async_computation.1 | async-start | bytes 4194304 | tf_op jit(solution)/shard_map/all_to_all | solution.py:258
  29.9 58.2 %all-gather.2.cloned.1.call-start = ((), (), s32[]{:S(2)}) async-start(), calls=%async_computation.5 | async-start | bytes 1114112 | tf_op jit(solution)/shard_map/all_gather | solution.py:247
  107.0 1.4 copy-start.1
  119.6 12.3 %all-to-all-start.2 = ((f32[16,1,1536]{2,1,0:T(1,128)}), f32[16,1,1536]{2,1,0:T(1,128)S(1)}, u32[]{:S(2)}, u32[]{:S(2)}) async-start(f32[16,1,1536]{2,1,0:T(1,128)} %broadcast_in_dim.21), calls=%async_computation.2 | async-start | bytes 196608 | tf_op jit(solution)/shard_map/all_to_all | solution.py:264
  158.1 33.0 %all-to-all-start.3 = ((bf16[16,128,256]{2,1,0:T(8,128)(2,1)}), bf16[16,128,256]{2,1,0:T(8,128)(2,1)S(1)}, u32[]{:S(2)}, u32[]{:S(2)}) async-start(bf16[16,128,256]{2,1,0:T(8,128)(2,1)} %shard_map.90), calls=%async_computation.3 | async-start | bytes 2097152 | tf_op jit(solution)/shard_map/all_to_all | solution.py:272
  191.1 32.4 %all-to-all-start.4 = ((bf16[16,128,256]{2,1,0:T(8,128)(2,1)}), bf16[16,128,256]{2,1,0:T(8,128)(2,1)S(1)}, u32[]{:S(2)}, u32[]{:S(2)}) async-start(bf16[16,128,256]{2,1,0:T(8,128)(2,1)} %shard_map.91), calls=%async_computation.4 | async-start | bytes 2097152 | tf_op jit(solution)/shard_map/all_to_all | solution.py:272
Sparse Core Ops, SparseCore 0:
  33.8 54.3 all-gather.1

commit v2 on v0

v2 whole, which is shorter than its diff:
```python
import functools
import jax
import jax.numpy as jnp
from jax import lax
from jax.experimental import pallas as pl
from jax.experimental.pallas import tpu as pltpu
from jax.sharding import PartitionSpec as P

F32 = jnp.float32
BF16 = jnp.bfloat16
LANES = 128
PHASE = 0.3
EPS = 1e-05
MIB = 1024 * 1024
RING = 4
WHOLE = pl.BlockSpec(memory_space=pltpu.VMEM)
SCALARS = pl.BlockSpec(memory_space=pltpu.SMEM)


def params(mib):
    return pltpu.CompilerParams(vmem_limit_bytes=mib * MIB)


def cost(flops, moved):
    return pl.CostEstimate(flops=flops, bytes_accessed=moved, transcendentals=0)


def split_kernel(slices, img_ref, out_ref, scratch):
    step, rows, _ = img_ref.shape
    block_rows = rows // slices
    for h in range(2):
        half = img_ref[:, :, h * LANES : (h + 1) * LANES].astype(F32)
        scratch[h] = half.reshape(step * rows, LANES)
    for j in range(slices):
        for b in range(block_rows):
            picked = pl.ds(j * block_rows + b, step, stride=rows)
            for h in range(2):
                out_ref[2 * b + h, j] = scratch[h, picked, :].astype(BF16)


def split_images(images, slices):
    particles, rows, width = images.shape
    block_rows = rows // slices
    step = 16
    return pl.pallas_call(
        functools.partial(split_kernel, slices),
        grid=(particles // step,),
        in_specs=[pl.BlockSpec((step, rows, width), lambda i: (i, 0, 0))],
        out_specs=pl.BlockSpec((2 * block_rows, slices, step, LANES), lambda i: (0, 0, i, 0)),
        out_shape=pltpu.HBM((2 * block_rows, slices, particles, LANES), BF16),
        scratch_shapes=[pltpu.VMEM((2, step * rows, LANES), F32)],
        compiler_params=params(56),
        cost_estimate=cost(0, images.size * 4),
    )(images)


def meta_kernel(
    capacity, blocks, owned, owner_ref, assign_ref, orient_ref, focus_ref, table_ref, meta_ref
):
    slices, particles = owner_ref.shape
    turns = table_ref.shape[1]
    count = slices * particles
    owners = (meta_ref.shape[2] - 2 * count - LANES) // capacity
    turn = lax.broadcasted_iota(jnp.int32, (turns, particles), 0)
    one_hot = (turn == orient_ref[...]).astype(BF16)
    place = jnp.dot(table_ref[...].astype(F32).astype(BF16), one_hot, preferred_element_type=F32)
    place = place + (assign_ref[...] * owned).astype(F32)
    owner = owner_ref[...].astype(F32)
    owner_row = jnp.concatenate([owner[j : j + 1, :] for j in range(slices)], axis=1)
    place_row = jnp.concatenate([place[j : j + 1, :] for j in range(slices)], axis=1)
    holder = lax.broadcasted_iota(jnp.int32, (owners, count), 0).astype(F32)
    match = (holder == owner_row).astype(BF16)
    before = lax.broadcasted_iota(jnp.int32, (count, count), 0)
    before = before < lax.broadcasted_iota(jnp.int32, (count, count), 1)
    earlier = jnp.dot(match, before.astype(BF16), preferred_element_type=F32)
    rank = jnp.sum(earlier * match.astype(F32), axis=0, keepdims=True)
    slot = owner_row * float(capacity) + rank
    slot_col = jnp.broadcast_to(slot, (8, count)).T[:, :1]
    every = lax.broadcasted_iota(jnp.int32, (count, owners * capacity), 1).astype(F32)
    at_slot = (every == slot_col).astype(BF16)
    shifted = jnp.broadcast_to(place_row + 1.0, (8, count)).astype(BF16)
    filled = jnp.dot(shifted, at_slot, preferred_element_type=F32)[:1] - 1.0
    last = 2 * count + owners * capacity
    tail = jnp.zeros((1, meta_ref.shape[2] - last - particles), F32)
    focus = jnp.concatenate([focus_ref[...].astype(F32), tail], axis=1)
    for d in range(meta_ref.shape[0]):
        meta_ref[d, :, :count] = owner_row * float(blocks) + place_row
        meta_ref[d, :, count : 2 * count] = slot
        meta_ref[d, :, 2 * count : last] = filled
        meta_ref[d, :, last:] = focus


def make_meta(owner, assign, orient, defocus, table, capacity, owners, blocks, owned, copies):
    particles, slices = owner.shape
    length = 2 * slices * particles + owners * capacity + LANES
    return pl.pallas_call(
        functools.partial(meta_kernel, capacity, blocks, owned),
        out_shape=jax.ShapeDtypeStruct((copies, 1, length), F32),
        compiler_params=params(56),
        cost_estimate=cost(100 * MIB, MIB),
    )(owner.T, assign[None, :], orient[None, :], defocus[None, :], table.T)


def after_kernel(x_ref, y_ref, z_ref, out_ref):
    pass


def after(x, y, z):
    hbm = pl.BlockSpec(memory_space=pltpu.HBM)
    anywhere = pl.BlockSpec(memory_space=pl.ANY)
    return pl.pallas_call(
        after_kernel,
        in_specs=[hbm, anywhere, anywhere],
        out_specs=hbm,
        out_shape=pltpu.HBM(x.shape, x.dtype),
        input_output_aliases={0: 0},
        compiler_params=params(1),
    )(x, y, z)


def contrast_kernel(extent, start, row_ref, meta_ref, ctf_ref):
    held, slices, particles, _ = ctf_ref.shape
    for k in range(held):
        focus = meta_ref[k, :, start : start + LANES]
        focus = jnp.broadcast_to(focus, (LANES, LANES)).T[:particles, :] / extent
        column = lax.broadcasted_iota(jnp.int32, (particles, LANES), 1).astype(F32)
        angle = focus * (column * column)
        cos_col, sin_col = jnp.cos(angle), jnp.sin(angle)
        row = column * 8.0 + row_ref[0]
        angle = focus * (row * row) + PHASE
        cos_row, sin_row = jnp.cos(angle), jnp.sin(angle)
        for j in range(slices):
            ctf_ref[k, j] = sin_row[:, j : j + 1] * cos_col + cos_row[:, j : j + 1] * sin_col


def contrast(row, meta, start, slices, particles, extent):
    senders, _, length = meta.shape
    held = 4
    return pl.pallas_call(
        functools.partial(contrast_kernel, extent, start),
        grid=(senders // held,),
        in_specs=[SCALARS, pl.BlockSpec((held, 1, length), lambda i: (i, 0, 0))],
        out_specs=pl.BlockSpec((held, slices, particles, LANES), lambda i: (i, 0, 0, 0)),
        out_shape=pltpu.HBM((senders, slices, particles, LANES), F32),
        compiler_params=params(8),
        cost_estimate=cost(1000 * MIB, 4 * MIB),
    )(row, meta)


def project_kernel(
    count, at_ref, meta_ref, ctf_ref, vol0, vol1, vol2, vol3, proj_ref, power_ref, pairs, one_hot
):
    taken, slices, particles, _ = proj_ref.shape
    held, blocks, _ = vol0.shape
    owned = blocks // 2
    holders = RING * held

    @pl.when(pl.program_id(0) == 0)
    def _():
        for t, vol in enumerate((vol0, vol1, vol2, vol3)):
            for i in range(held):
                where = pl.ds((t * held + i) * owned, owned)
                pairs[where, :LANES] = vol[i, :owned, :]
                pairs[where, LANES:] = vol[i, owned:, :]

    at_y = at_ref[0].astype(F32)
    at_z = at_ref[1].astype(F32)
    lane = lax.broadcasted_iota(jnp.int32, (count, LANES), 1).astype(F32)
    zero = jnp.zeros((count, owned), BF16)
    uppers = []
    for k in range(taken):
        key = meta_ref[k, :, :count]
        owner = jnp.floor(key * (1.0 / blocks))
        place = key - owner * float(blocks)
        upper = (place >= float(owned)).astype(F32)
        place = place - upper * float(owned)
        y = jnp.floor(owner * (1.0 / held))
        z = at_z - (owner - y * float(held))
        y = at_y - y
        y = jnp.where(y < 0.0, y + float(RING), y)
        z = jnp.where(z < 0.0, z + float(RING), z)
        rows = jnp.concatenate([place] * 8 + [upper] * 8 + [y * float(held) + z] * 8, axis=0).T
        hit = jnp.broadcast_to(rows[:, :1], (count, LANES)) == lane
        hit = hit.astype(BF16)
        uppers.append(jnp.broadcast_to(rows[:, 8:9], (count, LANES)) > 0.5)
        holder = jnp.broadcast_to(rows[:, 16:17], (count, LANES)).astype(BF16)
        for i in range(holders):
            one_hot[k, :, i * owned : (i + 1) * owned] = jnp.where(holder == i, hit, zero)
    powers = []
    for k in range(taken):
        acc = jnp.dot(one_hot[k], pairs[...], preferred_element_type=F32)
        picked = jnp.where(uppers[k], acc[:, LANES:], acc[:, :LANES])
        picked = picked.reshape(slices, particles, LANES)
        power = jnp.zeros((particles, LANES), F32)
        for j in range(slices):
            proj = ctf_ref[k, j] * picked[j]
            power += proj * proj
            proj_ref[k, j] = proj
        powers.append(power)
    power_ref[...] = jnp.sum(jnp.concatenate(powers, axis=0).T, axis=0, keepdims=True)


def project(at, meta, ctf, vols):
    senders, slices, particles, _ = ctf.shape
    held, blocks, _ = vols[0].shape
    span = RING * held * blocks // 2
    count = slices * particles
    taken = 4
    block = pl.BlockSpec((taken, slices, particles, LANES), lambda i: (i, 0, 0, 0))
    return pl.pallas_call(
        functools.partial(project_kernel, count),
        grid=(senders // taken,),
        in_specs=[
            SCALARS,
            pl.BlockSpec((taken, 1, meta.shape[2]), lambda i: (i, 0, 0)),
            block,
        ]
        + [pl.BlockSpec((held, blocks, LANES), lambda i: (0, 0, 0))] * RING,
        out_specs=[block, pl.BlockSpec((1, taken * particles), lambda i: (0, i))],
        out_shape=[
            pltpu.HBM(ctf.shape, F32),
            jax.ShapeDtypeStruct((1, senders * particles), F32),
        ],
        scratch_shapes=[
            pltpu.VMEM((span, 2 * LANES), BF16),
            pltpu.VMEM((taken, count, span), BF16),
        ],
        compiler_params=params(24),
        cost_estimate=cost(2 * senders * count * span * 2 * LANES, 10 * MIB),
    )(at, meta, ctf, *vols)


def sums_kernel(img_ref, proj_ref, power_ref, out_ref, cross, noise):
    senders, slices, particles, _ = img_ref.shape

    @pl.loop(0, senders)
    def _(s):
        cross_sum = jnp.zeros((particles, LANES), F32)
        noise_sum = jnp.zeros((particles, LANES), F32)
        for j in range(slices):
            img = img_ref[s, j].astype(F32)
            cross_sum += img * proj_ref[s, j]
            noise_sum += img * img
        cross[pl.ds(s * particles, particles), :] = cross_sum
        noise[pl.ds(s * particles, particles), :] = noise_sum

    total = senders * particles
    rows = [jnp.sum(ref[...].T, axis=0, keepdims=True) for ref in (cross, noise)]
    rows.append(power_ref[...])
    for d in range(senders):
        for i, row in enumerate(rows):
            out_ref[d, :, i * total : (i + 1) * total] = row


def partial_sums(img, proj, power):
    senders, slices, particles, _ = img.shape
    total = senders * particles
    return pl.pallas_call(
        sums_kernel,
        in_specs=[WHOLE] * 3,
        out_specs=WHOLE,
        out_shape=jax.ShapeDtypeStruct((senders, 1, 3 * total), F32),
        scratch_shapes=[pltpu.VMEM((total, LANES), F32)] * 2,
        compiler_params=params(12),
        cost_estimate=cost(img.size * 4, img.size * 6),
    )(img, proj, power)


def terms_kernel(pixels, part_ref, img_ref, ctf_ref, terms_ref, corr_ref, weight_col):
    senders, slices, particles, _ = img_ref.shape
    total = senders * particles
    sums = part_ref[0]
    for d in range(1, senders):
        sums = sums + part_ref[d]
    cross, power = sums[:, :total], sums[:, 2 * total :]
    noise = sums[:, total : 2 * total] / pixels + EPS
    corr = cross / jnp.sqrt((power + EPS) * noise)
    corr_ref[...] = corr
    weight = jax.nn.sigmoid(corr) / noise
    weight_col[...] = jnp.broadcast_to(weight, (LANES, total)).T

    @pl.loop(0, senders)
    def _(s):
        weight = weight_col[pl.ds(s * particles, particles), :]
        for j in range(slices):
            ctf = ctf_ref[s, j]
            scaled = weight * ctf
            rows = pl.ds(j * particles, particles)
            terms_ref[s, rows, :LANES] = (scaled * img_ref[s, j].astype(F32)).astype(BF16)
            terms_ref[s, rows, LANES:] = (scaled * ctf).astype(BF16)


def make_terms(partials, img, ctf, pixels):
    senders, slices, particles, _ = img.shape
    total = senders * particles
    return pl.pallas_call(
        functools.partial(terms_kernel, float(pixels)),
        in_specs=[WHOLE] * 3,
        out_specs=[WHOLE] * 2,
        out_shape=[
            jax.ShapeDtypeStruct((senders, slices * particles, 2 * LANES), BF16),
            jax.ShapeDtypeStruct((1, total), F32),
        ],
        scratch_shapes=[pltpu.VMEM((total, LANES), F32)],
        compiler_params=params(12),
        cost_estimate=cost(img.size * 4, img.size * 10),
    )(partials, img, ctf)


def scatter_kernel(capacity, offsets, at_ref, slot_ref, place_ref, terms_ref, out_ref, sorted_ref):
    senders, rows, width = terms_ref.shape
    blocks = out_ref.shape[1] * 2 // 3
    owned = blocks // 2
    holders = [at_ref[0] * RING + lax.rem(at_ref[1] + u, RING) for u in offsets]
    place_in = lax.broadcasted_iota(jnp.int32, (capacity, rows), 0)
    slot_at = [(place_in + h * capacity).astype(F32) for h in holders]
    slot_at = jnp.concatenate(slot_at, axis=0)
    for s in range(senders):
        pick = (slot_at == slot_ref[s]).astype(BF16)
        got = jnp.dot(pick, terms_ref[s], preferred_element_type=F32).astype(BF16)
        for i in range(len(offsets)):
            sorted_ref[i, s * capacity : (s + 1) * capacity, :] = got[
                i * capacity : (i + 1) * capacity
            ]
    block_at = lax.broadcasted_iota(jnp.int32, (blocks, senders * capacity), 0).astype(F32)
    for i, h in enumerate(holders):
        one_hot = (block_at == place_ref[h]).astype(BF16)
        summed = jnp.dot(one_hot, sorted_ref[i], preferred_element_type=F32)
        denom = jnp.where(at_ref[2] == 0, summed[:owned, LANES:], summed[owned:, LANES:])
        out_ref[i, :blocks, :] = summed[:, :LANES].astype(out_ref.dtype)
        out_ref[i, blocks:, :] = denom.astype(out_ref.dtype)


def scatter(at, offsets, slots, places, terms, blocks, capacity, kind):
    senders, rows, width = terms.shape
    held = len(offsets)
    return pl.pallas_call(
        functools.partial(scatter_kernel, capacity, offsets),
        in_specs=[SCALARS] + [WHOLE] * 3,
        out_specs=WHOLE,
        out_shape=jax.ShapeDtypeStruct((held, blocks * 3 // 2, LANES), kind),
        scratch_shapes=[pltpu.VMEM((held, senders * capacity, width), BF16)],
        compiler_params=params(12),
        cost_estimate=cost(
            2 * senders * held * capacity * width * (rows + blocks), 5 * MIB
        ),
    )(at, slots, places, terms)


def fold_kernel(own_ref, got1, got2, got3, *outs):
    for i, ref in enumerate(outs):
        total = own_ref[i]
        for got in (got1, got2, got3):
            total = total + got[i].astype(F32)
        ref[...] = total.astype(ref.dtype)


def fold(own, got, kinds):
    _, rows, width = own.shape
    return pl.pallas_call(
        fold_kernel,
        in_specs=[WHOLE] * 4,
        out_specs=[WHOLE] * len(kinds),
        out_shape=[jax.ShapeDtypeStruct((rows, width), k) for k in kinds],
        compiler_params=params(4),
        cost_estimate=cost(own.size * 4, own.size * 11),
    )(own, *got)


def ring(x, axis, size, step, shift):
    def target(i):
        place = i // step % RING
        return i + ((place + shift) % RING - place) * step

    return lax.ppermute(x, axis, [(i, target(i)) for i in range(size)])


def shards(images, defocus, assign, orient, owner, slice_loc, volume):
    owners = lax.axis_size("cls")
    groups = lax.axis_size("dom")
    me = lax.axis_index("dom")
    at = lax.axis_index("cls")
    at_y, at_z = at // RING, at % RING
    particles, image_rows, width = images.shape
    classes, owned, block_len = volume.shape
    slices = owner.shape[1]
    blocks = classes * owned
    rows = slices * particles
    capacity = 5 * rows // (2 * owners)

    at_yz = jnp.stack([at_y, at_z])

    meta = make_meta(
        owner, assign, orient, defocus, slice_loc, capacity, owners, blocks, owned, groups
    )
    meta = lax.all_to_all(meta, "dom", 0, 0, tiled=True)
    piece = lax.dynamic_slice_in_dim(volume, me * LANES, LANES, axis=2).reshape(blocks, LANES)
    near = jnp.stack([piece] + [ring(piece, "cls", owners, 1, t) for t in range(1, RING)])
    img = after(split_images(images, slices), near, meta)
    img = lax.all_to_all(img, "dom", 0, 0, tiled=True)
    vols = [near] + [ring(near, "cls", owners, RING, t) for t in range(1, RING)]

    slots = meta[:, :, rows : 2 * rows]
    last = 2 * rows + owners * capacity
    filled = meta[:, 0, 2 * rows : last].reshape(groups, owners, capacity).transpose(1, 0, 2)
    filled = filled.reshape(owners, 1, groups * capacity)

    row = (me // 2).astype(F32).reshape(1)
    ctf = contrast(row, meta, last, slices, particles, float(image_rows * image_rows))
    proj, power = project(at_yz, meta, ctf, vols)
    partial = partial_sums(img, proj, power)
    partial = lax.all_to_all(partial, "dom", 0, 0, tiled=True)
    terms, corr = make_terms(partial, img, ctf, image_rows * width)
    correlation = lax.dynamic_slice_in_dim(corr[0], me * particles, particles)

    def by_y(offsets, kinds):
        def part(t, kind):
            to = jnp.stack([(at_y + t) % RING, at_z, me % 2])
            return scatter(to, offsets, slots, filled, terms, blocks, capacity, kind)

        got = [ring(part(t, BF16), "cls", owners, RING, t) for t in (2, 1, 3)]
        return fold(part(0, F32), got, kinds)

    far, right = by_y((2, 1), (BF16, BF16))
    far, right = ring(far, "cls", owners, 1, 2), ring(right, "cls", owners, 1, 1)
    left, total = by_y((3, 0), (BF16, F32))
    left = ring(left, "cls", owners, 1, 3)
    total = total + far.astype(F32) + right.astype(F32) + left.astype(F32)
    numer, mine = total[:blocks], total[blocks:]
    other = lax.ppermute(mine, "dom", [(i, i ^ 1) for i in range(groups)])
    first = me % 2 == 0
    denom = jnp.concatenate([jnp.where(first, mine, other), jnp.where(first, other, mine)])
    new_volume = numer / (denom + 1.0)
    return (new_volume.reshape(classes, owned, LANES), correlation)


def solution(mesh):
    placed = (
        P(("dom", "cls"), None, None),
        P(("dom", "cls")),
        P(("dom", "cls")),
        P(("dom", "cls")),
        P(("dom", "cls"), None),
        P(),
        P(None, "cls", None),
    )
    return jax.shard_map(
        shards,
        mesh=mesh,
        in_specs=placed,
        out_specs=(P(None, "cls", "dom"), P(("dom", "cls"))),
        check_vma=False,
    )
```

time: 747 us -> 125 us (0.17)
  waiting for transfers between devices: 539 us -> 15.4 us
  local copies, waits for them, and re-layouts: 101 us -> 11.6 us
  other arithmetic: 58.6 us -> 1.15 us
  Pallas kernels: 0 us -> 44 us
  starting transfers between devices: 19.1 us -> 51.5 us
  between operations: 14 us -> 0.86 us
  matrix products: 10.9 us -> 0 us
    all_to_all x2 -> x3, waiting for transfers between devices: 252 us -> 2.08 us  [the longest x1 2.07 us: shards(): partial = lax.all_to_all(partial, 'dom', 0, 0, tiled=True)]
    all_gather x1 -> x0, waiting for transfers between devices: 175 us -> none  [shards(): piece = lax.all_gather(volume, 'cls', axis=1, tiled=True)]
    reduce_scatter x2 -> x0, waiting for transfers between devices: 111 us -> none  [the longest x1 67.6 us: shards(): lax.psum_scatter(numer_full, 'dom', scatter_dimension=2, tiled=True)]
    pallas_call x0 -> x17, Pallas kernels: none -> 44 us  [the longest x1 14.8 us: project(): pl.pallas_call(functools.partial(project_kernel, count), grid=(senders //...]
    gather x7 -> x0, local copies, waits for them, and re-layouts: 38.5 us -> none  [the longest x2 17.6 us: shards(): picked = piece.reshape(classes * span, block_len)[class_flat * span + safe]]
    ppermute x0 -> x16, starting transfers between devices: none -> 30.6 us  [the longest x15 28.4 us: ring(): return lax.ppermute(x, axis, [(i, target(i)) for i in range(size)])]
    convert_element_type x7 -> x0, other arithmetic: 20.3 us -> none  [the longest x1 15.8 us: shards(): (scaled * samples).astype(jnp.bfloat16).reshape(row_count, block_len)]
    reshape x3 -> x1, local copies, waits for them, and re-layouts: 20.5 us -> 1.08 us  [shards(): filled = filled.reshape(owners, 1, groups * capacity)]
  transfers between devices with their start and end apart: 5 -> 19, of which waited for: 4 -> 5; matrix products, arithmetic and copies ran while one was open for 19% -> 4% of each run, Pallas kernels for 0% -> 29%
where the time goes in v2:
time: 125 us; the launch traced here: 124 us
  starting transfers between devices  51.5 us (41%)
  Pallas kernels  44 us (35%)
  waiting for transfers between devices  15.4 us (12%)
  local copies, waits for them, and re-layouts  11.6 us (9%)
    ppermute x15, starting transfers between devices, ring(): return lax.ppermute(x, axis, [(i, target(i)) for i in range(size)])  28.4 us
    pallas_call x1, Pallas kernels, project(): pl.pallas_call(functools.partial(project_kernel, count), grid=(senders //...  14.8 us
    pallas_call x8, Pallas kernels, scatter(): pl.pallas_call(functools.partial(scatter_kernel, capacity, offsets), in_s...  13.9 us
    ppermute x15, waiting for transfers between devices, ring(): return lax.ppermute(x, axis, [(i, target(i)) for i in range(size)])  13 us
    all_to_all x1, starting transfers between devices, shards(): img = lax.all_to_all(img, 'dom', 0, 0, tiled=True)  7.48 us
    unnamed x12, local copies, waits for them, and re-layouts  7.26 us
    all_to_all x1, starting transfers between devices, shards(): meta = lax.all_to_all(meta, 'dom', 0, 0, tiled=True)  7.17 us
    all_to_all x1, starting transfers between devices, shards(): partial = lax.all_to_all(partial, 'dom', 0, 0, tiled=True)  6.33 us
  transfers between devices with their start and end apart: 19, of which 5 were waited for; matrix products, arithmetic and copies ran while one was open for 4% of the time, Pallas kernels for 29%

profile of v2, /device:TPU:1, one launch (start us, length us, event | category | flops | bytes accessed | tf_op | source)
XLA Modules:
  0.0 124.5 jit_solution(16764510067929727922)
XLA Ops:
  0.6 2.5 %shard_map.86 = f32[16,1,2432]{2,1,0:T(1,128)} custom-call(s32[16,32]{1,0:T(8,128)} %bitcast.34, s32[1,32]{1,0:T(1,128)} %bitcast.35, s32[1,32]{1,0:T(1,128)} %bitcast.36, bf16[1,32]{1,0:T(2,128)(2,1)} %bitcast.37, s32[16,512]{1,0:T(8,128)} %bitcast.33), custom_call_target="tpu_custom_call" | custom-call | flops 104857600 | bytes 1048576 | tf_op jit(solution)/shard_map/pallas_call | solution.py:96
  3.1 7.2 %all-to-all-start = ((f32[16,1,2432]{2,1,0:T(1,128)}), f32[16,1,2432]{2,1,0:T(1,128)S(1)}, u32[]{:S(2)}, u32[]{:S(2)}) async-start(f32[16,1,2432]{2,1,0:T(1,128)} %shard_map.86), calls=%async_computation | async-start | bytes 311296 | tf_op jit(solution)/shard_map/all_to_all | solution.py:396
  10.3 5.2 %collective-permute-start.2 = (bf16[256,128]{1,0:T(8,128)(2,1)S(1)}, bf16[256,128]{1,0:T(8,128)(2,1)S(1)}, u32[]{:S(2)}, u32[]{:S(2)}) collective-permute-start(bf16[256,128]{1,0:T(8,128)(2,1)S(1)} %bitcast.25), channel_id=1, source_target_pairs={{0,3},{1,0},{2,1},{3,2},{4,7},{5,4},{6,5},{7,6},{8,11},{9,8},{10,9... | collective-permute-start | bytes 196616 | tf_op jit(solution)/shard_map/ppermute | solution.py:375
  16.7 2.1 %collective-permute-start = (bf16[256,128]{1,0:T(8,128)(2,1)S(1)}, bf16[256,128]{1,0:T(8,128)(2,1)S(1)}, u32[]{:S(2)}, u32[]{:S(2)}) collective-permute-start(bf16[256,128]{1,0:T(8,128)(2,1)S(1)} %bitcast.27), channel_id=1, source_target_pairs={{0,1},{1,2},{2,3},{3,0},{4,5},{5,6},{6,7},{7,4},{8,9},{9,10},{10,1... | collective-permute-start | bytes 196616 | tf_op jit(solution)/shard_map/ppermute | solution.py:375
  18.8 4.8 %shard_map.87.x_ref = bf16[16,16,32,128]{3,2,1,0:T(8,128)(2,1)} custom-call(bf16[32,128,256]{2,1,0:T(8,128)(2,1)} %img_ref.1), custom_call_target="tpu_custom_call" | custom-call | bytes 4194304 | tf_op jit(solution)/shard_map/pallas_call | solution.py:45
  24.4 7.5 %all-to-all-start.1 = ((bf16[16,16,32,128]{3,2,1,0:T(8,128)(2,1)}), bf16[16,16,32,128]{3,2,1,0:T(8,128)(2,1)S(1)}, u32[]{:S(2)}, u32[]{:S(2)}) async-start(bf16[16,16,32,128]{3,2,1,0:T(8,128)(2,1)} %shard_map.88), calls=%async_computation.1 | async-start | bytes 4194304 | tf_op jit(solution)/shard_map/all_to_all | solution.py:400
  33.3 2.6 %collective-permute-start.4 = (bf16[4,256,128]{2,1,0:T(8,128)(2,1)}, bf16[4,256,128]{2,1,0:T(8,128)(2,1)}, u32[]{:S(2)}, u32[]{:S(2)}) collective-permute-start(bf16[4,256,128]{2,1,0:T(8,128)(2,1)} %copy-done.4), channel_id=1, source_target_pairs={{0,8},{1,9},{2,10},{3,11},{4,12},{5,13},{6,14},{7,15},{8,0},{9,1},... | collective-permute-start | bytes 786440 | tf_op jit(solution)/shard_map/ppermute | solution.py:375
  37.1 5.3 %shard_map.89.ctf_ref = f32[16,16,32,128]{3,2,1,0:T(8,128)} custom-call(f32[1]{0:T(128)} %bitcast.15.row_ref, f32[16,1,2432]{2,1,0:T(1,128)S(1)} %all-to-all-done.z_ref.meta_ref), custom_call_target="tpu_custom_call" | custom-call | flops 1048576000 | bytes 4194304 | tf_op jit(solution)/shard_map/pallas_call | solution.py:139
  42.5 5.6 %collective-permute-done.4.vol2 = bf16[4,256,128]{2,1,0:T(8,128)(2,1)} collective-permute-done((bf16[4,256,128]{2,1,0:T(8,128)(2,1)}, bf16[4,256,128]{2,1,0:T(8,128)(2,1)}, u32[]{:S(2)}, u32[]{:S(2)}) %collective-permute-start.4) | collective-permute-done | bytes 262176 | tf_op jit(solution)/shard_map/ppermute | solution.py:375
  48.1 2.2 %copy-done.1 = f32[16,16,32,128]{3,2,1,0:T(8,128)S(1)} copy-done((f32[16,16,32,128]{3,2,1,0:T(8,128)S(1)}, f32[16,16,32,128]{3,2,1,0:T(8,128)}, u32[]{:S(2)}) %copy-start.1) | copy-done | bytes 4194328
  50.3 14.8 %shard_map.90 = (f32[16,16,32,128]{3,2,1,0:T(8,128)}, f32[1,512]{1,0:T(1,128)S(1)}) custom-call(s32[2]{0:T(128)S(1)} %pad_add_fusion.at_ref, f32[16,1,2432]{2,1,0:T(1,128)S(1)} %all-to-all-done.z_ref.meta_ref, f32[16,16,32,128]{3,2,1,0:T(8,128)S(1)} %copy-done.1, bf16[4,256,128]{2,1,0:T(8,128)(2,1)S(1)} %copy-done.5, ...), custom_call_target="tpu_custom_call" | custom-call | flops 8589934592 | bytes 10485760 | tf_op jit(solution)/shard_map/pallas_call | solution.py:210
  65.1 2.2 %copy-done.3 = f32[16,16,32,128]{3,2,1,0:T(8,128)S(1)} copy-done((f32[16,16,32,128]{3,2,1,0:T(8,128)S(1)}, f32[16,16,32,128]{3,2,1,0:T(8,128)}, u32[]{:S(2)}) %copy-start.3) | copy-done | bytes 4194328
  68.7 6.3 %all-to-all-start.2 = ((f32[16,1,1536]{2,1,0:T(1,128)}), f32[16,1,1536]{2,1,0:T(1,128)S(1)}, u32[]{:S(2)}, u32[]{:S(2)}) async-start(f32[16,1,1536]{2,1,0:T(1,128)} %shard_map.91), calls=%async_computation.2 | async-start | bytes 196608 | tf_op jit(solution)/shard_map/all_to_all | solution.py:412
  78.8 2.1 %all-to-all-done.2.part_ref = f32[16,1,1536]{2,1,0:T(1,128)S(1)} async-done(((f32[16,1,1536]{2,1,0:T(1,128)}), f32[16,1,1536]{2,1,0:T(1,128)S(1)}, u32[]{:S(2)}, u32[]{:S(2)}) %all-to-all-start.2) | async-done | bytes 98336 | tf_op jit(solution)/shard_map/all_to_all | solution.py:412
  80.8 2.2 %copy-done.2 = f32[16,16,32,128]{3,2,1,0:T(8,128)S(1)} copy-done((f32[16,16,32,128]{3,2,1,0:T(8,128)S(1)}, f32[16,16,32,128]{3,2,1,0:T(8,128)}, u32[]{:S(2)}) %copy-start.2) | copy-done | bytes 4194328
  84.1 1.7 %shard_map.94 = bf16[2,384,128]{2,1,0:T(8,128)(2,1)S(1)} custom-call(s32[3]{0:T(128)S(1)} %add_add_fusion.1.at_ref, f32[16,1,512]{2,1,0:T(1,128)S(1)} %slice.16.slot_ref, f32[16,1,1280]{2,1,0:T(1,128)S(1)} %reshape.17.place_ref, bf16[16,512,256]{2,1,0:T(8,128)(2,1)S(1)} %get-tuple-element.12.terms_ref), custom_call_target="tpu_custom_call" | custom-call | flops 1006632960 | bytes 5242880 | tf_op jit(solution)/shard_map/pallas_call | solution.py:337
  87.6 2.4 %collective-permute-start.6 = (bf16[2,384,128]{2,1,0:T(8,128)(2,1)S(1)}, bf16[2,384,128]{2,1,0:T(8,128)(2,1)S(1)}, u32[]{:S(2)}, u32[]{:S(2)}) collective-permute-start(bf16[2,384,128]{2,1,0:T(8,128)(2,1)S(1)} %shard_map.94), channel_id=1, source_target_pairs={{0,8},{1,9},{2,10},{3,11},{4,12},{5,13},{6,14},{7,15},{8,0},{9,1},... | collective-permute-start | bytes 589832 | tf_op jit(solution)/shard_map/ppermute | solution.py:375
  93.7 2.6 %collective-permute-start.8 = (bf16[2,384,128]{2,1,0:T(8,128)(2,1)S(1)}, bf16[2,384,128]{2,1,0:T(8,128)(2,1)S(1)}, u32[]{:S(2)}, u32[]{:S(2)}) collective-permute-start(bf16[2,384,128]{2,1,0:T(8,128)(2,1)S(1)} %shard_map.96), channel_id=1, source_target_pairs={{0,12},{1,13},{2,14},{3,15},{4,0},{5,1},{6,2},{7,3},{8,4},{9,5},{1... | collective-permute-start | bytes 589832 | tf_op jit(solution)/shard_map/ppermute | solution.py:375
  100.5 2.3 %collective-permute-start.11 = (bf16[2,384,128]{2,1,0:T(8,128)(2,1)S(1)}, bf16[2,384,128]{2,1,0:T(8,128)(2,1)S(1)}, u32[]{:S(2)}, u32[]{:S(2)}) collective-permute-start(bf16[2,384,128]{2,1,0:T(8,128)(2,1)S(1)} %shard_map.101), channel_id=1, source_target_pairs={{0,12},{1,13},{2,14},{3,15},{4,0},{5,1},{6,2},{7,3},{8,4},{9,5},{1... | collective-permute-start | bytes 589832 | tf_op jit(solution)/shard_map/ppermute | solution.py:375
  106.5 2.7 %collective-permute-start.14 = (bf16[384,128]{1,0:T(8,128)(2,1)S(1)}, bf16[384,128]{1,0:T(8,128)(2,1)S(1)}, u32[]{:S(2)}, u32[]{:S(2)}) collective-permute-start(bf16[384,128]{1,0:T(8,128)(2,1)S(1)} %get-tuple-element.16), channel_id=1, source_target_pairs={{0,3},{1,0},{2,1},{3,2},{4,7},{5,4},{6,5},{7,6},{8,11},{9,8},{10,9... | collective-permute-start | bytes 294920 | tf_op jit(solution)/shard_map/ppermute | solution.py:375
  110.0 3.3 %collective-permute-start.12 = (bf16[384,128]{1,0:T(8,128)(2,1)S(1)}, bf16[384,128]{1,0:T(8,128)(2,1)S(1)}, u32[]{:S(2)}, u32[]{:S(2)}) collective-permute-start(bf16[384,128]{1,0:T(8,128)(2,1)S(1)} %get-tuple-element.14), channel_id=1, source_target_pairs={{0,2},{1,3},{2,0},{3,1},{4,6},{5,7},{6,4},{7,5},{8,10},{9,11},{10,... | collective-permute-start | bytes 294920 | tf_op jit(solution)/shard_map/ppermute | solution.py:375
  113.3 2.1 %collective-permute-done.13 = bf16[384,128]{1,0:T(8,128)(2,1)S(1)} collective-permute-done((bf16[384,128]{1,0:T(8,128)(2,1)S(1)}, bf16[384,128]{1,0:T(8,128)(2,1)S(1)}, u32[]{:S(2)}, u32[]{:S(2)}) %collective-permute-start.13) | collective-permute-done | bytes 98336 | tf_op jit(solution)/shard_map/ppermute | solution.py:375
  115.4 5.2 %collective-permute-done.12 = bf16[384,128]{1,0:T(8,128)(2,1)S(1)} collective-permute-done((bf16[384,128]{1,0:T(8,128)(2,1)S(1)}, bf16[384,128]{1,0:T(8,128)(2,1)S(1)}, u32[]{:S(2)}, u32[]{:S(2)}) %collective-permute-start.12) | collective-permute-done | bytes 98336 | tf_op jit(solution)/shard_map/ppermute | solution.py:375
  120.7 2.2 %collective-permute-start.15 = (f32[128,128]{1,0:T(8,128)S(1)}, f32[128,128]{1,0:T(8,128)S(1)}, u32[]{:S(2)}, u32[]{:S(2)}) collective-permute-start(f32[128,128]{1,0:T(8,128)S(1)} %slice.19), channel_id=1, source_target_pairs={{0,16},{16,0},{32,48},{48,32},{64,80},{80,64},{96,112},{112,96},{1... | collective-permute-start | bytes 196616 | tf_op jit(solution)/shard_map/ppermute | solution.py:430
  (60 shorter events, 26.4 us)
Async XLA Ops:
  0.6 9.7 %copy-start = (bf16[2,128,2048]{2,1,0:T(8,128)(2,1)S(1)}, bf16[2,128,2048]{2,1,0:T(8,128)(2,1)}, u32[]{:S(2)}) copy-start(bf16[2,128,2048]{2,1,0:T(8,128)(2,1)} %param.13) | copy-start | bytes 3145732
  3.1 20.6 %all-to-all-start = ((f32[16,1,2432]{2,1,0:T(1,128)}), f32[16,1,2432]{2,1,0:T(1,128)S(1)}, u32[]{:S(2)}, u32[]{:S(2)}) async-start(f32[16,1,2432]{2,1,0:T(1,128)} %shard_map.86), calls=%async_computation | async-start | bytes 311296 | tf_op jit(solution)/shard_map/all_to_all | solution.py:396
  10.3 13.3 %collective-permute-start.2 = (bf16[256,128]{1,0:T(8,128)(2,1)S(1)}, bf16[256,128]{1,0:T(8,128)(2,1)S(1)}, u32[]{:S(2)}, u32[]{:S(2)}) collective-permute-start(bf16[256,128]{1,0:T(8,128)(2,1)S(1)} %bitcast.25), channel_id=1, source_target_pairs={{0,3},{1,0},{2,1},{3,2},{4,7},{5,4},{6,5},{7,6},{8,11},{9,8},{10,9... | collective-permute-start | bytes 196616 | tf_op jit(solution)/shard_map/ppermute | solution.py:375
  15.6 8.1 %collective-permute-start.1 = (bf16[256,128]{1,0:T(8,128)(2,1)S(1)}, bf16[256,128]{1,0:T(8,128)(2,1)S(1)}, u32[]{:S(2)}, u32[]{:S(2)}) collective-permute-start(bf16[256,128]{1,0:T(8,128)(2,1)S(1)} %bitcast.26), channel_id=1, source_target_pairs={{0,2},{1,3},{2,0},{3,1},{4,6},{5,7},{6,4},{7,5},{8,10},{9,11},{10,... | collective-permute-start | bytes 196616 | tf_op jit(solution)/shard_map/ppermute | solution.py:375
  16.7 6.9 %collective-permute-start = (bf16[256,128]{1,0:T(8,128)(2,1)S(1)}, bf16[256,128]{1,0:T(8,128)(2,1)S(1)}, u32[]{:S(2)}, u32[]{:S(2)}) collective-permute-start(bf16[256,128]{1,0:T(8,128)(2,1)S(1)} %bitcast.27), channel_id=1, source_target_pairs={{0,1},{1,2},{2,3},{3,0},{4,5},{5,6},{6,7},{7,4},{8,9},{9,10},{10,1... | collective-permute-start | bytes 196616 | tf_op jit(solution)/shard_map/ppermute | solution.py:375
  24.4 40.7 %all-to-all-start.1 = ((bf16[16,16,32,128]{3,2,1,0:T(8,128)(2,1)}), bf16[16,16,32,128]{3,2,1,0:T(8,128)(2,1)S(1)}, u32[]{:S(2)}, u32[]{:S(2)}) async-start(bf16[16,16,32,128]{3,2,1,0:T(8,128)(2,1)} %shard_map.88), calls=%async_computation.1 | async-start | bytes 4194304 | tf_op jit(solution)/shard_map/all_to_all | solution.py:400
  32.0 10.5 %collective-permute-start.3 = (bf16[4,256,128]{2,1,0:T(8,128)(2,1)}, bf16[4,256,128]{2,1,0:T(8,128)(2,1)}, u32[]{:S(2)}, u32[]{:S(2)}) collective-permute-start(bf16[4,256,128]{2,1,0:T(8,128)(2,1)} %copy-done.4), channel_id=1, source_target_pairs={{0,4},{1,5},{2,6},{3,7},{4,8},{5,9},{6,10},{7,11},{8,12},{9,13},{1... | collective-permute-start | bytes 786440 | tf_op jit(solution)/shard_map/ppermute | solution.py:375
  33.3 14.8 %collective-permute-start.4 = (bf16[4,256,128]{2,1,0:T(8,128)(2,1)}, bf16[4,256,128]{2,1,0:T(8,128)(2,1)}, u32[]{:S(2)}, u32[]{:S(2)}) collective-permute-start(bf16[4,256,128]{2,1,0:T(8,128)(2,1)} %copy-done.4), channel_id=1, source_target_pairs={{0,8},{1,9},{2,10},{3,11},{4,12},{5,13},{6,14},{7,15},{8,0},{9,1},... | collective-permute-start | bytes 786440 | tf_op jit(solution)/shard_map/ppermute | solution.py:375
  35.9 12.2 %collective-permute-start.5 = (bf16[4,256,128]{2,1,0:T(8,128)(2,1)}, bf16[4,256,128]{2,1,0:T(8,128)(2,1)}, u32[]{:S(2)}, u32[]{:S(2)}) collective-permute-start(bf16[4,256,128]{2,1,0:T(8,128)(2,1)} %copy-done.4), channel_id=1, source_target_pairs={{0,12},{1,13},{2,14},{3,15},{4,0},{5,1},{6,2},{7,3},{8,4},{9,5},{1... | collective-permute-start | bytes 786440 | tf_op jit(solution)/shard_map/ppermute | solution.py:375
  37.1 11.0 %copy-start.5 = (bf16[4,256,128]{2,1,0:T(8,128)(2,1)S(1)}, bf16[4,256,128]{2,1,0:T(8,128)(2,1)}, u32[]{:S(2)}) copy-start(bf16[4,256,128]{2,1,0:T(8,128)(2,1)} %copy-done.4) | copy-start | bytes 786436
  48.1 2.2 %copy-start.1 = (f32[16,16,32,128]{3,2,1,0:T(8,128)S(1)}, f32[16,16,32,128]{3,2,1,0:T(8,128)}, u32[]{:S(2)}) copy-start(f32[16,16,32,128]{3,2,1,0:T(8,128)} %shard_map.89.ctf_ref) | copy-start | bytes 12582916
  65.1 2.2 %copy-start.3 = (f32[16,16,32,128]{3,2,1,0:T(8,128)S(1)}, f32[16,16,32,128]{3,2,1,0:T(8,128)}, u32[]{:S(2)}) copy-start(f32[16,16,32,128]{3,2,1,0:T(8,128)} %get-tuple-element.10.proj_ref) | copy-start | bytes 12582916
  68.7 12.2 %all-to-all-start.2 = ((f32[16,1,1536]{2,1,0:T(1,128)}), f32[16,1,1536]{2,1,0:T(1,128)S(1)}, u32[]{:S(2)}, u32[]{:S(2)}) async-start(f32[16,1,1536]{2,1,0:T(1,128)} %shard_map.91), calls=%async_computation.2 | async-start | bytes 196608 | tf_op jit(solution)/shard_map/all_to_all | solution.py:412
  80.8 2.2 %copy-start.2 = (f32[16,16,32,128]{3,2,1,0:T(8,128)S(1)}, f32[16,16,32,128]{3,2,1,0:T(8,128)}, u32[]{:S(2)}) copy-start(f32[16,16,32,128]{3,2,1,0:T(8,128)} %shard_map.89.ctf_ref) | copy-start | bytes 12582916
  87.6 12.9 %collective-permute-start.6 = (bf16[2,384,128]{2,1,0:T(8,128)(2,1)S(1)}, bf16[2,384,128]{2,1,0:T(8,128)(2,1)S(1)}, u32[]{:S(2)}, u32[]{:S(2)}) collective-permute-start(bf16[2,384,128]{2,1,0:T(8,128)(2,1)S(1)} %shard_map.94), channel_id=1, source_target_pairs={{0,8},{1,9},{2,10},{3,11},{4,12},{5,13},{6,14},{7,15},{8,0},{9,1},... | collective-permute-start | bytes 589832 | tf_op jit(solution)/shard_map/ppermute | solution.py:375
  91.7 14.7 %collective-permute-start.7 = (bf16[2,384,128]{2,1,0:T(8,128)(2,1)S(1)}, bf16[2,384,128]{2,1,0:T(8,128)(2,1)S(1)}, u32[]{:S(2)}, u32[]{:S(2)}) collective-permute-start(bf16[2,384,128]{2,1,0:T(8,128)(2,1)S(1)} %shard_map.95), channel_id=1, source_target_pairs={{0,4},{1,5},{2,6},{3,7},{4,8},{5,9},{6,10},{7,11},{8,12},{9,13},{1... | collective-permute-start | bytes 589832 | tf_op jit(solution)/shard_map/ppermute | solution.py:375
  93.7 12.7 %collective-permute-start.8 = (bf16[2,384,128]{2,1,0:T(8,128)(2,1)S(1)}, bf16[2,384,128]{2,1,0:T(8,128)(2,1)S(1)}, u32[]{:S(2)}, u32[]{:S(2)}) collective-permute-start(bf16[2,384,128]{2,1,0:T(8,128)(2,1)S(1)} %shard_map.96), channel_id=1, source_target_pairs={{0,12},{1,13},{2,14},{3,15},{4,0},{5,1},{6,2},{7,3},{8,4},{9,5},{1... | collective-permute-start | bytes 589832 | tf_op jit(solution)/shard_map/ppermute | solution.py:375
  96.3 13.0 %collective-permute-start.9 = (bf16[2,384,128]{2,1,0:T(8,128)(2,1)S(1)}, bf16[2,384,128]{2,1,0:T(8,128)(2,1)S(1)}, u32[]{:S(2)}, u32[]{:S(2)}) collective-permute-start(bf16[2,384,128]{2,1,0:T(8,128)(2,1)S(1)} %shard_map.99), channel_id=1, source_target_pairs={{0,8},{1,9},{2,10},{3,11},{4,12},{5,13},{6,14},{7,15},{8,0},{9,1},... | collective-permute-start | bytes 589832 | tf_op jit(solution)/shard_map/ppermute | solution.py:375
  98.0 11.2 %collective-permute-start.10 = (bf16[2,384,128]{2,1,0:T(8,128)(2,1)S(1)}, bf16[2,384,128]{2,1,0:T(8,128)(2,1)S(1)}, u32[]{:S(2)}, u32[]{:S(2)}) collective-permute-start(bf16[2,384,128]{2,1,0:T(8,128)(2,1)S(1)} %shard_map.100), channel_id=1, source_target_pairs={{0,4},{1,5},{2,6},{3,7},{4,8},{5,9},{6,10},{7,11},{8,12},{9,13},{1... | collective-permute-start | bytes 589832 | tf_op jit(solution)/shard_map/ppermute | solution.py:375
  100.5 8.7 %collective-permute-start.11 = (bf16[2,384,128]{2,1,0:T(8,128)(2,1)S(1)}, bf16[2,384,128]{2,1,0:T(8,128)(2,1)S(1)}, u32[]{:S(2)}, u32[]{:S(2)}) collective-permute-start(bf16[2,384,128]{2,1,0:T(8,128)(2,1)S(1)} %shard_map.101), channel_id=1, source_target_pairs={{0,12},{1,13},{2,14},{3,15},{4,0},{5,1},{6,2},{7,3},{8,4},{9,5},{1... | collective-permute-start | bytes 589832 | tf_op jit(solution)/shard_map/ppermute | solution.py:375
  106.5 6.7 %collective-permute-start.14 = (bf16[384,128]{1,0:T(8,128)(2,1)S(1)}, bf16[384,128]{1,0:T(8,128)(2,1)S(1)}, u32[]{:S(2)}, u32[]{:S(2)}) collective-permute-start(bf16[384,128]{1,0:T(8,128)(2,1)S(1)} %get-tuple-element.16), channel_id=1, source_target_pairs={{0,3},{1,0},{2,1},{3,2},{4,7},{5,4},{6,5},{7,6},{8,11},{9,8},{10,9... | collective-permute-start | bytes 294920 | tf_op jit(solution)/shard_map/ppermute | solution.py:375
  109.4 6.0 %collective-permute-start.13 = (bf16[384,128]{1,0:T(8,128)(2,1)S(1)}, bf16[384,128]{1,0:T(8,128)(2,1)S(1)}, u32[]{:S(2)}, u32[]{:S(2)}) collective-permute-start(bf16[384,128]{1,0:T(8,128)(2,1)S(1)} %get-tuple-element.15), channel_id=1, source_target_pairs={{0,1},{1,2},{2,3},{3,0},{4,5},{5,6},{6,7},{7,4},{8,9},{9,10},{10,1... | collective-permute-start | bytes 294920 | tf_op jit(solution)/shard_map/ppermute | solution.py:375
  110.0 10.6 %collective-permute-start.12 = (bf16[384,128]{1,0:T(8,128)(2,1)S(1)}, bf16[384,128]{1,0:T(8,128)(2,1)S(1)}, u32[]{:S(2)}, u32[]{:S(2)}) collective-permute-start(bf16[384,128]{1,0:T(8,128)(2,1)S(1)} %get-tuple-element.14), channel_id=1, source_target_pairs={{0,2},{1,3},{2,0},{3,1},{4,6},{5,7},{6,4},{7,5},{8,10},{9,11},{10,... | collective-permute-start | bytes 294920 | tf_op jit(solution)/shard_map/ppermute | solution.py:375
  120.7 3.1 %collective-permute-start.15 = (f32[128,128]{1,0:T(8,128)S(1)}, f32[128,128]{1,0:T(8,128)S(1)}, u32[]{:S(2)}, u32[]{:S(2)}) collective-permute-start(f32[128,128]{1,0:T(8,128)S(1)} %slice.19), channel_id=1, source_target_pairs={{0,16},{16,0},{32,48},{48,32},{64,80},{80,64},{96,112},{112,96},{1... | collective-permute-start | bytes 196616 | tf_op jit(solution)/shard_map/ppermute | solution.py:430
  (1 other events, 0.7 us)

commit v3 on v2

--- a/solution.py
+++ b/solution.py
@@ -13,6 +13,7 @@
 EPS = 1e-05
 MIB = 1024 * 1024
 RING = 4
+PACK = 16
 WHOLE = pl.BlockSpec(memory_space=pltpu.VMEM)
 SCALARS = pl.BlockSpec(memory_space=pltpu.SMEM)
 
@@ -25,32 +26,41 @@
     return pl.CostEstimate(flops=flops, bytes_accessed=moved, transcendentals=0)
 
 
-def split_kernel(slices, img_ref, out_ref, scratch):
-    step, rows, _ = img_ref.shape
-    block_rows = rows // slices
-    for h in range(2):
-        half = img_ref[:, :, h * LANES : (h + 1) * LANES].astype(F32)
-        scratch[h] = half.reshape(step * rows, LANES)
-    for j in range(slices):
-        for b in range(block_rows):
-            picked = pl.ds(j * block_rows + b, step, stride=rows)
-            for h in range(2):
-                out_ref[2 * b + h, j] = scratch[h, picked, :].astype(BF16)
+def split_kernel(slices, img_ref, out_ref):
+    particles, rows, _ = img_ref.shape
+    block_rows = out_ref.shape[0] // 2
+    together = PACK // block_rows
+    size = PACK * PACK
+    to = lax.broadcasted_iota(jnp.int32, (size, size), 0)
+    come = lax.broadcasted_iota(jnp.int32, (size, size), 1)
+    moved = (come == (to % PACK) * PACK + to // PACK).astype(BF16)
+    for g in range(rows // PACK):
+        for i in range(particles // PACK):
+            part = img_ref[i * PACK : (i + 1) * PACK, g * PACK : (g + 1) * PACK, :]
+            part = part.reshape(size, 2 * LANES)
+            got = jnp.dot(moved, part, preferred_element_type=F32).astype(BF16)
+            for k in range(PACK):
+                j, b = g * together + k // block_rows, k % block_rows
+                for h in range(2):
+                    out_ref[2 * b + h, j, i * PACK : (i + 1) * PACK, :] = got[
+                        k * PACK : (k + 1) * PACK, h * LANES : (h + 1) * LANES
+                    ]
 
 
 def split_images(images, slices):
     particles, rows, width = images.shape
     block_rows = rows // slices
-    step = 16
+    steps = 2
     return pl.pallas_call(
         functools.partial(split_kernel, slices),
-        grid=(particles // step,),
-        in_specs=[pl.BlockSpec((step, rows, width), lambda i: (i, 0, 0))],
-        out_specs=pl.BlockSpec((2 * block_rows, slices, step, LANES), lambda i: (0, 0, i, 0)),
+        grid=(steps,),
+        in_specs=[pl.BlockSpec((particles, rows // steps, width), lambda i: (0, i, 0))],
+        out_specs=pl.BlockSpec(
+            (2 * block_rows, slices // steps, particles, LANES), lambda i: (0, i, 0, 0)
+        ),
         out_shape=pltpu.HBM((2 * block_rows, slices, particles, LANES), BF16),
-        scratch_shapes=[pltpu.VMEM((2, step * rows, LANES), F32)],
         compiler_params=params(56),
-        cost_estimate=cost(0, images.size * 4),
+        cost_estimate=cost(2 * images.size * PACK * PACK, images.size * 4),
     )(images)
 
 
@@ -118,37 +128,56 @@
     )(x, y, z)
 
 
-def contrast_kernel(extent, start, row_ref, meta_ref, ctf_ref):
+def contrast_kernel(extent, capacity, at_ref, meta_ref, ctf_ref, place_ref):
     held, slices, particles, _ = ctf_ref.shape
+    owners = place_ref.shape[0]
+    start = meta_ref.shape[2] - LANES
     for k in range(held):
-        focus = meta_ref[k, :, start : start + LANES]
+        focus = meta_ref[k, :, start:]
         focus = jnp.broadcast_to(focus, (LANES, LANES)).T[:particles, :] / extent
         column = lax.broadcasted_iota(jnp.int32, (particles, LANES), 1).astype(F32)
         angle = focus * (column * column)
         cos_col, sin_col = jnp.cos(angle), jnp.sin(angle)
-        row = column * 8.0 + row_ref[0]
+        row = column * 8.0 + at_ref[3].astype(F32)
         angle = focus * (row * row) + PHASE
         cos_row, sin_row = jnp.cos(angle), jnp.sin(angle)
         for j in range(slices):
             ctf_ref[k, j] = sin_row[:, j : j + 1] * cos_col + cos_row[:, j : j + 1] * sin_col
 
-
-def contrast(row, meta, start, slices, particles, extent):
+    first = start - owners * capacity
+    for i in range(place_ref.shape[2] // (held * capacity)):
+
+        @pl.when(pl.program_id(0) == i)
+        def _():
+            for h in range(owners):
+                at = first + h * capacity
+                got = [meta_ref[k, :, at : at + capacity] for k in range(held)]
+                to = i * held * capacity
+                place_ref[h, :, to : to + held * capacity] = jnp.concatenate(got, axis=1)
+
+
+def contrast(at, meta, slices, particles, owners, capacity, extent):
     senders, _, length = meta.shape
     held = 4
     return pl.pallas_call(
-        functools.partial(contrast_kernel, extent, start),
+        functools.partial(contrast_kernel, extent, capacity),
         grid=(senders // held,),
         in_specs=[SCALARS, pl.BlockSpec((held, 1, length), lambda i: (i, 0, 0))],
-        out_specs=pl.BlockSpec((held, slices, particles, LANES), lambda i: (i, 0, 0, 0)),
-        out_shape=pltpu.HBM((senders, slices, particles, LANES), F32),
-        compiler_params=params(8),
-        cost_estimate=cost(1000 * MIB, 4 * MIB),
-    )(row, meta)
+        out_specs=[
+            pl.BlockSpec((held, slices, particles, LANES), lambda i: (i, 0, 0, 0)),
+            pl.BlockSpec((owners, 1, senders * capacity), lambda i: (0, 0, 0)),
+        ],
+        out_shape=[
+            pltpu.HBM((senders, slices, particles, LANES), F32),
+            jax.ShapeDtypeStruct((owners, 1, senders * capacity), F32),
+        ],
+        compiler_params=params(32),
+        cost_estimate=cost(MIB, MIB),
+    )(at, meta)
 
 
 def project_kernel(
-    count, at_ref, meta_ref, ctf_ref, vol0, vol1, vol2, vol3, proj_ref, power_ref, pairs, one_hot
+    count, at_ref, meta_ref, ctf_ref, vol0, vol1, vol2, vol3, proj_ref, power_ref, pairs
 ):
     taken, slices, particles, _ = proj_ref.shape
     held, blocks, _ = vol0.shape
@@ -167,7 +196,7 @@
     at_z = at_ref[1].astype(F32)
     lane = lax.broadcasted_iota(jnp.int32, (count, LANES), 1).astype(F32)
     zero = jnp.zeros((count, owned), BF16)
-    uppers = []
+    powers = []
     for k in range(taken):
         key = meta_ref[k, :, :count]
         owner = jnp.floor(key * (1.0 / blocks))
@@ -182,14 +211,15 @@
         rows = jnp.concatenate([place] * 8 + [upper] * 8 + [y * float(held) + z] * 8, axis=0).T
         hit = jnp.broadcast_to(rows[:, :1], (count, LANES)) == lane
         hit = hit.astype(BF16)
-        uppers.append(jnp.broadcast_to(rows[:, 8:9], (count, LANES)) > 0.5)
+        upper = jnp.broadcast_to(rows[:, 8:9], (count, LANES)) > 0.5
         holder = jnp.broadcast_to(rows[:, 16:17], (count, LANES)).astype(BF16)
-        for i in range(holders):
-            one_hot[k, :, i * owned : (i + 1) * owned] = jnp.where(holder == i, hit, zero)
-    powers = []
-    for k in range(taken):
-        acc = jnp.dot(one_hot[k], pairs[...], preferred_element_type=F32)
-        picked = jnp.where(uppers[k], acc[:, LANES:], acc[:, :LANES])
+        acc = jnp.zeros((count, 2 * LANES), F32)
+        for i in range(0, holders, held):
+            one_hot = [jnp.where(holder == i + q, hit, zero) for q in range(held)]
+            one_hot = jnp.concatenate(one_hot, axis=1)
+            some = pairs[i * owned : (i + held) * owned, :]
+            acc += jnp.dot(one_hot, some, preferred_element_type=F32)
+        picked = jnp.where(upper, acc[:, LANES:], acc[:, :LANES])
         picked = picked.reshape(slices, particles, LANES)
         power = jnp.zeros((particles, LANES), F32)
         for j in range(slices):
@@ -205,7 +235,7 @@
     held, blocks, _ = vols[0].shape
     span = RING * held * blocks // 2
     count = slices * particles
-    taken = 4
+    taken = 8
     block = pl.BlockSpec((taken, slices, particles, LANES), lambda i: (i, 0, 0, 0))
     return pl.pallas_call(
         functools.partial(project_kernel, count),
@@ -221,32 +251,51 @@
             pltpu.HBM(ctf.shape, F32),
             jax.ShapeDtypeStruct((1, senders * particles), F32),
         ],
-        scratch_shapes=[
-            pltpu.VMEM((span, 2 * LANES), BF16),
-            pltpu.VMEM((taken, count, span), BF16),
-        ],
-        compiler_params=params(24),
-        cost_estimate=cost(2 * senders * count * span * 2 * LANES, 10 * MIB),
-    )(at, meta, ctf, *vols)
-
-
-def sums_kernel(img_ref, proj_ref, power_ref, out_ref, cross, noise):
+        scratch_shapes=[pltpu.VMEM((span, 2 * LANES), BF16)],
+        compiler_params=params(32),
+        cost_estimate=cost(5 * 2 * senders * count * span * 2 * LANES, 10 * MIB),
+    )(at, meta, in_hbm(ctf), *vols)
+
+
+def in_hbm(x):
+    return pltpu.with_memory_space_constraint(x, pltpu.HBM)
+
+
+def fetch(src, dst, sems):
+    parts = sems.shape[0]
+    size = src.shape[0] // parts
+    copies = []
+    for i in range(parts):
+        at = pl.ds(i * size, size)
+        copies.append(pltpu.make_async_copy(src.at[at], dst.at[at], sems.at[i]))
+        copies[-1].start()
+    return copies
+
+
+def sums_kernel(img_ref, proj_hbm, power_hbm, out_ref, cross, noise, power, proj, sems, sem):
     senders, slices, particles, _ = img_ref.shape
-
-    @pl.loop(0, senders)
-    def _(s):
-        cross_sum = jnp.zeros((particles, LANES), F32)
-        noise_sum = jnp.zeros((particles, LANES), F32)
-        for j in range(slices):
-            img = img_ref[s, j].astype(F32)
-            cross_sum += img * proj_ref[s, j]
-            noise_sum += img * img
-        cross[pl.ds(s * particles, particles), :] = cross_sum
-        noise[pl.ds(s * particles, particles), :] = noise_sum
+    copies = fetch(proj_hbm, proj, sems)
+    last = pltpu.make_async_copy(power_hbm, power, sem)
+    last.start()
+    size = senders // len(copies)
+    for i, copy in enumerate(copies):
+        copy.wait()
+
+        @pl.loop(i * size, (i + 1) * size)
+        def _(s):
+            cross_sum = jnp.zeros((particles, LANES), F32)
+            noise_sum = jnp.zeros((particles, LANES), F32)
+            for j in range(slices):
+                img = img_ref[s, j].astype(F32)
+                cross_sum += img * proj[s, j]
+                noise_sum += img * img
+            cross[pl.ds(s * particles, particles), :] = cross_sum
+            noise[pl.ds(s * particles, particles), :] = noise_sum
 
     total = senders * particles
     rows = [jnp.sum(ref[...].T, axis=0, keepdims=True) for ref in (cross, noise)]
-    rows.append(power_ref[...])
+    last.wait()
+    rows.append(power[...])
     for d in range(senders):
         for i, row in enumerate(rows):
             out_ref[d, :, i * total : (i + 1) * total] = row
@@ -257,18 +306,26 @@
     total = senders * particles
     return pl.pallas_call(
         sums_kernel,
-        in_specs=[WHOLE] * 3,
+        in_specs=[WHOLE] + [pl.BlockSpec(memory_space=pltpu.HBM)] * 2,
         out_specs=WHOLE,
         out_shape=jax.ShapeDtypeStruct((senders, 1, 3 * total), F32),
-        scratch_shapes=[pltpu.VMEM((total, LANES), F32)] * 2,
+        scratch_shapes=[pltpu.VMEM((total, LANES), F32)] * 2
+        + [
+            pltpu.VMEM(power.shape, F32),
+            pltpu.VMEM(proj.shape, F32),
+            pltpu.SemaphoreType.DMA((4,)),
+            pltpu.SemaphoreType.DMA,
+        ],
         compiler_params=params(12),
         cost_estimate=cost(img.size * 4, img.size * 6),
-    )(img, proj, power)
-
-
-def terms_kernel(pixels, part_ref, img_ref, ctf_ref, terms_ref, corr_ref, weight_col):
+    )(img, in_hbm(proj), in_hbm(power))
+
+
+def terms_kernel(pixels, part_ref, img_ref, ctf_hbm, terms_ref, corr_ref, weight_col, ctf_all, sems):
     senders, slices, particles, _ = img_ref.shape
     total = senders * particles
+    copies = fetch(ctf_hbm, ctf_all, sems)
+    size = senders // len(copies)
     sums = part_ref[0]
     for d in range(1, senders):
         sums = sums + part_ref[d]
@@ -278,16 +335,18 @@
     corr_ref[...] = corr
     weight = jax.nn.sigmoid(corr) / noise
     weight_col[...] = jnp.broadcast_to(weight, (LANES, total)).T
-
-    @pl.loop(0, senders)
-    def _(s):
-        weight = weight_col[pl.ds(s * particles, particles), :]
-        for j in range(slices):
-            ctf = ctf_ref[s, j]
-            scaled = weight * ctf
-            rows = pl.ds(j * particles, particles)
-            terms_ref[s, rows, :LANES] = (scaled * img_ref[s, j].astype(F32)).astype(BF16)
-            terms_ref[s, rows, LANES:] = (scaled * ctf).astype(BF16)
+    for i, copy in enumerate(copies):
+        copy.wait()
+
+        @pl.loop(i * size, (i + 1) * size)
+        def _(s):
+            weight = weight_col[pl.ds(s * particles, particles), :]
+            for j in range(slices):
+                ctf = ctf_all[s, j]
+                scaled = weight * ctf
+                rows = pl.ds(j * particles, particles)
+                terms_ref[s, rows, :LANES] = (scaled * img_ref[s, j].astype(F32)).astype(BF16)
+                terms_ref[s, rows, LANES:] = (scaled * ctf).astype(BF16)
 
 
 def make_terms(partials, img, ctf, pixels):
@@ -295,28 +354,35 @@
     total = senders * particles
     return pl.pallas_call(
         functools.partial(terms_kernel, float(pixels)),
-        in_specs=[WHOLE] * 3,
+        in_specs=[WHOLE, WHOLE, pl.BlockSpec(memory_space=pltpu.HBM)],
         out_specs=[WHOLE] * 2,
         out_shape=[
             jax.ShapeDtypeStruct((senders, slices * particles, 2 * LANES), BF16),
             jax.ShapeDtypeStruct((1, total), F32),
         ],
-        scratch_shapes=[pltpu.VMEM((total, LANES), F32)],
+        scratch_shapes=[
+            pltpu.VMEM((total, LANES), F32),
+            pltpu.VMEM(ctf.shape, F32),
+            pltpu.SemaphoreType.DMA((4,)),
+        ],
         compiler_params=params(12),
         cost_estimate=cost(img.size * 4, img.size * 10),
-    )(partials, img, ctf)
-
-
-def scatter_kernel(capacity, offsets, at_ref, slot_ref, place_ref, terms_ref, out_ref, sorted_ref):
+    )(partials, img, in_hbm(ctf))
+
+
+def scatter_kernel(
+    capacity, shift, offsets, at_ref, meta_ref, place_ref, terms_ref, out_ref, sorted_ref
+):
     senders, rows, width = terms_ref.shape
     blocks = out_ref.shape[1] * 2 // 3
     owned = blocks // 2
-    holders = [at_ref[0] * RING + lax.rem(at_ref[1] + u, RING) for u in offsets]
+    y = lax.rem(at_ref[0] + shift, RING)
+    holders = [y * RING + lax.rem(at_ref[1] + u, RING) for u in offsets]
     place_in = lax.broadcasted_iota(jnp.int32, (capacity, rows), 0)
     slot_at = [(place_in + h * capacity).astype(F32) for h in holders]
     slot_at = jnp.concatenate(slot_at, axis=0)
     for s in range(senders):
-        pick = (slot_at == slot_ref[s]).astype(BF16)
+        pick = (slot_at == meta_ref[s, :, rows : 2 * rows]).astype(BF16)
         got = jnp.dot(pick, terms_ref[s], preferred_element_type=F32).astype(BF16)
         for i in range(len(offsets)):
             sorted_ref[i, s * capacity : (s + 1) * capacity, :] = got[
@@ -331,20 +397,21 @@
         out_ref[i, blocks:, :] = denom.astype(out_ref.dtype)
 
 
-def scatter(at, offsets, slots, places, terms, blocks, capacity, kind):
+def scatter(at, shift, offsets, meta, places, terms, blocks, capacity, kind):
     senders, rows, width = terms.shape
     held = len(offsets)
-    return pl.pallas_call(
-        functools.partial(scatter_kernel, capacity, offsets),
+    out = jax.ShapeDtypeStruct((held, blocks * 3 // 2, LANES), kind)
+    return pl.pallas_call(
+        functools.partial(scatter_kernel, capacity, shift, offsets),
         in_specs=[SCALARS] + [WHOLE] * 3,
         out_specs=WHOLE,
-        out_shape=jax.ShapeDtypeStruct((held, blocks * 3 // 2, LANES), kind),
+        out_shape=out,
         scratch_shapes=[pltpu.VMEM((held, senders * capacity, width), BF16)],
         compiler_params=params(12),
         cost_estimate=cost(
             2 * senders * held * capacity * width * (rows + blocks), 5 * MIB
         ),
-    )(at, slots, places, terms)
+    )(at, meta, places, terms)
 
 
 def fold_kernel(own_ref, got1, got2, got3, *outs):
@@ -388,7 +455,7 @@
     rows = slices * particles
     capacity = 5 * rows // (2 * owners)
 
-    at_yz = jnp.stack([at_y, at_z])
+    at_all = jnp.stack([at_y, at_z, me % 2, me // 2])
 
     meta = make_meta(
         owner, assign, orient, defocus, slice_loc, capacity, owners, blocks, owned, groups
@@ -400,30 +467,22 @@
     img = lax.all_to_all(img, "dom", 0, 0, tiled=True)
     vols = [near] + [ring(near, "cls", owners, RING, t) for t in range(1, RING)]
 
-    slots = meta[:, :, rows : 2 * rows]
-    last = 2 * rows + owners * capacity
-    filled = meta[:, 0, 2 * rows : last].reshape(groups, owners, capacity).transpose(1, 0, 2)
-    filled = filled.reshape(owners, 1, groups * capacity)
-
-    row = (me // 2).astype(F32).reshape(1)
-    ctf = contrast(row, meta, last, slices, particles, float(image_rows * image_rows))
-    proj, power = project(at_yz, meta, ctf, vols)
+    extent = float(image_rows * image_rows)
+    ctf, places = contrast(at_all, meta, slices, particles, owners, capacity, extent)
+    proj, power = project(at_all, meta, ctf, vols)
     partial = partial_sums(img, proj, power)
     partial = lax.all_to_all(partial, "dom", 0, 0, tiled=True)
     terms, corr = make_terms(partial, img, ctf, image_rows * width)
     correlation = lax.dynamic_slice_in_dim(corr[0], me * particles, particles)
 
-    def by_y(offsets, kinds):
-        def part(t, kind):
-            to = jnp.stack([(at_y + t) % RING, at_z, me % 2])
-            return scatter(to, offsets, slots, filled, terms, blocks, capacity, kind)
-
-        got = [ring(part(t, BF16), "cls", owners, RING, t) for t in (2, 1, 3)]
-        return fold(part(0, F32), got, kinds)
-
-    far, right = by_y((2, 1), (BF16, BF16))
-    far, right = ring(far, "cls", owners, 1, 2), ring(right, "cls", owners, 1, 1)
-    left, total = by_y((3, 0), (BF16, F32))
+    parts = {}
+    for t in (2, 1, 3, 0):
+        kind = BF16 if t else F32
+        parts[t] = scatter(at_all, t, (2, 1, 3, 0), meta, places, terms, blocks, capacity, kind)
+    got = [ring(parts[t], "cls", owners, RING, t) for t in (2, 1, 3)]
+    far, right, left, total = fold(parts[0], got, (BF16, BF16, BF16, F32))
+    far = ring(far, "cls", owners, 1, 2)
+    right = ring(right, "cls", owners, 1, 1)
     left = ring(left, "cls", owners, 1, 3)
     total = total + far.astype(F32) + right.astype(F32) + left.astype(F32)
     numer, mine = total[:blocks], total[blocks:]

time: 125 us -> 119 us (0.952)
  starting transfers between devices: 51.5 us -> 39.5 us
  blocking collectives: 0 us -> 9.52 us
  local copies, waits for them, and re-layouts: 11.6 us -> 2.4 us
  waiting for transfers between devices: 15.4 us -> 22.1 us
  Pallas kernels: 44 us -> 42.3 us
    all_to_all x0 -> x1, blocking collectives: none -> 9.52 us  [shards(): partial = lax.all_to_all(partial, 'dom', 0, 0, tiled=True)]
    all_to_all x1 -> x0, starting transfers between devices: 6.33 us -> none  [shards(): partial = lax.all_to_all(partial, 'dom', 0, 0, tiled=True)]
    all_to_all x1, waiting for transfers between devices: 0.01 us -> 6.01 us  [shards(): img = lax.all_to_all(img, 'dom', 0, 0, tiled=True)]
    unnamed x12 -> x4, local copies, waits for them, and re-layouts: 7.26 us -> 1.79 us
    ppermute x15 -> x12, starting transfers between devices: 28.4 us -> 24.6 us  [ring(): return lax.ppermute(x, axis, [(i, target(i)) for i in range(size)])]
    ppermute x15 -> x12, waiting for transfers between devices: 13 us -> 15.7 us  [ring(): return lax.ppermute(x, axis, [(i, target(i)) for i in range(size)])]
    another operation x2 -> x0, local copies, waits for them, and re-layouts: 2.38 us -> none  [shards(): meta[:, 0, 2 * rows:last].reshape(groups, owners, capacity)]
    all_to_all x1 -> x0, waiting for transfers between devices: 2.07 us -> none  [shards(): partial = lax.all_to_all(partial, 'dom', 0, 0, tiled=True)]
  transfers between devices with their start and end apart: 19 -> 15, of which waited for: 5 -> 5; matrix products, arithmetic and copies ran while one was open for 4% -> 1% of each run, Pallas kernels for 29% -> 29%
where the time goes in v3:
time: 119 us; the launch traced here: 118 us
  Pallas kernels  42.3 us (36%)
  starting transfers between devices  39.5 us (33%)
  waiting for transfers between devices  22.1 us (19%)
  blocking collectives  9.52 us (8%)
  local copies, waits for them, and re-layouts  2.4 us (2%)
  other arithmetic  1.55 us (1%)
    ppermute x12, starting transfers between devices, ring(): return lax.ppermute(x, axis, [(i, target(i)) for i in range(size)])  24.6 us
    ppermute x12, waiting for transfers between devices, ring(): return lax.ppermute(x, axis, [(i, target(i)) for i in range(size)])  15.7 us
    pallas_call x1, Pallas kernels, project(): pl.pallas_call(functools.partial(project_kernel, count), grid=(senders //...  13.7 us
    pallas_call x4, Pallas kernels, scatter(): pl.pallas_call(functools.partial(scatter_kernel, capacity, shift, offsets...  11 us
    all_to_all x1, blocking collectives, shards(): partial = lax.all_to_all(partial, 'dom', 0, 0, tiled=True)  9.52 us
    pallas_call x1, Pallas kernels, contrast(): pl.pallas_call(functools.partial(contrast_kernel, extent, capacity), grid...  6.8 us
    all_to_all x1, starting transfers between devices, shards(): img = lax.all_to_all(img, 'dom', 0, 0, tiled=True)  6.54 us
    all_to_all x1, starting transfers between devices, shards(): meta = lax.all_to_all(meta, 'dom', 0, 0, tiled=True)  6.28 us
  transfers between devices with their start and end apart: 15, of which 5 were waited for; matrix products, arithmetic and copies ran while one was open for 1% of the time, Pallas kernels for 29%

profile of v3, /device:TPU:1, one launch (start us, length us, event | category | flops | bytes accessed | tf_op | source)
XLA Modules:
  0.0 118.1 jit_solution(11434928425451085438)
XLA Ops:
  1.9 6.9 %collective-permute-start.2 = (bf16[256,128]{1,0:T(8,128)(2,1)S(1)}, bf16[256,128]{1,0:T(8,128)(2,1)S(1)}, u32[]{:S(2)}, u32[]{:S(2)}) collective-permute-start(bf16[256,128]{1,0:T(8,128)(2,1)S(1)} %bitcast.17), channel_id=1, source_target_pairs={{0,3},{1,0},{2,1},{3,2},{4,7},{5,4},{6,5},{7,6},{8,11},{9,8},{10,9... | collective-permute-start | bytes 196616 | tf_op jit(solution)/shard_map/ppermute | solution.py:442
  9.8 2.3 %collective-permute-start = (bf16[256,128]{1,0:T(8,128)(2,1)S(1)}, bf16[256,128]{1,0:T(8,128)(2,1)S(1)}, u32[]{:S(2)}, u32[]{:S(2)}) collective-permute-start(bf16[256,128]{1,0:T(8,128)(2,1)S(1)} %bitcast.19), channel_id=1, source_target_pairs={{0,1},{1,2},{2,3},{3,0},{4,5},{5,6},{6,7},{7,4},{8,9},{9,10},{10,1... | collective-permute-start | bytes 196616 | tf_op jit(solution)/shard_map/ppermute | solution.py:442
  12.1 2.4 %shard_map.86 = f32[16,1,2432]{2,1,0:T(1,128)} custom-call(s32[16,32]{1,0:T(8,128)} %bitcast.26, s32[1,32]{1,0:T(1,128)} %bitcast.27, s32[1,32]{1,0:T(1,128)} %bitcast.28, bf16[1,32]{1,0:T(2,128)(2,1)} %bitcast.29, s32[16,512]{1,0:T(8,128)} %bitcast.25), custom_call_target="tpu_custom_call" | custom-call | flops 104857600 | bytes 1048576 | tf_op jit(solution)/shard_map/pallas_call | solution.py:106
  14.4 6.3 %all-to-all-start = ((f32[16,1,2432]{2,1,0:T(1,128)}), f32[16,1,2432]{2,1,0:T(1,128)S(1)}, u32[]{:S(2)}, u32[]{:S(2)}) async-start(f32[16,1,2432]{2,1,0:T(1,128)} %shard_map.86), calls=%async_computation | async-start | bytes 311296 | tf_op jit(solution)/shard_map/all_to_all | solution.py:463
  21.5 2.8 %collective-permute-start.5 = (bf16[4,256,128]{2,1,0:T(8,128)(2,1)}, bf16[4,256,128]{2,1,0:T(8,128)(2,1)}, u32[]{:S(2)}, u32[]{:S(2)}) collective-permute-start(bf16[4,256,128]{2,1,0:T(8,128)(2,1)} %pad_maximum_fusion.y_ref.vol0), channel_id=1, source_target_pairs={{0,12},{1,13},{2,14},{3,15},{4,0},{5,1},{6,2},{7,3},{8,4},{9,5},{1... | collective-permute-start | bytes 786440 | tf_op jit(solution)/shard_map/ppermute | solution.py:442
  25.3 3.1 %shard_map.88.x_ref = bf16[16,16,32,128]{3,2,1,0:T(8,128)(2,1)} custom-call(bf16[32,128,256]{2,1,0:T(8,128)(2,1)} %img_ref.1), custom_call_target="tpu_custom_call" | custom-call | flops 536870912 | bytes 4194304 | tf_op jit(solution)/shard_map/pallas_call | solution.py:54
  28.5 6.5 %all-to-all-start.1 = ((bf16[16,16,32,128]{3,2,1,0:T(8,128)(2,1)}), bf16[16,16,32,128]{3,2,1,0:T(8,128)(2,1)S(1)}, u32[]{:S(2)}, u32[]{:S(2)}) async-start(bf16[16,16,32,128]{3,2,1,0:T(8,128)(2,1)} %shard_map.89), calls=%async_computation.1 | async-start | bytes 4194304 | tf_op jit(solution)/shard_map/all_to_all | solution.py:467
  35.0 6.8 %shard_map.87 = (f32[16,16,32,128]{3,2,1,0:T(8,128)}, f32[16,1,1280]{2,1,0:T(1,128)S(1)}) custom-call(s32[4]{0:T(128)S(1)} %pad_add_fusion.at_ref, f32[16,1,2432]{2,1,0:T(1,128)S(1)} %all-to-all-done.meta_ref.z_ref), custom_call_target="tpu_custom_call" | custom-call | flops 1048576 | bytes 1048576 | tf_op jit(solution)/shard_map/pallas_call | solution.py:162
  41.8 13.7 %shard_map.90 = (f32[16,16,32,128]{3,2,1,0:T(8,128)}, f32[1,512]{1,0:T(1,128)S(1)}) custom-call(s32[4]{0:T(128)S(1)} %pad_add_fusion.at_ref, f32[16,1,2432]{2,1,0:T(1,128)S(1)} %all-to-all-done.meta_ref.z_ref, f32[16,16,32,128]{3,2,1,0:T(8,128)} %get-tuple-element.13.ctf_ref.ctf_hbm, bf16[4,256,128]{2,1,0:T(8,128)(2,1)} %pad_maximum_fusion.y_ref.vol0, ...), custom_call_target="tpu_custom_call" | custom-call | flops 42949672960 | bytes 10485760 | tf_op jit(solution)/shard_map/pallas_call | solution.py:240
  56.1 6.0 %all-to-all-done.1.img_ref = bf16[16,16,32,128]{3,2,1,0:T(8,128)(2,1)S(1)} async-done(((bf16[16,16,32,128]{3,2,1,0:T(8,128)(2,1)}), bf16[16,16,32,128]{3,2,1,0:T(8,128)(2,1)S(1)}, u32[]{:S(2)}, u32[]{:S(2)}) %all-to-all-start.1) | async-done | bytes 2097184 | tf_op jit(solution)/shard_map/all_to_all | solution.py:467
  62.2 2.6 %shard_map.91 = f32[16,1,1536]{2,1,0:T(1,128)S(1)} custom-call(bf16[16,16,32,128]{3,2,1,0:T(8,128)(2,1)S(1)} %all-to-all-done.1.img_ref, f32[16,16,32,128]{3,2,1,0:T(8,128)} %get-tuple-element.14.proj_hbm, f32[1,512]{1,0:T(1,128)} %copy-done.1), custom_call_target="tpu_custom_call" | custom-call | flops 4194304 | bytes 6291456 | tf_op jit(solution)/shard_map/pallas_call | solution.py:307
  64.8 9.5 %all_to_all.15.part_ref = f32[16,1,1536]{2,1,0:T(1,128)S(1)} all-to-all(f32[16,1,1536]{2,1,0:T(1,128)S(1)} %shard_map.91), channel_id=1, replica_groups=mesh['dom'=16,'cls'=16] {'dom'}, dimensions={0} | all-to-all | bytes 196608 | tf_op jit(solution)/shard_map/all_to_all | solution.py:474
  74.3 2.5 %shard_map.92 = (bf16[16,512,256]{2,1,0:T(8,128)(2,1)S(1)}, f32[1,512]{1,0:T(1,128)S(1)}) custom-call(f32[16,1,1536]{2,1,0:T(1,128)S(1)} %all_to_all.15.part_ref, bf16[16,16,32,128]{3,2,1,0:T(8,128)(2,1)S(1)} %all-to-all-done.1.img_ref, f32[16,16,32,128]{3,2,1,0:T(8,128)} %get-tuple-element.13.ctf_ref.ctf_hbm), custom_call_target="tpu_custom_call" | custom-call | flops 4194304 | bytes 10485760 | tf_op jit(solution)/shard_map/pallas_call | solution.py:355
  76.8 2.8 %shard_map.94 = bf16[4,384,128]{2,1,0:T(8,128)(2,1)S(1)} custom-call(s32[4]{0:T(128)S(1)} %pad_add_fusion.at_ref, f32[16,1,2432]{2,1,0:T(1,128)S(1)} %all-to-all-done.meta_ref.z_ref, f32[16,1,1280]{2,1,0:T(1,128)S(1)} %get-tuple-element.12.place_ref, bf16[16,512,256]{2,1,0:T(8,128)(2,1)S(1)} %get-tuple-element.16.terms_ref), custom_call_target="tpu_custom_call" | custom-call | flops 2013265920 | bytes 5242880 | tf_op jit(solution)/shard_map/pallas_call | solution.py:404
  81.3 2.8 %shard_map.95 = bf16[4,384,128]{2,1,0:T(8,128)(2,1)S(1)} custom-call(s32[4]{0:T(128)S(1)} %pad_add_fusion.at_ref, f32[16,1,2432]{2,1,0:T(1,128)S(1)} %all-to-all-done.meta_ref.z_ref, f32[16,1,1280]{2,1,0:T(1,128)S(1)} %get-tuple-element.12.place_ref, bf16[16,512,256]{2,1,0:T(8,128)(2,1)S(1)} %get-tuple-element.16.terms_ref), custom_call_target="tpu_custom_call" | custom-call | flops 2013265920 | bytes 5242880 | tf_op jit(solution)/shard_map/pallas_call | solution.py:404
  85.2 2.8 %shard_map.96 = bf16[4,384,128]{2,1,0:T(8,128)(2,1)S(1)} custom-call(s32[4]{0:T(128)S(1)} %pad_add_fusion.at_ref, f32[16,1,2432]{2,1,0:T(1,128)S(1)} %all-to-all-done.meta_ref.z_ref, f32[16,1,1280]{2,1,0:T(1,128)S(1)} %get-tuple-element.12.place_ref, bf16[16,512,256]{2,1,0:T(8,128)(2,1)S(1)} %get-tuple-element.16.terms_ref), custom_call_target="tpu_custom_call" | custom-call | flops 2013265920 | bytes 5242880 | tf_op jit(solution)/shard_map/pallas_call | solution.py:404
  88.0 1.8 %collective-permute-start.8 = (bf16[4,384,128]{2,1,0:T(8,128)(2,1)S(1)}, bf16[4,384,128]{2,1,0:T(8,128)(2,1)S(1)}, u32[]{:S(2)}, u32[]{:S(2)}) collective-permute-start(bf16[4,384,128]{2,1,0:T(8,128)(2,1)S(1)} %shard_map.96), channel_id=1, source_target_pairs={{0,12},{1,13},{2,14},{3,15},{4,0},{5,1},{6,2},{7,3},{8,4},{9,5},{1... | collective-permute-start | bytes 1179656 | tf_op jit(solution)/shard_map/ppermute | solution.py:442
  89.8 2.7 %shard_map.93.own_ref = f32[4,384,128]{2,1,0:T(8,128)S(1)} custom-call(s32[4]{0:T(128)S(1)} %pad_add_fusion.at_ref, f32[16,1,2432]{2,1,0:T(1,128)S(1)} %all-to-all-done.meta_ref.z_ref, f32[16,1,1280]{2,1,0:T(1,128)S(1)} %get-tuple-element.12.place_ref, bf16[16,512,256]{2,1,0:T(8,128)(2,1)S(1)} %get-tuple-element.16.terms_ref), custom_call_target="tpu_custom_call" | custom-call | flops 2013265920 | bytes 5242880 | tf_op jit(solution)/shard_map/pallas_call | solution.py:404
  92.6 8.0 %collective-permute-done.7.got2 = bf16[4,384,128]{2,1,0:T(8,128)(2,1)S(1)} collective-permute-done((bf16[4,384,128]{2,1,0:T(8,128)(2,1)S(1)}, bf16[4,384,128]{2,1,0:T(8,128)(2,1)S(1)}, u32[]{:S(2)}, u32[]{:S(2)}) %collective-permute-start.7) | collective-permute-done | bytes 393248 | tf_op jit(solution)/shard_map/ppermute | solution.py:442
  100.8 1.9 %collective-permute-start.9 = (bf16[384,128]{1,0:T(8,128)(2,1)S(1)}, bf16[384,128]{1,0:T(8,128)(2,1)S(1)}, u32[]{:S(2)}, u32[]{:S(2)}) collective-permute-start(bf16[384,128]{1,0:T(8,128)(2,1)S(1)} %get-tuple-element.18), channel_id=1, source_target_pairs={{0,2},{1,3},{2,0},{3,1},{4,6},{5,7},{6,4},{7,5},{8,10},{9,11},{10,... | collective-permute-start | bytes 294920 | tf_op jit(solution)/shard_map/ppermute | solution.py:442
  104.4 2.1 %collective-permute-start.11 = (bf16[384,128]{1,0:T(8,128)(2,1)S(1)}, bf16[384,128]{1,0:T(8,128)(2,1)S(1)}, u32[]{:S(2)}, u32[]{:S(2)}) collective-permute-start(bf16[384,128]{1,0:T(8,128)(2,1)S(1)} %get-tuple-element.20), channel_id=1, source_target_pairs={{0,3},{1,0},{2,1},{3,2},{4,7},{5,4},{6,5},{7,6},{8,11},{9,8},{10,9... | collective-permute-start | bytes 294920 | tf_op jit(solution)/shard_map/ppermute | solution.py:442
  106.6 2.1 %collective-permute-done.9 = bf16[384,128]{1,0:T(8,128)(2,1)S(1)} collective-permute-done((bf16[384,128]{1,0:T(8,128)(2,1)S(1)}, bf16[384,128]{1,0:T(8,128)(2,1)S(1)}, u32[]{:S(2)}, u32[]{:S(2)}) %collective-permute-start.9) | collective-permute-done | bytes 98336 | tf_op jit(solution)/shard_map/ppermute | solution.py:442
  108.6 5.6 %collective-permute-done.10 = bf16[384,128]{1,0:T(8,128)(2,1)S(1)} collective-permute-done((bf16[384,128]{1,0:T(8,128)(2,1)S(1)}, bf16[384,128]{1,0:T(8,128)(2,1)S(1)}, u32[]{:S(2)}, u32[]{:S(2)}) %collective-permute-start.10) | collective-permute-done | bytes 98336 | tf_op jit(solution)/shard_map/ppermute | solution.py:442
  114.3 2.1 %collective-permute-start.12 = (f32[128,128]{1,0:T(8,128)S(1)}, f32[128,128]{1,0:T(8,128)S(1)}, u32[]{:S(2)}, u32[]{:S(2)}) collective-permute-start(f32[128,128]{1,0:T(8,128)S(1)} %slice.9), channel_id=1, source_target_pairs={{0,16},{16,0},{32,48},{48,32},{64,80},{80,64},{96,112},{112,96},{1... | collective-permute-start | bytes 196616 | tf_op jit(solution)/shard_map/ppermute | solution.py:489
  (31 shorter events, 11.2 us)
Async XLA Ops:
  0.6 1.2 %copy-start = (bf16[2,128,2048]{2,1,0:T(8,128)(2,1)S(1)}, bf16[2,128,2048]{2,1,0:T(8,128)(2,1)}, u32[]{:S(2)}) copy-start(bf16[2,128,2048]{2,1,0:T(8,128)(2,1)} %param.13) | copy-start | bytes 3145732
  1.9 18.8 %collective-permute-start.2 = (bf16[256,128]{1,0:T(8,128)(2,1)S(1)}, bf16[256,128]{1,0:T(8,128)(2,1)S(1)}, u32[]{:S(2)}, u32[]{:S(2)}) collective-permute-start(bf16[256,128]{1,0:T(8,128)(2,1)S(1)} %bitcast.17), channel_id=1, source_target_pairs={{0,3},{1,0},{2,1},{3,2},{4,7},{5,4},{6,5},{7,6},{8,11},{9,8},{10,9... | collective-permute-start | bytes 196616 | tf_op jit(solution)/shard_map/ppermute | solution.py:442
  8.8 11.9 %collective-permute-start.1 = (bf16[256,128]{1,0:T(8,128)(2,1)S(1)}, bf16[256,128]{1,0:T(8,128)(2,1)S(1)}, u32[]{:S(2)}, u32[]{:S(2)}) collective-permute-start(bf16[256,128]{1,0:T(8,128)(2,1)S(1)} %bitcast.18), channel_id=1, source_target_pairs={{0,2},{1,3},{2,0},{3,1},{4,6},{5,7},{6,4},{7,5},{8,10},{9,11},{10,... | collective-permute-start | bytes 196616 | tf_op jit(solution)/shard_map/ppermute | solution.py:442
  9.8 10.9 %collective-permute-start = (bf16[256,128]{1,0:T(8,128)(2,1)S(1)}, bf16[256,128]{1,0:T(8,128)(2,1)S(1)}, u32[]{:S(2)}, u32[]{:S(2)}) collective-permute-start(bf16[256,128]{1,0:T(8,128)(2,1)S(1)} %bitcast.19), channel_id=1, source_target_pairs={{0,1},{1,2},{2,3},{3,0},{4,5},{5,6},{6,7},{7,4},{8,9},{9,10},{10,1... | collective-permute-start | bytes 196616 | tf_op jit(solution)/shard_map/ppermute | solution.py:442
  14.4 14.1 %all-to-all-start = ((f32[16,1,2432]{2,1,0:T(1,128)}), f32[16,1,2432]{2,1,0:T(1,128)S(1)}, u32[]{:S(2)}, u32[]{:S(2)}) async-start(f32[16,1,2432]{2,1,0:T(1,128)} %shard_map.86), calls=%async_computation | async-start | bytes 311296 | tf_op jit(solution)/shard_map/all_to_all | solution.py:463
  21.5 20.4 %collective-permute-start.5 = (bf16[4,256,128]{2,1,0:T(8,128)(2,1)}, bf16[4,256,128]{2,1,0:T(8,128)(2,1)}, u32[]{:S(2)}, u32[]{:S(2)}) collective-permute-start(bf16[4,256,128]{2,1,0:T(8,128)(2,1)} %pad_maximum_fusion.y_ref.vol0), channel_id=1, source_target_pairs={{0,12},{1,13},{2,14},{3,15},{4,0},{5,1},{6,2},{7,3},{8,4},{9,5},{1... | collective-permute-start | bytes 786440 | tf_op jit(solution)/shard_map/ppermute | solution.py:442
  24.2 17.6 %collective-permute-start.4 = (bf16[4,256,128]{2,1,0:T(8,128)(2,1)}, bf16[4,256,128]{2,1,0:T(8,128)(2,1)}, u32[]{:S(2)}, u32[]{:S(2)}) collective-permute-start(bf16[4,256,128]{2,1,0:T(8,128)(2,1)} %pad_maximum_fusion.y_ref.vol0), channel_id=1, source_target_pairs={{0,8},{1,9},{2,10},{3,11},{4,12},{5,13},{6,14},{7,15},{8,0},{9,1},... | collective-permute-start | bytes 786440 | tf_op jit(solution)/shard_map/ppermute | solution.py:442
  24.6 17.3 %collective-permute-start.3 = (bf16[4,256,128]{2,1,0:T(8,128)(2,1)}, bf16[4,256,128]{2,1,0:T(8,128)(2,1)}, u32[]{:S(2)}, u32[]{:S(2)}) collective-permute-start(bf16[4,256,128]{2,1,0:T(8,128)(2,1)} %pad_maximum_fusion.y_ref.vol0), channel_id=1, source_target_pairs={{0,4},{1,5},{2,6},{3,7},{4,8},{5,9},{6,10},{7,11},{8,12},{9,13},{1... | collective-permute-start | bytes 786440 | tf_op jit(solution)/shard_map/ppermute | solution.py:442
  28.5 33.7 %all-to-all-start.1 = ((bf16[16,16,32,128]{3,2,1,0:T(8,128)(2,1)}), bf16[16,16,32,128]{3,2,1,0:T(8,128)(2,1)S(1)}, u32[]{:S(2)}, u32[]{:S(2)}) async-start(bf16[16,16,32,128]{3,2,1,0:T(8,128)(2,1)} %shard_map.89), calls=%async_computation.1 | async-start | bytes 4194304 | tf_op jit(solution)/shard_map/all_to_all | solution.py:467
  55.6 0.6 copy-start.1
  79.5 13.1 %collective-permute-start.6 = (bf16[4,384,128]{2,1,0:T(8,128)(2,1)S(1)}, bf16[4,384,128]{2,1,0:T(8,128)(2,1)S(1)}, u32[]{:S(2)}, u32[]{:S(2)}) collective-permute-start(bf16[4,384,128]{2,1,0:T(8,128)(2,1)S(1)} %shard_map.94), channel_id=1, source_target_pairs={{0,8},{1,9},{2,10},{3,11},{4,12},{5,13},{6,14},{7,15},{8,0},{9,1},... | collective-permute-start | bytes 1179656 | tf_op jit(solution)/shard_map/ppermute | solution.py:442
  84.0 16.6 %collective-permute-start.7 = (bf16[4,384,128]{2,1,0:T(8,128)(2,1)S(1)}, bf16[4,384,128]{2,1,0:T(8,128)(2,1)S(1)}, u32[]{:S(2)}, u32[]{:S(2)}) collective-permute-start(bf16[4,384,128]{2,1,0:T(8,128)(2,1)S(1)} %shard_map.95), channel_id=1, source_target_pairs={{0,4},{1,5},{2,6},{3,7},{4,8},{5,9},{6,10},{7,11},{8,12},{9,13},{1... | collective-permute-start | bytes 1179656 | tf_op jit(solution)/shard_map/ppermute | solution.py:442
  88.0 12.6 %collective-permute-start.8 = (bf16[4,384,128]{2,1,0:T(8,128)(2,1)S(1)}, bf16[4,384,128]{2,1,0:T(8,128)(2,1)S(1)}, u32[]{:S(2)}, u32[]{:S(2)}) collective-permute-start(bf16[4,384,128]{2,1,0:T(8,128)(2,1)S(1)} %shard_map.96), channel_id=1, source_target_pairs={{0,12},{1,13},{2,14},{3,15},{4,0},{5,1},{6,2},{7,3},{8,4},{9,5},{1... | collective-permute-start | bytes 1179656 | tf_op jit(solution)/shard_map/ppermute | solution.py:442
  100.8 7.9 %collective-permute-start.9 = (bf16[384,128]{1,0:T(8,128)(2,1)S(1)}, bf16[384,128]{1,0:T(8,128)(2,1)S(1)}, u32[]{:S(2)}, u32[]{:S(2)}) collective-permute-start(bf16[384,128]{1,0:T(8,128)(2,1)S(1)} %get-tuple-element.18), channel_id=1, source_target_pairs={{0,2},{1,3},{2,0},{3,1},{4,6},{5,7},{6,4},{7,5},{8,10},{9,11},{10,... | collective-permute-start | bytes 294920 | tf_op jit(solution)/shard_map/ppermute | solution.py:442
  102.7 11.6 %collective-permute-start.10 = (bf16[384,128]{1,0:T(8,128)(2,1)S(1)}, bf16[384,128]{1,0:T(8,128)(2,1)S(1)}, u32[]{:S(2)}, u32[]{:S(2)}) collective-permute-start(bf16[384,128]{1,0:T(8,128)(2,1)S(1)} %get-tuple-element.19), channel_id=1, source_target_pairs={{0,1},{1,2},{2,3},{3,0},{4,5},{5,6},{6,7},{7,4},{8,9},{9,10},{10,1... | collective-permute-start | bytes 294920 | tf_op jit(solution)/shard_map/ppermute | solution.py:442
  104.4 9.9 %collective-permute-start.11 = (bf16[384,128]{1,0:T(8,128)(2,1)S(1)}, bf16[384,128]{1,0:T(8,128)(2,1)S(1)}, u32[]{:S(2)}, u32[]{:S(2)}) collective-permute-start(bf16[384,128]{1,0:T(8,128)(2,1)S(1)} %get-tuple-element.20), channel_id=1, source_target_pairs={{0,3},{1,0},{2,1},{3,2},{4,7},{5,4},{6,5},{7,6},{8,11},{9,8},{10,9... | collective-permute-start | bytes 294920 | tf_op jit(solution)/shard_map/ppermute | solution.py:442
  114.3 3.1 %collective-permute-start.12 = (f32[128,128]{1,0:T(8,128)S(1)}, f32[128,128]{1,0:T(8,128)S(1)}, u32[]{:S(2)}, u32[]{:S(2)}) collective-permute-start(f32[128,128]{1,0:T(8,128)S(1)} %slice.9), channel_id=1, source_target_pairs={{0,16},{16,0},{32,48},{48,32},{64,80},{80,64},{96,112},{112,96},{1... | collective-permute-start | bytes 196616 | tf_op jit(solution)/shard_map/ppermute | solution.py:489

commit v4 on v3

--- a/solution.py
+++ b/solution.py
@@ -24,6 +24,34 @@
 
 def cost(flops, moved):
     return pl.CostEstimate(flops=flops, bytes_accessed=moved, transcendentals=0)
+
+
+def in_vmem(x):
+    return pltpu.with_memory_space_constraint(x, pltpu.VMEM)
+
+
+def in_hbm(x):
+    return pltpu.with_memory_space_constraint(x, pltpu.HBM)
+
+
+def piece_kernel(column_ref, vol_hbm, out_ref, sem):
+    at = pl.ds(pl.multiple_of(column_ref[0] * LANES, LANES), LANES)
+    copy = pltpu.make_async_copy(vol_hbm.at[:, :, at], out_ref, sem)
+    copy.start()
+    copy.wait()
+
+
+def piece_of(volume, column):
+    classes, owned, _ = volume.shape
+    return pl.pallas_call(
+        piece_kernel,
+        in_specs=[SCALARS, pl.BlockSpec(memory_space=pltpu.HBM)],
+        out_specs=WHOLE,
+        out_shape=jax.ShapeDtypeStruct((classes, owned, LANES), BF16),
+        scratch_shapes=[pltpu.SemaphoreType.DMA],
+        compiler_params=params(1),
+        cost_estimate=cost(0, 4 * classes * owned * LANES),
+    )(column.reshape(1), in_hbm(volume))
 
 
 def split_kernel(slices, img_ref, out_ref):
@@ -168,10 +196,10 @@
             pl.BlockSpec((owners, 1, senders * capacity), lambda i: (0, 0, 0)),
         ],
         out_shape=[
-            pltpu.HBM((senders, slices, particles, LANES), F32),
+            pltpu.VMEM((senders, slices, particles, LANES), F32),
             jax.ShapeDtypeStruct((owners, 1, senders * capacity), F32),
         ],
-        compiler_params=params(32),
+        compiler_params=params(12),
         cost_estimate=cost(MIB, MIB),
     )(at, meta)
 
@@ -235,7 +263,7 @@
     held, blocks, _ = vols[0].shape
     span = RING * held * blocks // 2
     count = slices * particles
-    taken = 8
+    taken = 4
     block = pl.BlockSpec((taken, slices, particles, LANES), lambda i: (i, 0, 0, 0))
     return pl.pallas_call(
         functools.partial(project_kernel, count),
@@ -252,13 +280,9 @@
             jax.ShapeDtypeStruct((1, senders * particles), F32),
         ],
         scratch_shapes=[pltpu.VMEM((span, 2 * LANES), BF16)],
-        compiler_params=params(32),
+        compiler_params=params(20),
         cost_estimate=cost(5 * 2 * senders * count * span * 2 * LANES, 10 * MIB),
-    )(at, meta, in_hbm(ctf), *vols)
-
-
-def in_hbm(x):
-    return pltpu.with_memory_space_constraint(x, pltpu.HBM)
+    )(at, meta, in_vmem(ctf), *vols)
 
 
 def fetch(src, dst, sems):
@@ -321,11 +345,9 @@
     )(img, in_hbm(proj), in_hbm(power))
 
 
-def terms_kernel(pixels, part_ref, img_ref, ctf_hbm, terms_ref, corr_ref, weight_col, ctf_all, sems):
+def terms_kernel(pixels, part_ref, img_ref, ctf_ref, terms_ref, corr_ref, weight_col):
     senders, slices, particles, _ = img_ref.shape
     total = senders * particles
-    copies = fetch(ctf_hbm, ctf_all, sems)
-    size = senders // len(copies)
     sums = part_ref[0]
     for d in range(1, senders):
         sums = sums + part_ref[d]
@@ -335,18 +357,16 @@
     corr_ref[...] = corr
     weight = jax.nn.sigmoid(corr) / noise
     weight_col[...] = jnp.broadcast_to(weight, (LANES, total)).T
-    for i, copy in enumerate(copies):
-        copy.wait()
-
-        @pl.loop(i * size, (i + 1) * size)
-        def _(s):
-            weight = weight_col[pl.ds(s * particles, particles), :]
-            for j in range(slices):
-                ctf = ctf_all[s, j]
-                scaled = weight * ctf
-                rows = pl.ds(j * particles, particles)
-                terms_ref[s, rows, :LANES] = (scaled * img_ref[s, j].astype(F32)).astype(BF16)
-                terms_ref[s, rows, LANES:] = (scaled * ctf).astype(BF16)
+
+    @pl.loop(0, senders)
+    def _(s):
+        weight = weight_col[pl.ds(s * particles, particles), :]
+        for j in range(slices):
+            ctf = ctf_ref[s, j]
+            scaled = weight * ctf
+            rows = pl.ds(j * particles, particles)
+            terms_ref[s, rows, :LANES] = (scaled * img_ref[s, j].astype(F32)).astype(BF16)
+            terms_ref[s, rows, LANES:] = (scaled * ctf).astype(BF16)
 
 
 def make_terms(partials, img, ctf, pixels):
@@ -354,20 +374,16 @@
     total = senders * particles
     return pl.pallas_call(
         functools.partial(terms_kernel, float(pixels)),
-        in_specs=[WHOLE, WHOLE, pl.BlockSpec(memory_space=pltpu.HBM)],
+        in_specs=[WHOLE] * 3,
         out_specs=[WHOLE] * 2,
         out_shape=[
             jax.ShapeDtypeStruct((senders, slices * particles, 2 * LANES), BF16),
             jax.ShapeDtypeStruct((1, total), F32),
         ],
-        scratch_shapes=[
-            pltpu.VMEM((total, LANES), F32),
-            pltpu.VMEM(ctf.shape, F32),
-            pltpu.SemaphoreType.DMA((4,)),
-        ],
-        compiler_params=params(12),
+        scratch_shapes=[pltpu.VMEM((total, LANES), F32)],
+        compiler_params=params(8),
         cost_estimate=cost(img.size * 4, img.size * 10),
-    )(partials, img, in_hbm(ctf))
+    )(partials, img, in_vmem(ctf))
 
 
 def scatter_kernel(
@@ -461,7 +477,7 @@
         owner, assign, orient, defocus, slice_loc, capacity, owners, blocks, owned, groups
     )
     meta = lax.all_to_all(meta, "dom", 0, 0, tiled=True)
-    piece = lax.dynamic_slice_in_dim(volume, me * LANES, LANES, axis=2).reshape(blocks, LANES)
+    piece = piece_of(volume, me).reshape(blocks, LANES)
     near = jnp.stack([piece] + [ring(piece, "cls", owners, 1, t) for t in range(1, RING)])
     img = after(split_images(images, slices), near, meta)
     img = lax.all_to_all(img, "dom", 0, 0, tiled=True)

time: 119 us -> 116 us (0.975)
  Pallas kernels: 42.3 us -> 40.3 us
    pallas_call x1, Pallas kernels: 2.47 us -> 1.12 us  [make_terms(): pl.pallas_call(functools.partial(terms_kernel, float(pixels)), in_specs=[...]
    unnamed x4 -> x6, local copies, waits for them, and re-layouts: 1.79 us -> 2.58 us
  transfers between devices with their start and end apart: 15 -> 15, of which waited for: 5 -> 5; matrix products, arithmetic and copies ran while one was open for 1% -> 1% of each run, Pallas kernels for 29% -> 28%
where the time goes in v4:
time: 116 us
  Pallas kernels  40.3 us (35%)
  starting transfers between devices  39.4 us (34%)
  waiting for transfers between devices  21.9 us (19%)
  blocking collectives  9.52 us (8%)
  local copies, waits for them, and re-layouts  3.16 us (3%)
    ppermute x12, starting transfers between devices, ring(): return lax.ppermute(x, axis, [(i, target(i)) for i in range(size)])  24.4 us
    ppermute x12, waiting for transfers between devices, ring(): return lax.ppermute(x, axis, [(i, target(i)) for i in range(size)])  16 us
    pallas_call x1, Pallas kernels, project(): pl.pallas_call(functools.partial(project_kernel, count), grid=(senders //...  13.1 us
    pallas_call x4, Pallas kernels, scatter(): pl.pallas_call(functools.partial(scatter_kernel, capacity, shift, offsets...  11 us
    all_to_all x1, blocking collectives, shards(): partial = lax.all_to_all(partial, 'dom', 0, 0, tiled=True)  9.52 us
    all_to_all x1, starting transfers between devices, shards(): img = lax.all_to_all(img, 'dom', 0, 0, tiled=True)  6.54 us
    all_to_all x1, starting transfers between devices, shards(): meta = lax.all_to_all(meta, 'dom', 0, 0, tiled=True)  6.28 us
    pallas_call x1, Pallas kernels, contrast(): pl.pallas_call(functools.partial(contrast_kernel, extent, capacity), grid...  5.81 us
  transfers between devices with their start and end apart: 15, of which 5 were waited for; matrix products, arithmetic and copies ran while one was open for 1% of the time, Pallas kernels for 28%

profile of v4, /device:TPU:1, one launch (start us, length us, event | category | flops | bytes accessed | tf_op | source)
XLA Modules:
  0.0 115.9 jit_solution(9888334295185097892)
XLA Ops:
  1.5 6.9 %collective-permute-start.2 = (bf16[256,128]{1,0:T(8,128)(2,1)S(1)}, bf16[256,128]{1,0:T(8,128)(2,1)S(1)}, u32[]{:S(2)}, u32[]{:S(2)}) collective-permute-start(bf16[256,128]{1,0:T(8,128)(2,1)S(1)} %bitcast.18), channel_id=1, source_target_pairs={{0,3},{1,0},{2,1},{3,2},{4,7},{5,4},{6,5},{7,6},{8,11},{9,8},{10,9... | collective-permute-start | bytes 196616 | tf_op jit(solution)/shard_map/ppermute | solution.py:458
  9.4 2.3 %collective-permute-start = (bf16[256,128]{1,0:T(8,128)(2,1)S(1)}, bf16[256,128]{1,0:T(8,128)(2,1)S(1)}, u32[]{:S(2)}, u32[]{:S(2)}) collective-permute-start(bf16[256,128]{1,0:T(8,128)(2,1)S(1)} %bitcast.20), channel_id=1, source_target_pairs={{0,1},{1,2},{2,3},{3,0},{4,5},{5,6},{6,7},{7,4},{8,9},{9,10},{10,1... | collective-permute-start | bytes 196616 | tf_op jit(solution)/shard_map/ppermute | solution.py:458
  11.7 2.4 %shard_map.86 = f32[16,1,2432]{2,1,0:T(1,128)} custom-call(s32[16,32]{1,0:T(8,128)} %bitcast.27, s32[1,32]{1,0:T(1,128)} %bitcast.28, s32[1,32]{1,0:T(1,128)} %bitcast.29, bf16[1,32]{1,0:T(2,128)(2,1)} %bitcast.30, s32[16,512]{1,0:T(8,128)} %bitcast.26), custom_call_target="tpu_custom_call" | custom-call | flops 104857600 | bytes 1048576 | tf_op jit(solution)/shard_map/pallas_call | solution.py:134
  14.1 6.3 %all-to-all-start = ((f32[16,1,2432]{2,1,0:T(1,128)}), f32[16,1,2432]{2,1,0:T(1,128)S(1)}, u32[]{:S(2)}, u32[]{:S(2)}) async-start(f32[16,1,2432]{2,1,0:T(1,128)} %shard_map.86), calls=%async_computation | async-start | bytes 311296 | tf_op jit(solution)/shard_map/all_to_all | solution.py:479
  20.4 2.8 %collective-permute-start.5 = (bf16[4,256,128]{2,1,0:T(8,128)(2,1)S(1)}, bf16[4,256,128]{2,1,0:T(8,128)(2,1)S(1)}, u32[]{:S(2)}, u32[]{:S(2)}) collective-permute-start(bf16[4,256,128]{2,1,0:T(8,128)(2,1)S(1)} %pad_maximum_fusion.y_ref.vol0), channel_id=1, source_target_pairs={{0,12},{1,13},{2,14},{3,15},{4,0},{5,1},{6,2},{7,3},{8,4},{9,5},{1... | collective-permute-start | bytes 786440 | tf_op jit(solution)/shard_map/ppermute | solution.py:458
  24.3 3.1 %shard_map.88.x_ref = bf16[16,16,32,128]{3,2,1,0:T(8,128)(2,1)} custom-call(bf16[32,128,256]{2,1,0:T(8,128)(2,1)} %img_ref.1), custom_call_target="tpu_custom_call" | custom-call | flops 536870912 | bytes 4194304 | tf_op jit(solution)/shard_map/pallas_call | solution.py:82
  27.5 6.5 %all-to-all-start.1 = ((bf16[16,16,32,128]{3,2,1,0:T(8,128)(2,1)}), bf16[16,16,32,128]{3,2,1,0:T(8,128)(2,1)S(1)}, u32[]{:S(2)}, u32[]{:S(2)}) async-start(bf16[16,16,32,128]{3,2,1,0:T(8,128)(2,1)} %shard_map.90), calls=%async_computation.1 | async-start | bytes 4194304 | tf_op jit(solution)/shard_map/all_to_all | solution.py:483
  34.0 5.8 %shard_map.87 = (f32[16,16,32,128]{3,2,1,0:T(8,128)S(1)}, f32[16,1,1280]{2,1,0:T(1,128)S(1)}) custom-call(s32[4]{0:T(128)S(1)} %pad_add_fusion.at_ref, f32[16,1,2432]{2,1,0:T(1,128)S(1)} %all-to-all-done.meta_ref.z_ref), custom_call_target="tpu_custom_call" | custom-call | flops 1048576 | bytes 1048576 | tf_op jit(solution)/shard_map/pallas_call | solution.py:190
  39.9 13.1 %shard_map.91 = (f32[16,16,32,128]{3,2,1,0:T(8,128)}, f32[1,512]{1,0:T(1,128)S(1)}) custom-call(s32[4]{0:T(128)S(1)} %pad_add_fusion.at_ref, f32[16,1,2432]{2,1,0:T(1,128)S(1)} %all-to-all-done.meta_ref.z_ref, f32[16,16,32,128]{3,2,1,0:T(8,128)S(1)} %get-tuple-element.13.ctf_ref, bf16[4,256,128]{2,1,0:T(8,128)(2,1)S(1)} %pad_maximum_fusion.y_ref.vol0, ...), custom_call_target="tpu_custom_call" | custom-call | flops 42949672960 | bytes 10485760 | tf_op jit(solution)/shard_map/pallas_call | solution.py:268
  53.0 2.0 %copy-done = f32[16,16,32,128]{3,2,1,0:T(8,128)} copy-done((f32[16,16,32,128]{3,2,1,0:T(8,128)}, f32[16,16,32,128]{3,2,1,0:T(8,128)S(1)}, u32[]{:S(2)}) %copy-start) | copy-done | bytes 4194328
  55.6 5.6 %all-to-all-done.1.img_ref = bf16[16,16,32,128]{3,2,1,0:T(8,128)(2,1)S(1)} async-done(((bf16[16,16,32,128]{3,2,1,0:T(8,128)(2,1)}), bf16[16,16,32,128]{3,2,1,0:T(8,128)(2,1)S(1)}, u32[]{:S(2)}, u32[]{:S(2)}) %all-to-all-start.1) | async-done | bytes 2097184 | tf_op jit(solution)/shard_map/all_to_all | solution.py:483
  61.2 2.7 %shard_map.92 = f32[16,1,1536]{2,1,0:T(1,128)S(1)} custom-call(bf16[16,16,32,128]{3,2,1,0:T(8,128)(2,1)S(1)} %all-to-all-done.1.img_ref, f32[16,16,32,128]{3,2,1,0:T(8,128)} %get-tuple-element.14.proj_hbm, f32[1,512]{1,0:T(1,128)} %copy-done.2), custom_call_target="tpu_custom_call" | custom-call | flops 4194304 | bytes 6291456 | tf_op jit(solution)/shard_map/pallas_call | solution.py:331
  63.9 9.5 %all_to_all.15.part_ref = f32[16,1,1536]{2,1,0:T(1,128)S(1)} all-to-all(f32[16,1,1536]{2,1,0:T(1,128)S(1)} %shard_map.92), channel_id=1, replica_groups=mesh['dom'=16,'cls'=16] {'dom'}, dimensions={0} | all-to-all | bytes 196608 | tf_op jit(solution)/shard_map/all_to_all | solution.py:490
  74.6 2.8 %shard_map.95 = bf16[4,384,128]{2,1,0:T(8,128)(2,1)S(1)} custom-call(s32[4]{0:T(128)S(1)} %pad_add_fusion.at_ref, f32[16,1,2432]{2,1,0:T(1,128)S(1)} %all-to-all-done.meta_ref.z_ref, f32[16,1,1280]{2,1,0:T(1,128)S(1)} %get-tuple-element.12.place_ref, bf16[16,512,256]{2,1,0:T(8,128)(2,1)S(1)} %get-tuple-element.16.terms_ref), custom_call_target="tpu_custom_call" | custom-call | flops 2013265920 | bytes 5242880 | tf_op jit(solution)/shard_map/pallas_call | solution.py:420
  79.1 2.7 %shard_map.96 = bf16[4,384,128]{2,1,0:T(8,128)(2,1)S(1)} custom-call(s32[4]{0:T(128)S(1)} %pad_add_fusion.at_ref, f32[16,1,2432]{2,1,0:T(1,128)S(1)} %all-to-all-done.meta_ref.z_ref, f32[16,1,1280]{2,1,0:T(1,128)S(1)} %get-tuple-element.12.place_ref, bf16[16,512,256]{2,1,0:T(8,128)(2,1)S(1)} %get-tuple-element.16.terms_ref), custom_call_target="tpu_custom_call" | custom-call | flops 2013265920 | bytes 5242880 | tf_op jit(solution)/shard_map/pallas_call | solution.py:420
  82.8 2.8 %shard_map.97 = bf16[4,384,128]{2,1,0:T(8,128)(2,1)S(1)} custom-call(s32[4]{0:T(128)S(1)} %pad_add_fusion.at_ref, f32[16,1,2432]{2,1,0:T(1,128)S(1)} %all-to-all-done.meta_ref.z_ref, f32[16,1,1280]{2,1,0:T(1,128)S(1)} %get-tuple-element.12.place_ref, bf16[16,512,256]{2,1,0:T(8,128)(2,1)S(1)} %get-tuple-element.16.terms_ref), custom_call_target="tpu_custom_call" | custom-call | flops 2013265920 | bytes 5242880 | tf_op jit(solution)/shard_map/pallas_call | solution.py:420
  85.6 1.8 %collective-permute-start.8 = (bf16[4,384,128]{2,1,0:T(8,128)(2,1)S(1)}, bf16[4,384,128]{2,1,0:T(8,128)(2,1)S(1)}, u32[]{:S(2)}, u32[]{:S(2)}) collective-permute-start(bf16[4,384,128]{2,1,0:T(8,128)(2,1)S(1)} %shard_map.97), channel_id=1, source_target_pairs={{0,12},{1,13},{2,14},{3,15},{4,0},{5,1},{6,2},{7,3},{8,4},{9,5},{1... | collective-permute-start | bytes 1179656 | tf_op jit(solution)/shard_map/ppermute | solution.py:458
  87.4 2.7 %shard_map.94.own_ref = f32[4,384,128]{2,1,0:T(8,128)S(1)} custom-call(s32[4]{0:T(128)S(1)} %pad_add_fusion.at_ref, f32[16,1,2432]{2,1,0:T(1,128)S(1)} %all-to-all-done.meta_ref.z_ref, f32[16,1,1280]{2,1,0:T(1,128)S(1)} %get-tuple-element.12.place_ref, bf16[16,512,256]{2,1,0:T(8,128)(2,1)S(1)} %get-tuple-element.16.terms_ref), custom_call_target="tpu_custom_call" | custom-call | flops 2013265920 | bytes 5242880 | tf_op jit(solution)/shard_map/pallas_call | solution.py:420
  90.2 8.2 %collective-permute-done.7.got2 = bf16[4,384,128]{2,1,0:T(8,128)(2,1)S(1)} collective-permute-done((bf16[4,384,128]{2,1,0:T(8,128)(2,1)S(1)}, bf16[4,384,128]{2,1,0:T(8,128)(2,1)S(1)}, u32[]{:S(2)}, u32[]{:S(2)}) %collective-permute-start.7) | collective-permute-done | bytes 393248 | tf_op jit(solution)/shard_map/ppermute | solution.py:458
  98.6 1.9 %collective-permute-start.9 = (bf16[384,128]{1,0:T(8,128)(2,1)S(1)}, bf16[384,128]{1,0:T(8,128)(2,1)S(1)}, u32[]{:S(2)}, u32[]{:S(2)}) collective-permute-start(bf16[384,128]{1,0:T(8,128)(2,1)S(1)} %get-tuple-element.18), channel_id=1, source_target_pairs={{0,2},{1,3},{2,0},{3,1},{4,6},{5,7},{6,4},{7,5},{8,10},{9,11},{10,... | collective-permute-start | bytes 294920 | tf_op jit(solution)/shard_map/ppermute | solution.py:458
  102.2 2.1 %collective-permute-start.11 = (bf16[384,128]{1,0:T(8,128)(2,1)S(1)}, bf16[384,128]{1,0:T(8,128)(2,1)S(1)}, u32[]{:S(2)}, u32[]{:S(2)}) collective-permute-start(bf16[384,128]{1,0:T(8,128)(2,1)S(1)} %get-tuple-element.20), channel_id=1, source_target_pairs={{0,3},{1,0},{2,1},{3,2},{4,7},{5,4},{6,5},{7,6},{8,11},{9,8},{10,9... | collective-permute-start | bytes 294920 | tf_op jit(solution)/shard_map/ppermute | solution.py:458
  104.4 2.1 %collective-permute-done.9 = bf16[384,128]{1,0:T(8,128)(2,1)S(1)} collective-permute-done((bf16[384,128]{1,0:T(8,128)(2,1)S(1)}, bf16[384,128]{1,0:T(8,128)(2,1)S(1)}, u32[]{:S(2)}, u32[]{:S(2)}) %collective-permute-start.9) | collective-permute-done | bytes 98336 | tf_op jit(solution)/shard_map/ppermute | solution.py:458
  106.4 5.6 %collective-permute-done.10 = bf16[384,128]{1,0:T(8,128)(2,1)S(1)} collective-permute-done((bf16[384,128]{1,0:T(8,128)(2,1)S(1)}, bf16[384,128]{1,0:T(8,128)(2,1)S(1)}, u32[]{:S(2)}, u32[]{:S(2)}) %collective-permute-start.10) | collective-permute-done | bytes 98336 | tf_op jit(solution)/shard_map/ppermute | solution.py:458
  112.1 2.1 %collective-permute-start.12 = (f32[128,128]{1,0:T(8,128)S(1)}, f32[128,128]{1,0:T(8,128)S(1)}, u32[]{:S(2)}, u32[]{:S(2)}) collective-permute-start(f32[128,128]{1,0:T(8,128)S(1)} %slice.9), channel_id=1, source_target_pairs={{0,16},{16,0},{32,48},{48,32},{64,80},{80,64},{96,112},{112,96},{1... | collective-permute-start | bytes 196616 | tf_op jit(solution)/shard_map/ppermute | solution.py:505
  (33 shorter events, 11.0 us)
Async XLA Ops:
  1.5 18.8 %collective-permute-start.2 = (bf16[256,128]{1,0:T(8,128)(2,1)S(1)}, bf16[256,128]{1,0:T(8,128)(2,1)S(1)}, u32[]{:S(2)}, u32[]{:S(2)}) collective-permute-start(bf16[256,128]{1,0:T(8,128)(2,1)S(1)} %bitcast.18), channel_id=1, source_target_pairs={{0,3},{1,0},{2,1},{3,2},{4,7},{5,4},{6,5},{7,6},{8,11},{9,8},{10,9... | collective-permute-start | bytes 196616 | tf_op jit(solution)/shard_map/ppermute | solution.py:458
  8.4 11.9 %collective-permute-start.1 = (bf16[256,128]{1,0:T(8,128)(2,1)S(1)}, bf16[256,128]{1,0:T(8,128)(2,1)S(1)}, u32[]{:S(2)}, u32[]{:S(2)}) collective-permute-start(bf16[256,128]{1,0:T(8,128)(2,1)S(1)} %bitcast.19), channel_id=1, source_target_pairs={{0,2},{1,3},{2,0},{3,1},{4,6},{5,7},{6,4},{7,5},{8,10},{9,11},{10,... | collective-permute-start | bytes 196616 | tf_op jit(solution)/shard_map/ppermute | solution.py:458
  9.4 10.9 %collective-permute-start = (bf16[256,128]{1,0:T(8,128)(2,1)S(1)}, bf16[256,128]{1,0:T(8,128)(2,1)S(1)}, u32[]{:S(2)}, u32[]{:S(2)}) collective-permute-start(bf16[256,128]{1,0:T(8,128)(2,1)S(1)} %bitcast.20), channel_id=1, source_target_pairs={{0,1},{1,2},{2,3},{3,0},{4,5},{5,6},{6,7},{7,4},{8,9},{9,10},{10,1... | collective-permute-start | bytes 196616 | tf_op jit(solution)/shard_map/ppermute | solution.py:458
  14.1 13.5 %all-to-all-start = ((f32[16,1,2432]{2,1,0:T(1,128)}), f32[16,1,2432]{2,1,0:T(1,128)S(1)}, u32[]{:S(2)}, u32[]{:S(2)}) async-start(f32[16,1,2432]{2,1,0:T(1,128)} %shard_map.86), calls=%async_computation | async-start | bytes 311296 | tf_op jit(solution)/shard_map/all_to_all | solution.py:479
  20.4 19.5 %collective-permute-start.5 = (bf16[4,256,128]{2,1,0:T(8,128)(2,1)S(1)}, bf16[4,256,128]{2,1,0:T(8,128)(2,1)S(1)}, u32[]{:S(2)}, u32[]{:S(2)}) collective-permute-start(bf16[4,256,128]{2,1,0:T(8,128)(2,1)S(1)} %pad_maximum_fusion.y_ref.vol0), channel_id=1, source_target_pairs={{0,12},{1,13},{2,14},{3,15},{4,0},{5,1},{6,2},{7,3},{8,4},{9,5},{1... | collective-permute-start | bytes 786440 | tf_op jit(solution)/shard_map/ppermute | solution.py:458
  23.2 16.6 %collective-permute-start.4 = (bf16[4,256,128]{2,1,0:T(8,128)(2,1)S(1)}, bf16[4,256,128]{2,1,0:T(8,128)(2,1)S(1)}, u32[]{:S(2)}, u32[]{:S(2)}) collective-permute-start(bf16[4,256,128]{2,1,0:T(8,128)(2,1)S(1)} %pad_maximum_fusion.y_ref.vol0), channel_id=1, source_target_pairs={{0,8},{1,9},{2,10},{3,11},{4,12},{5,13},{6,14},{7,15},{8,0},{9,1},... | collective-permute-start | bytes 786440 | tf_op jit(solution)/shard_map/ppermute | solution.py:458
  23.6 16.3 %collective-permute-start.3 = (bf16[4,256,128]{2,1,0:T(8,128)(2,1)S(1)}, bf16[4,256,128]{2,1,0:T(8,128)(2,1)S(1)}, u32[]{:S(2)}, u32[]{:S(2)}) collective-permute-start(bf16[4,256,128]{2,1,0:T(8,128)(2,1)S(1)} %pad_maximum_fusion.y_ref.vol0), channel_id=1, source_target_pairs={{0,4},{1,5},{2,6},{3,7},{4,8},{5,9},{6,10},{7,11},{8,12},{9,13},{1... | collective-permute-start | bytes 786440 | tf_op jit(solution)/shard_map/ppermute | solution.py:458
  27.5 33.7 %all-to-all-start.1 = ((bf16[16,16,32,128]{3,2,1,0:T(8,128)(2,1)}), bf16[16,16,32,128]{3,2,1,0:T(8,128)(2,1)S(1)}, u32[]{:S(2)}, u32[]{:S(2)}) async-start(bf16[16,16,32,128]{3,2,1,0:T(8,128)(2,1)} %shard_map.90), calls=%async_computation.1 | async-start | bytes 4194304 | tf_op jit(solution)/shard_map/all_to_all | solution.py:483
  53.0 2.0 %copy-start = (f32[16,16,32,128]{3,2,1,0:T(8,128)}, f32[16,16,32,128]{3,2,1,0:T(8,128)S(1)}, u32[]{:S(2)}) copy-start(f32[16,16,32,128]{3,2,1,0:T(8,128)S(1)} %get-tuple-element.13.ctf_ref) | copy-start | bytes 12582916
  55.0 0.6 copy-start.2
  61.2 12.3 %copy-start.1 = (f32[16,16,32,128]{3,2,1,0:T(8,128)S(1)}, f32[16,16,32,128]{3,2,1,0:T(8,128)}, u32[]{:S(2)}) copy-start(f32[16,16,32,128]{3,2,1,0:T(8,128)} %copy-done) | copy-start | bytes 12582916
  77.3 12.8 %collective-permute-start.6 = (bf16[4,384,128]{2,1,0:T(8,128)(2,1)S(1)}, bf16[4,384,128]{2,1,0:T(8,128)(2,1)S(1)}, u32[]{:S(2)}, u32[]{:S(2)}) collective-permute-start(bf16[4,384,128]{2,1,0:T(8,128)(2,1)S(1)} %shard_map.95), channel_id=1, source_target_pairs={{0,8},{1,9},{2,10},{3,11},{4,12},{5,13},{6,14},{7,15},{8,0},{9,1},... | collective-permute-start | bytes 1179656 | tf_op jit(solution)/shard_map/ppermute | solution.py:458
  81.8 16.6 %collective-permute-start.7 = (bf16[4,384,128]{2,1,0:T(8,128)(2,1)S(1)}, bf16[4,384,128]{2,1,0:T(8,128)(2,1)S(1)}, u32[]{:S(2)}, u32[]{:S(2)}) collective-permute-start(bf16[4,384,128]{2,1,0:T(8,128)(2,1)S(1)} %shard_map.96), channel_id=1, source_target_pairs={{0,4},{1,5},{2,6},{3,7},{4,8},{5,9},{6,10},{7,11},{8,12},{9,13},{1... | collective-permute-start | bytes 1179656 | tf_op jit(solution)/shard_map/ppermute | solution.py:458
  85.6 12.8 %collective-permute-start.8 = (bf16[4,384,128]{2,1,0:T(8,128)(2,1)S(1)}, bf16[4,384,128]{2,1,0:T(8,128)(2,1)S(1)}, u32[]{:S(2)}, u32[]{:S(2)}) collective-permute-start(bf16[4,384,128]{2,1,0:T(8,128)(2,1)S(1)} %shard_map.97), channel_id=1, source_target_pairs={{0,12},{1,13},{2,14},{3,15},{4,0},{5,1},{6,2},{7,3},{8,4},{9,5},{1... | collective-permute-start | bytes 1179656 | tf_op jit(solution)/shard_map/ppermute | solution.py:458
  98.6 7.9 %collective-permute-start.9 = (bf16[384,128]{1,0:T(8,128)(2,1)S(1)}, bf16[384,128]{1,0:T(8,128)(2,1)S(1)}, u32[]{:S(2)}, u32[]{:S(2)}) collective-permute-start(bf16[384,128]{1,0:T(8,128)(2,1)S(1)} %get-tuple-element.18), channel_id=1, source_target_pairs={{0,2},{1,3},{2,0},{3,1},{4,6},{5,7},{6,4},{7,5},{8,10},{9,11},{10,... | collective-permute-start | bytes 294920 | tf_op jit(solution)/shard_map/ppermute | solution.py:458
  100.5 11.6 %collective-permute-start.10 = (bf16[384,128]{1,0:T(8,128)(2,1)S(1)}, bf16[384,128]{1,0:T(8,128)(2,1)S(1)}, u32[]{:S(2)}, u32[]{:S(2)}) collective-permute-start(bf16[384,128]{1,0:T(8,128)(2,1)S(1)} %get-tuple-element.19), channel_id=1, source_target_pairs={{0,1},{1,2},{2,3},{3,0},{4,5},{5,6},{6,7},{7,4},{8,9},{9,10},{10,1... | collective-permute-start | bytes 294920 | tf_op jit(solution)/shard_map/ppermute | solution.py:458
  102.2 9.9 %collective-permute-start.11 = (bf16[384,128]{1,0:T(8,128)(2,1)S(1)}, bf16[384,128]{1,0:T(8,128)(2,1)S(1)}, u32[]{:S(2)}, u32[]{:S(2)}) collective-permute-start(bf16[384,128]{1,0:T(8,128)(2,1)S(1)} %get-tuple-element.20), channel_id=1, source_target_pairs={{0,3},{1,0},{2,1},{3,2},{4,7},{5,4},{6,5},{7,6},{8,11},{9,8},{10,9... | collective-permute-start | bytes 294920 | tf_op jit(solution)/shard_map/ppermute | solution.py:458
  112.1 3.0 %collective-permute-start.12 = (f32[128,128]{1,0:T(8,128)S(1)}, f32[128,128]{1,0:T(8,128)S(1)}, u32[]{:S(2)}, u32[]{:S(2)}) collective-permute-start(f32[128,128]{1,0:T(8,128)S(1)} %slice.9), channel_id=1, source_target_pairs={{0,16},{16,0},{32,48},{48,32},{64,80},{80,64},{96,112},{112,96},{1... | collective-permute-start | bytes 196616 | tf_op jit(solution)/shard_map/ppermute | solution.py:505

commit v5 on v4

--- a/solution.py
+++ b/solution.py
@@ -302,27 +302,34 @@
     last = pltpu.make_async_copy(power_hbm, power, sem)
     last.start()
     size = senders // len(copies)
+    total = senders * particles
+
+    def put(i, row):
+        for d in range(senders):
+            out_ref[d, :, i * total : (i + 1) * total] = row
+
+    @pl.loop(0, senders)
+    def _(s):
+        noise_sum = jnp.zeros((particles, LANES), F32)
+        for j in range(slices):
+            img = img_ref[s, j].astype(F32)
+            noise_sum += img * img
+        noise[pl.ds(s * particles, particles), :] = noise_sum
+
+    put(1, jnp.sum(noise[...].T, axis=0, keepdims=True))
+    last.wait()
+    put(2, power[...])
     for i, copy in enumerate(copies):
         copy.wait()
 
         @pl.loop(i * size, (i + 1) * size)
         def _(s):
             cross_sum = jnp.zeros((particles, LANES), F32)
-            noise_sum = jnp.zeros((particles, LANES), F32)
             for j in range(slices):
-                img = img_ref[s, j].astype(F32)
-                cross_sum += img * proj[s, j]
-                noise_sum += img * img
+                cross_sum += img_ref[s, j].astype(F32) * proj[s, j]
             cross[pl.ds(s * particles, particles), :] = cross_sum
-            noise[pl.ds(s * particles, particles), :] = noise_sum
-
-    total = senders * particles
-    rows = [jnp.sum(ref[...].T, axis=0, keepdims=True) for ref in (cross, noise)]
-    last.wait()
-    rows.append(power[...])
-    for d in range(senders):
-        for i, row in enumerate(rows):
-            out_ref[d, :, i * total : (i + 1) * total] = row
+
+    put(0, jnp.sum(cross[...].T, axis=0, keepdims=True))
 
 
 def partial_sums(img, proj, power):
@@ -337,7 +344,7 @@
         + [
             pltpu.VMEM(power.shape, F32),
             pltpu.VMEM(proj.shape, F32),
-            pltpu.SemaphoreType.DMA((4,)),
+            pltpu.SemaphoreType.DMA((8,)),
             pltpu.SemaphoreType.DMA,
         ],
         compiler_params=params(12),

time: 116 us -> 117 us (level)
  no operation moved by 1% of the time
where the time goes in v5:
time: 117 us; the launch traced here: 116 us
  Pallas kernels  40.6 us (35%)
  starting transfers between devices  39.4 us (34%)
  waiting for transfers between devices  21.9 us (19%)
  blocking collectives  9.52 us (8%)
  local copies, waits for them, and re-layouts  3.16 us (3%)
    ppermute x12, starting transfers between devices, ring(): return lax.ppermute(x, axis, [(i, target(i)) for i in range(size)])  24.4 us
    ppermute x12, waiting for transfers between devices, ring(): return lax.ppermute(x, axis, [(i, target(i)) for i in range(size)])  16 us
    pallas_call x1, Pallas kernels, project(): pl.pallas_call(functools.partial(project_kernel, count), grid=(senders //...  13.1 us
    pallas_call x4, Pallas kernels, scatter(): pl.pallas_call(functools.partial(scatter_kernel, capacity, shift, offsets...  11 us
    all_to_all x1, blocking collectives, shards(): partial = lax.all_to_all(partial, 'dom', 0, 0, tiled=True)  9.52 us
    all_to_all x1, starting transfers between devices, shards(): img = lax.all_to_all(img, 'dom', 0, 0, tiled=True)  6.54 us
    all_to_all x1, starting transfers between devices, shards(): meta = lax.all_to_all(meta, 'dom', 0, 0, tiled=True)  6.28 us
    pallas_call x1, Pallas kernels, contrast(): pl.pallas_call(functools.partial(contrast_kernel, extent, capacity), grid...  5.81 us
  transfers between devices with their start and end apart: 15, of which 5 were waited for; matrix products, arithmetic and copies ran while one was open for 1% of the time, Pallas kernels for 28%

profile of v5, /device:TPU:1, one launch (start us, length us, event | category | flops | bytes accessed | tf_op | source)
XLA Modules:
  0.0 116.2 jit_solution(13719030236432051236)
XLA Ops:
  1.5 6.9 %collective-permute-start.2 = (bf16[256,128]{1,0:T(8,128)(2,1)S(1)}, bf16[256,128]{1,0:T(8,128)(2,1)S(1)}, u32[]{:S(2)}, u32[]{:S(2)}) collective-permute-start(bf16[256,128]{1,0:T(8,128)(2,1)S(1)} %bitcast.18), channel_id=1, source_target_pairs={{0,3},{1,0},{2,1},{3,2},{4,7},{5,4},{6,5},{7,6},{8,11},{9,8},{10,9... | collective-permute-start | bytes 196616 | tf_op jit(solution)/shard_map/ppermute | solution.py:465
  9.4 2.3 %collective-permute-start = (bf16[256,128]{1,0:T(8,128)(2,1)S(1)}, bf16[256,128]{1,0:T(8,128)(2,1)S(1)}, u32[]{:S(2)}, u32[]{:S(2)}) collective-permute-start(bf16[256,128]{1,0:T(8,128)(2,1)S(1)} %bitcast.20), channel_id=1, source_target_pairs={{0,1},{1,2},{2,3},{3,0},{4,5},{5,6},{6,7},{7,4},{8,9},{9,10},{10,1... | collective-permute-start | bytes 196616 | tf_op jit(solution)/shard_map/ppermute | solution.py:465
  11.7 2.4 %shard_map.86 = f32[16,1,2432]{2,1,0:T(1,128)} custom-call(s32[16,32]{1,0:T(8,128)} %bitcast.27, s32[1,32]{1,0:T(1,128)} %bitcast.28, s32[1,32]{1,0:T(1,128)} %bitcast.29, bf16[1,32]{1,0:T(2,128)(2,1)} %bitcast.30, s32[16,512]{1,0:T(8,128)} %bitcast.26), custom_call_target="tpu_custom_call" | custom-call | flops 104857600 | bytes 1048576 | tf_op jit(solution)/shard_map/pallas_call | solution.py:134
  14.1 6.3 %all-to-all-start = ((f32[16,1,2432]{2,1,0:T(1,128)}), f32[16,1,2432]{2,1,0:T(1,128)S(1)}, u32[]{:S(2)}, u32[]{:S(2)}) async-start(f32[16,1,2432]{2,1,0:T(1,128)} %shard_map.86), calls=%async_computation | async-start | bytes 311296 | tf_op jit(solution)/shard_map/all_to_all | solution.py:486
  20.4 2.8 %collective-permute-start.5 = (bf16[4,256,128]{2,1,0:T(8,128)(2,1)S(1)}, bf16[4,256,128]{2,1,0:T(8,128)(2,1)S(1)}, u32[]{:S(2)}, u32[]{:S(2)}) collective-permute-start(bf16[4,256,128]{2,1,0:T(8,128)(2,1)S(1)} %pad_maximum_fusion.y_ref.vol0), channel_id=1, source_target_pairs={{0,12},{1,13},{2,14},{3,15},{4,0},{5,1},{6,2},{7,3},{8,4},{9,5},{1... | collective-permute-start | bytes 786440 | tf_op jit(solution)/shard_map/ppermute | solution.py:465
  24.3 3.1 %shard_map.88.x_ref = bf16[16,16,32,128]{3,2,1,0:T(8,128)(2,1)} custom-call(bf16[32,128,256]{2,1,0:T(8,128)(2,1)} %img_ref.1), custom_call_target="tpu_custom_call" | custom-call | flops 536870912 | bytes 4194304 | tf_op jit(solution)/shard_map/pallas_call | solution.py:82
  27.5 6.5 %all-to-all-start.1 = ((bf16[16,16,32,128]{3,2,1,0:T(8,128)(2,1)}), bf16[16,16,32,128]{3,2,1,0:T(8,128)(2,1)S(1)}, u32[]{:S(2)}, u32[]{:S(2)}) async-start(bf16[16,16,32,128]{3,2,1,0:T(8,128)(2,1)} %shard_map.90), calls=%async_computation.1 | async-start | bytes 4194304 | tf_op jit(solution)/shard_map/all_to_all | solution.py:490
  34.0 5.8 %shard_map.87 = (f32[16,16,32,128]{3,2,1,0:T(8,128)S(1)}, f32[16,1,1280]{2,1,0:T(1,128)S(1)}) custom-call(s32[4]{0:T(128)S(1)} %pad_add_fusion.at_ref, f32[16,1,2432]{2,1,0:T(1,128)S(1)} %all-to-all-done.meta_ref.z_ref), custom_call_target="tpu_custom_call" | custom-call | flops 1048576 | bytes 1048576 | tf_op jit(solution)/shard_map/pallas_call | solution.py:190
  39.9 13.1 %shard_map.91 = (f32[16,16,32,128]{3,2,1,0:T(8,128)}, f32[1,512]{1,0:T(1,128)S(1)}) custom-call(s32[4]{0:T(128)S(1)} %pad_add_fusion.at_ref, f32[16,1,2432]{2,1,0:T(1,128)S(1)} %all-to-all-done.meta_ref.z_ref, f32[16,16,32,128]{3,2,1,0:T(8,128)S(1)} %get-tuple-element.13.ctf_ref, bf16[4,256,128]{2,1,0:T(8,128)(2,1)S(1)} %pad_maximum_fusion.y_ref.vol0, ...), custom_call_target="tpu_custom_call" | custom-call | flops 42949672960 | bytes 10485760 | tf_op jit(solution)/shard_map/pallas_call | solution.py:268
  53.0 2.0 %copy-done = f32[16,16,32,128]{3,2,1,0:T(8,128)} copy-done((f32[16,16,32,128]{3,2,1,0:T(8,128)}, f32[16,16,32,128]{3,2,1,0:T(8,128)S(1)}, u32[]{:S(2)}) %copy-start) | copy-done | bytes 4194328
  55.6 5.6 %all-to-all-done.1.img_ref = bf16[16,16,32,128]{3,2,1,0:T(8,128)(2,1)S(1)} async-done(((bf16[16,16,32,128]{3,2,1,0:T(8,128)(2,1)}), bf16[16,16,32,128]{3,2,1,0:T(8,128)(2,1)S(1)}, u32[]{:S(2)}, u32[]{:S(2)}) %all-to-all-start.1) | async-done | bytes 2097184 | tf_op jit(solution)/shard_map/all_to_all | solution.py:490
  61.2 3.0 %shard_map.92 = f32[16,1,1536]{2,1,0:T(1,128)S(1)} custom-call(bf16[16,16,32,128]{3,2,1,0:T(8,128)(2,1)S(1)} %all-to-all-done.1.img_ref, f32[16,16,32,128]{3,2,1,0:T(8,128)} %get-tuple-element.14.proj_hbm, f32[1,512]{1,0:T(1,128)} %copy-done.2), custom_call_target="tpu_custom_call" | custom-call | flops 4194304 | bytes 6291456 | tf_op jit(solution)/shard_map/pallas_call | solution.py:338
  64.2 9.5 %all_to_all.15.part_ref = f32[16,1,1536]{2,1,0:T(1,128)S(1)} all-to-all(f32[16,1,1536]{2,1,0:T(1,128)S(1)} %shard_map.92), channel_id=1, replica_groups=mesh['dom'=16,'cls'=16] {'dom'}, dimensions={0} | all-to-all | bytes 196608 | tf_op jit(solution)/shard_map/all_to_all | solution.py:497
  74.8 2.8 %shard_map.95 = bf16[4,384,128]{2,1,0:T(8,128)(2,1)S(1)} custom-call(s32[4]{0:T(128)S(1)} %pad_add_fusion.at_ref, f32[16,1,2432]{2,1,0:T(1,128)S(1)} %all-to-all-done.meta_ref.z_ref, f32[16,1,1280]{2,1,0:T(1,128)S(1)} %get-tuple-element.12.place_ref, bf16[16,512,256]{2,1,0:T(8,128)(2,1)S(1)} %get-tuple-element.16.terms_ref), custom_call_target="tpu_custom_call" | custom-call | flops 2013265920 | bytes 5242880 | tf_op jit(solution)/shard_map/pallas_call | solution.py:427
  79.3 2.7 %shard_map.96 = bf16[4,384,128]{2,1,0:T(8,128)(2,1)S(1)} custom-call(s32[4]{0:T(128)S(1)} %pad_add_fusion.at_ref, f32[16,1,2432]{2,1,0:T(1,128)S(1)} %all-to-all-done.meta_ref.z_ref, f32[16,1,1280]{2,1,0:T(1,128)S(1)} %get-tuple-element.12.place_ref, bf16[16,512,256]{2,1,0:T(8,128)(2,1)S(1)} %get-tuple-element.16.terms_ref), custom_call_target="tpu_custom_call" | custom-call | flops 2013265920 | bytes 5242880 | tf_op jit(solution)/shard_map/pallas_call | solution.py:427
  83.1 2.8 %shard_map.97 = bf16[4,384,128]{2,1,0:T(8,128)(2,1)S(1)} custom-call(s32[4]{0:T(128)S(1)} %pad_add_fusion.at_ref, f32[16,1,2432]{2,1,0:T(1,128)S(1)} %all-to-all-done.meta_ref.z_ref, f32[16,1,1280]{2,1,0:T(1,128)S(1)} %get-tuple-element.12.place_ref, bf16[16,512,256]{2,1,0:T(8,128)(2,1)S(1)} %get-tuple-element.16.terms_ref), custom_call_target="tpu_custom_call" | custom-call | flops 2013265920 | bytes 5242880 | tf_op jit(solution)/shard_map/pallas_call | solution.py:427
  85.8 1.8 %collective-permute-start.8 = (bf16[4,384,128]{2,1,0:T(8,128)(2,1)S(1)}, bf16[4,384,128]{2,1,0:T(8,128)(2,1)S(1)}, u32[]{:S(2)}, u32[]{:S(2)}) collective-permute-start(bf16[4,384,128]{2,1,0:T(8,128)(2,1)S(1)} %shard_map.97), channel_id=1, source_target_pairs={{0,12},{1,13},{2,14},{3,15},{4,0},{5,1},{6,2},{7,3},{8,4},{9,5},{1... | collective-permute-start | bytes 1179656 | tf_op jit(solution)/shard_map/ppermute | solution.py:465
  87.7 2.7 %shard_map.94.own_ref = f32[4,384,128]{2,1,0:T(8,128)S(1)} custom-call(s32[4]{0:T(128)S(1)} %pad_add_fusion.at_ref, f32[16,1,2432]{2,1,0:T(1,128)S(1)} %all-to-all-done.meta_ref.z_ref, f32[16,1,1280]{2,1,0:T(1,128)S(1)} %get-tuple-element.12.place_ref, bf16[16,512,256]{2,1,0:T(8,128)(2,1)S(1)} %get-tuple-element.16.terms_ref), custom_call_target="tpu_custom_call" | custom-call | flops 2013265920 | bytes 5242880 | tf_op jit(solution)/shard_map/pallas_call | solution.py:427
  90.4 8.2 %collective-permute-done.7.got2 = bf16[4,384,128]{2,1,0:T(8,128)(2,1)S(1)} collective-permute-done((bf16[4,384,128]{2,1,0:T(8,128)(2,1)S(1)}, bf16[4,384,128]{2,1,0:T(8,128)(2,1)S(1)}, u32[]{:S(2)}, u32[]{:S(2)}) %collective-permute-start.7) | collective-permute-done | bytes 393248 | tf_op jit(solution)/shard_map/ppermute | solution.py:465
  98.8 1.9 %collective-permute-start.9 = (bf16[384,128]{1,0:T(8,128)(2,1)S(1)}, bf16[384,128]{1,0:T(8,128)(2,1)S(1)}, u32[]{:S(2)}, u32[]{:S(2)}) collective-permute-start(bf16[384,128]{1,0:T(8,128)(2,1)S(1)} %get-tuple-element.18), channel_id=1, source_target_pairs={{0,2},{1,3},{2,0},{3,1},{4,6},{5,7},{6,4},{7,5},{8,10},{9,11},{10,... | collective-permute-start | bytes 294920 | tf_op jit(solution)/shard_map/ppermute | solution.py:465
  102.5 2.1 %collective-permute-start.11 = (bf16[384,128]{1,0:T(8,128)(2,1)S(1)}, bf16[384,128]{1,0:T(8,128)(2,1)S(1)}, u32[]{:S(2)}, u32[]{:S(2)}) collective-permute-start(bf16[384,128]{1,0:T(8,128)(2,1)S(1)} %get-tuple-element.20), channel_id=1, source_target_pairs={{0,3},{1,0},{2,1},{3,2},{4,7},{5,4},{6,5},{7,6},{8,11},{9,8},{10,9... | collective-permute-start | bytes 294920 | tf_op jit(solution)/shard_map/ppermute | solution.py:465
  104.6 2.1 %collective-permute-done.9 = bf16[384,128]{1,0:T(8,128)(2,1)S(1)} collective-permute-done((bf16[384,128]{1,0:T(8,128)(2,1)S(1)}, bf16[384,128]{1,0:T(8,128)(2,1)S(1)}, u32[]{:S(2)}, u32[]{:S(2)}) %collective-permute-start.9) | collective-permute-done | bytes 98336 | tf_op jit(solution)/shard_map/ppermute | solution.py:465
  106.7 5.6 %collective-permute-done.10 = bf16[384,128]{1,0:T(8,128)(2,1)S(1)} collective-permute-done((bf16[384,128]{1,0:T(8,128)(2,1)S(1)}, bf16[384,128]{1,0:T(8,128)(2,1)S(1)}, u32[]{:S(2)}, u32[]{:S(2)}) %collective-permute-start.10) | collective-permute-done | bytes 98336 | tf_op jit(solution)/shard_map/ppermute | solution.py:465
  112.4 2.1 %collective-permute-start.12 = (f32[128,128]{1,0:T(8,128)S(1)}, f32[128,128]{1,0:T(8,128)S(1)}, u32[]{:S(2)}, u32[]{:S(2)}) collective-permute-start(f32[128,128]{1,0:T(8,128)S(1)} %slice.9), channel_id=1, source_target_pairs={{0,16},{16,0},{32,48},{48,32},{64,80},{80,64},{96,112},{112,96},{1... | collective-permute-start | bytes 196616 | tf_op jit(solution)/shard_map/ppermute | solution.py:512
  (33 shorter events, 11.0 us)
Async XLA Ops:
  1.5 18.8 %collective-permute-start.2 = (bf16[256,128]{1,0:T(8,128)(2,1)S(1)}, bf16[256,128]{1,0:T(8,128)(2,1)S(1)}, u32[]{:S(2)}, u32[]{:S(2)}) collective-permute-start(bf16[256,128]{1,0:T(8,128)(2,1)S(1)} %bitcast.18), channel_id=1, source_target_pairs={{0,3},{1,0},{2,1},{3,2},{4,7},{5,4},{6,5},{7,6},{8,11},{9,8},{10,9... | collective-permute-start | bytes 196616 | tf_op jit(solution)/shard_map/ppermute | solution.py:465
  8.4 11.9 %collective-permute-start.1 = (bf16[256,128]{1,0:T(8,128)(2,1)S(1)}, bf16[256,128]{1,0:T(8,128)(2,1)S(1)}, u32[]{:S(2)}, u32[]{:S(2)}) collective-permute-start(bf16[256,128]{1,0:T(8,128)(2,1)S(1)} %bitcast.19), channel_id=1, source_target_pairs={{0,2},{1,3},{2,0},{3,1},{4,6},{5,7},{6,4},{7,5},{8,10},{9,11},{10,... | collective-permute-start | bytes 196616 | tf_op jit(solution)/shard_map/ppermute | solution.py:465
  9.4 10.9 %collective-permute-start = (bf16[256,128]{1,0:T(8,128)(2,1)S(1)}, bf16[256,128]{1,0:T(8,128)(2,1)S(1)}, u32[]{:S(2)}, u32[]{:S(2)}) collective-permute-start(bf16[256,128]{1,0:T(8,128)(2,1)S(1)} %bitcast.20), channel_id=1, source_target_pairs={{0,1},{1,2},{2,3},{3,0},{4,5},{5,6},{6,7},{7,4},{8,9},{9,10},{10,1... | collective-permute-start | bytes 196616 | tf_op jit(solution)/shard_map/ppermute | solution.py:465
  14.1 13.5 %all-to-all-start = ((f32[16,1,2432]{2,1,0:T(1,128)}), f32[16,1,2432]{2,1,0:T(1,128)S(1)}, u32[]{:S(2)}, u32[]{:S(2)}) async-start(f32[16,1,2432]{2,1,0:T(1,128)} %shard_map.86), calls=%async_computation | async-start | bytes 311296 | tf_op jit(solution)/shard_map/all_to_all | solution.py:486
  20.4 19.5 %collective-permute-start.5 = (bf16[4,256,128]{2,1,0:T(8,128)(2,1)S(1)}, bf16[4,256,128]{2,1,0:T(8,128)(2,1)S(1)}, u32[]{:S(2)}, u32[]{:S(2)}) collective-permute-start(bf16[4,256,128]{2,1,0:T(8,128)(2,1)S(1)} %pad_maximum_fusion.y_ref.vol0), channel_id=1, source_target_pairs={{0,12},{1,13},{2,14},{3,15},{4,0},{5,1},{6,2},{7,3},{8,4},{9,5},{1... | collective-permute-start | bytes 786440 | tf_op jit(solution)/shard_map/ppermute | solution.py:465
  23.2 16.6 %collective-permute-start.4 = (bf16[4,256,128]{2,1,0:T(8,128)(2,1)S(1)}, bf16[4,256,128]{2,1,0:T(8,128)(2,1)S(1)}, u32[]{:S(2)}, u32[]{:S(2)}) collective-permute-start(bf16[4,256,128]{2,1,0:T(8,128)(2,1)S(1)} %pad_maximum_fusion.y_ref.vol0), channel_id=1, source_target_pairs={{0,8},{1,9},{2,10},{3,11},{4,12},{5,13},{6,14},{7,15},{8,0},{9,1},... | collective-permute-start | bytes 786440 | tf_op jit(solution)/shard_map/ppermute | solution.py:465
  23.6 16.3 %collective-permute-start.3 = (bf16[4,256,128]{2,1,0:T(8,128)(2,1)S(1)}, bf16[4,256,128]{2,1,0:T(8,128)(2,1)S(1)}, u32[]{:S(2)}, u32[]{:S(2)}) collective-permute-start(bf16[4,256,128]{2,1,0:T(8,128)(2,1)S(1)} %pad_maximum_fusion.y_ref.vol0), channel_id=1, source_target_pairs={{0,4},{1,5},{2,6},{3,7},{4,8},{5,9},{6,10},{7,11},{8,12},{9,13},{1... | collective-permute-start | bytes 786440 | tf_op jit(solution)/shard_map/ppermute | solution.py:465
  27.5 33.7 %all-to-all-start.1 = ((bf16[16,16,32,128]{3,2,1,0:T(8,128)(2,1)}), bf16[16,16,32,128]{3,2,1,0:T(8,128)(2,1)S(1)}, u32[]{:S(2)}, u32[]{:S(2)}) async-start(bf16[16,16,32,128]{3,2,1,0:T(8,128)(2,1)} %shard_map.90), calls=%async_computation.1 | async-start | bytes 4194304 | tf_op jit(solution)/shard_map/all_to_all | solution.py:490
  53.0 2.0 %copy-start = (f32[16,16,32,128]{3,2,1,0:T(8,128)}, f32[16,16,32,128]{3,2,1,0:T(8,128)S(1)}, u32[]{:S(2)}) copy-start(f32[16,16,32,128]{3,2,1,0:T(8,128)S(1)} %get-tuple-element.13.ctf_ref) | copy-start | bytes 12582916
  55.0 0.6 copy-start.2
  61.2 12.5 %copy-start.1 = (f32[16,16,32,128]{3,2,1,0:T(8,128)S(1)}, f32[16,16,32,128]{3,2,1,0:T(8,128)}, u32[]{:S(2)}) copy-start(f32[16,16,32,128]{3,2,1,0:T(8,128)} %copy-done) | copy-start | bytes 12582916
  77.6 12.8 %collective-permute-start.6 = (bf16[4,384,128]{2,1,0:T(8,128)(2,1)S(1)}, bf16[4,384,128]{2,1,0:T(8,128)(2,1)S(1)}, u32[]{:S(2)}, u32[]{:S(2)}) collective-permute-start(bf16[4,384,128]{2,1,0:T(8,128)(2,1)S(1)} %shard_map.95), channel_id=1, source_target_pairs={{0,8},{1,9},{2,10},{3,11},{4,12},{5,13},{6,14},{7,15},{8,0},{9,1},... | collective-permute-start | bytes 1179656 | tf_op jit(solution)/shard_map/ppermute | solution.py:465
  82.1 16.6 %collective-permute-start.7 = (bf16[4,384,128]{2,1,0:T(8,128)(2,1)S(1)}, bf16[4,384,128]{2,1,0:T(8,128)(2,1)S(1)}, u32[]{:S(2)}, u32[]{:S(2)}) collective-permute-start(bf16[4,384,128]{2,1,0:T(8,128)(2,1)S(1)} %shard_map.96), channel_id=1, source_target_pairs={{0,4},{1,5},{2,6},{3,7},{4,8},{5,9},{6,10},{7,11},{8,12},{9,13},{1... | collective-permute-start | bytes 1179656 | tf_op jit(solution)/shard_map/ppermute | solution.py:465
  85.8 12.8 %collective-permute-start.8 = (bf16[4,384,128]{2,1,0:T(8,128)(2,1)S(1)}, bf16[4,384,128]{2,1,0:T(8,128)(2,1)S(1)}, u32[]{:S(2)}, u32[]{:S(2)}) collective-permute-start(bf16[4,384,128]{2,1,0:T(8,128)(2,1)S(1)} %shard_map.97), channel_id=1, source_target_pairs={{0,12},{1,13},{2,14},{3,15},{4,0},{5,1},{6,2},{7,3},{8,4},{9,5},{1... | collective-permute-start | bytes 1179656 | tf_op jit(solution)/shard_map/ppermute | solution.py:465
  98.8 7.9 %collective-permute-start.9 = (bf16[384,128]{1,0:T(8,128)(2,1)S(1)}, bf16[384,128]{1,0:T(8,128)(2,1)S(1)}, u32[]{:S(2)}, u32[]{:S(2)}) collective-permute-start(bf16[384,128]{1,0:T(8,128)(2,1)S(1)} %get-tuple-element.18), channel_id=1, source_target_pairs={{0,2},{1,3},{2,0},{3,1},{4,6},{5,7},{6,4},{7,5},{8,10},{9,11},{10,... | collective-permute-start | bytes 294920 | tf_op jit(solution)/shard_map/ppermute | solution.py:465
  100.8 11.6 %collective-permute-start.10 = (bf16[384,128]{1,0:T(8,128)(2,1)S(1)}, bf16[384,128]{1,0:T(8,128)(2,1)S(1)}, u32[]{:S(2)}, u32[]{:S(2)}) collective-permute-start(bf16[384,128]{1,0:T(8,128)(2,1)S(1)} %get-tuple-element.19), channel_id=1, source_target_pairs={{0,1},{1,2},{2,3},{3,0},{4,5},{5,6},{6,7},{7,4},{8,9},{9,10},{10,1... | collective-permute-start | bytes 294920 | tf_op jit(solution)/shard_map/ppermute | solution.py:465
  102.5 9.9 %collective-permute-start.11 = (bf16[384,128]{1,0:T(8,128)(2,1)S(1)}, bf16[384,128]{1,0:T(8,128)(2,1)S(1)}, u32[]{:S(2)}, u32[]{:S(2)}) collective-permute-start(bf16[384,128]{1,0:T(8,128)(2,1)S(1)} %get-tuple-element.20), channel_id=1, source_target_pairs={{0,3},{1,0},{2,1},{3,2},{4,7},{5,4},{6,5},{7,6},{8,11},{9,8},{10,9... | collective-permute-start | bytes 294920 | tf_op jit(solution)/shard_map/ppermute | solution.py:465
  112.4 3.0 %collective-permute-start.12 = (f32[128,128]{1,0:T(8,128)S(1)}, f32[128,128]{1,0:T(8,128)S(1)}, u32[]{:S(2)}, u32[]{:S(2)}) collective-permute-start(f32[128,128]{1,0:T(8,128)S(1)} %slice.9), channel_id=1, source_target_pairs={{0,16},{16,0},{32,48},{48,32},{64,80},{80,64},{96,112},{112,96},{1... | collective-permute-start | bytes 196616 | tf_op jit(solution)/shard_map/ppermute | solution.py:512
